TPU v7x, 32 devices: a whole 2x2x4 slice. The times are simulated.
32 devices in a mesh: opg: 8 (over z, x), sec: 4 (over y, core).
Axes of the slice: x: 2, y: 2, z: 4, core: 2. Of those that a mesh axis runs over, the one named last changes fastest.
Arguments:
- psi: bfloat16 [8, 384, 384], P('sec'), may hold values from -6 to 6
- left_ops: bfloat16 [64, 8, 384, 384], P('opg', 'sec'), may hold values from -0.15625 to 0.15625
- right_ops: bfloat16 [64, 8, 384, 384], P('opg', 'sec'), may hold values from -0.109375 to 0.109375
- source: int32 [64, 8], P('opg', 'sec'), may hold values from 0 to 7
- coef_index: int32 [64, 8], P('opg', 'sec'), may hold values from 0 to 63
- sixj: float32 [64], replicated, may hold values from -1 to 1
Outputs:
- sigma: bfloat16 [384, 8, 384], P('opg', 'sec')
All inputs are finite; a program needn't handle non-finite values.
Results may differ from a plain program's by a relative error of at most 0.005.
Values may be sent and summed in bfloat16 or wider, within the bound.
No kernel may reach another device: no remote copies, remote signals or barrier semaphores. Data moves between devices by JAX's collectives and lax.ppermute only.
A program may use at most 64 MiB of HBM per device.

v0:
```python
import functools

import jax
import jax.numpy as jnp
from jax import lax
from jax.experimental import pallas as pl
from jax.experimental.pallas import tpu as pltpu
from jax.sharding import PartitionSpec as P

OPG = "opg"
SEC = "sec"
PARTS = 4
HALVES = 2
NEAR = 2
KERNEL_VMEM = 24_000_000
PLAN_FLOPS = 20_000_000_000


def flip(x, axis, size, bit):
    return lax.ppermute(x, axis, [(i, i ^ bit) for i in range(size)])


def bits_of(size):
    return [1 << k for k in range(size.bit_length() - 1)]


CLASSES = 3


def make_plan(meta, plan, scale, pairs, local):
    slots = local * pairs
    for kind in range(CLASSES):
        plan[kind, 3 * slots] = 0
    me_sec = lax.axis_index(SEC)

    def sector(s):
        def one(p, carry):
            src = meta[s, p].astype(jnp.int32)
            r, j = lax.div(src, local) ^ me_sec, lax.rem(src, local)
            kind = jnp.where(r < NEAR, 0, 1 + lax.rem(r, 2))
            block = jnp.where(r < NEAR, r, lax.div(r, 2) - 1) * local + j
            n = plan[kind, 3 * slots]
            plan[kind, n] = p
            plan[kind, slots + n] = s
            plan[kind, 2 * slots + n] = block
            scale[kind, n] = meta[local + s, p]
            plan[kind, 3 * slots] = n + 1
            return carry

        lax.fori_loop(0, pairs, one, 0)

    for s in range(local):
        sector(s)


def thirds(x, w, transposed):
    size = x.shape[1] // 3
    cut = [slice(i * size, (i + 1) * size) for i in range(3)]
    none = jnp.zeros((size, size), w.dtype)

    def tile(depth, columns, absent):
        def block(k, n):
            if (k, n) in absent:
                return none
            return w[cut[n], cut[k]] if transposed else w[cut[k], cut[n]]

        one, two = (columns, depth) if transposed else (depth, columns)
        rows = [
            jnp.concatenate(
                [block(j, i) if transposed else block(i, j) for j in two], axis=1
            )
            for i in one
        ]
        return jnp.concatenate(rows, axis=0)

    def product(depth, columns, absent):
        return lax.dot_general(
            jnp.concatenate([x[:, cut[k]] for k in depth], axis=1),
            tile(depth, columns, absent),
            (((1,), (1 if transposed else 0,)), ((), ())),
            preferred_element_type=jnp.float32,
        )

    p = product((0, 1), (0, 1), ())
    q = product((0, 2), (2, 0), ((0, 0),))
    r = product((1, 2), (2, 1), ((1, 1), (2, 2)))
    low, high = slice(0, size), slice(size, 2 * size)
    return list(zip(cut, (p[:, low] + q[:, high], p[:, high] + r[:, high], q[:, low] + r[:, low])))


def run(kind, plan, scale, left, right, psi, acc, even, odd):
    pairs, local = left.shape[:2]
    slots = local * pairs
    count = plan[kind, 3 * slots]

    def first(i, halves):
        i = jnp.minimum(i, count - 1)
        p, s, block = [plan[kind, k * slots + i] for k in range(3)]
        for c, half in thirds(left.at[p, s], psi.at[block], False):
            halves[:, c] = (half * scale[kind, i]).astype(jnp.bfloat16)

    def second(i, halves):
        p, s = [plan[kind, k * slots + i] for k in range(2)]
        for c, term in thirds(halves, right.at[p, s], True):
            acc[s, :, c] += term

    def two(j, carry):
        i = 2 * j
        first(i + 1, odd)
        second(i, even)
        first(i + 2, even)
        second(i + 1, odd)
        return carry

    @pl.when(count > 0)
    def _():
        first(0, even)
        lax.fori_loop(0, lax.div(count, 2), two, 0)

        @pl.when(lax.rem(count, 2) == 1)
        def _():
            second(count - 1, even)


def plan_kernel(local, meta, plan, scale):
    make_plan(meta, plan, scale, meta.shape[1], local)


def products_kernel(kind, n_opg, plan, scale, left, right, *refs):
    local, sb = left.shape[1:3]
    last = kind == CLASSES - 1
    outs = n_opg if last else 1
    pieces, refs = refs[: -outs - 3 - last], refs[-outs - 3 - last :]
    psi, even, odd = refs[outs : outs + 3]
    acc = refs[-1] if last else refs[0]
    if kind:
        acc[...] = pieces[0][...]
        pieces = pieces[1:]
    else:
        acc[...] = jnp.zeros_like(acc)
    if kind == 0:
        for i, piece in enumerate(pieces):
            psi[i * local : (i + 1) * local] = piece[...]
    else:
        half = lax.rem(lax.axis_index(OPG), HALVES)
        rows = sb // HALVES
        for i in range(len(pieces) // 3):
            whole, here, there = pieces[3 * i : 3 * i + 3]
            end = (i + 1) * local - 1
            psi[i * local : end] = whole[...]
            psi[end, pl.ds(pl.multiple_of(half * rows, 16), rows), :] = here[...]
            psi[end, pl.ds(pl.multiple_of((1 - half) * rows, 16), rows), :] = there[...]
    run(kind, plan, scale, left, right, psi, acc, even, odd)
    if last:
        me_opg = lax.axis_index(OPG)
        rows = sb // n_opg
        for r, send in enumerate(refs[:outs]):
            at = pl.multiple_of((r ^ me_opg) * rows, 8)
            send[...] = acc[:, pl.ds(at, rows), :].astype(send.dtype)


SMEM = pl.BlockSpec(memory_space=pltpu.SMEM)
VMEM = pl.BlockSpec(memory_space=pltpu.VMEM)


def products(kind, n_opg, plan, scale, left, right, totals, pieces):
    pairs, local, sb, _ = left.shape
    out_shape = jax.ShapeDtypeStruct((local, sb, sb), jnp.float32)
    scratch = []
    if kind == CLASSES - 1:
        scratch = [pltpu.VMEM(out_shape.shape, out_shape.dtype)]
        out_shape = tuple(
            jax.ShapeDtypeStruct(
                (local, sb // n_opg, sb), jnp.bfloat16 if r % PARTS else jnp.float32
            )
            for r in range(n_opg)
        )
    return pl.pallas_call(
        functools.partial(products_kernel, kind, n_opg),
        out_shape=out_shape,
        in_specs=[SMEM] * 2 + [VMEM] * (2 + len(totals) + len(pieces)),
        out_specs=jax.tree.map(lambda _: VMEM, out_shape),
        scratch_shapes=[
            pltpu.VMEM((len(pieces) // (3 if kind else 1) * local, sb, sb), jnp.bfloat16),
            pltpu.VMEM((sb, sb), jnp.bfloat16),
            pltpu.VMEM((sb, sb), jnp.bfloat16),
            *scratch,
        ],
        compiler_params=pltpu.CompilerParams(vmem_limit_bytes=KERNEL_VMEM),
        cost_estimate=pl.CostEstimate(flops=sb, bytes_accessed=0, transcendentals=0),
    )(plan, scale, left, right, *totals, *pieces)


def scatter_sum(sends, n_opg):
    out = []
    for high in reversed(range(n_opg // PARTS)):
        at = high * PARTS
        total = sends[at]
        for low in (3, 1, 2):
            total = total + flip(sends[at + low], OPG, n_opg, low).astype(jnp.float32)
        if high:
            total = flip(total.astype(jnp.bfloat16), OPG, n_opg, at).astype(jnp.float32)
        out.append(total)
    return sum(out[:-1], out[-1])


def on_device(n_opg, n_sec, psi, left_ops, right_ops, source, coef_index, sixj):
    local, sb, _ = psi.shape
    pairs = left_ops.shape[0]

    half = lax.rem(lax.axis_index(OPG), HALVES)
    cut = psi[local - 1].reshape(HALVES, sb // HALVES, sb)
    here = {0: lax.dynamic_index_in_dim(cut, half, axis=0, keepdims=False)}
    whole = {0: psi[: local - 1]}
    for bit in bits_of(n_sec)[1:]:
        for held in (here, whole):
            held.update({r | bit: flip(x, SEC, n_sec, bit) for r, x in held.items()})
    far = range(NEAR, n_sec, 2)
    here, whole = [here[r] for r in far], [whole[r] for r in far]
    partner = flip(psi, SEC, n_sec, 1)

    table = jnp.arange(sixj.shape[0], dtype=jnp.int32)
    coef = jnp.sum(jnp.where(coef_index.T[:, :, None] == table, sixj, 0.0), axis=2)
    meta = jnp.concatenate([source.T.astype(jnp.float32), coef])
    plan, scale = pl.pallas_call(
        functools.partial(plan_kernel, local),
        out_shape=(
            jax.ShapeDtypeStruct((CLASSES, 3 * local * pairs + 1), jnp.int32),
            jax.ShapeDtypeStruct((CLASSES, local * pairs), jnp.float32),
        ),
        in_specs=[SMEM],
        out_specs=(SMEM, SMEM),
        compiler_params=pltpu.CompilerParams(vmem_limit_bytes=KERNEL_VMEM),
        cost_estimate=pl.CostEstimate(flops=PLAN_FLOPS, bytes_accessed=0, transcendentals=0),
    )(meta)

    def onto(kind, totals, pieces):
        return products(kind, n_opg, plan, scale, left_ops, right_ops, totals, pieces)

    def to_other_core(pieces):
        return [flip(x, SEC, n_sec, 1) for x in pieces]

    here, plan, scale = lax.optimization_barrier((here, plan, scale))
    there = [flip(x, OPG, n_opg, 1) for x in here]
    here_crossed = to_other_core(here)
    done = onto(0, [], [psi, partner])
    there, whole, here_crossed, done = lax.optimization_barrier((there, whole, here_crossed, done))
    there_crossed, whole_crossed = to_other_core(there), to_other_core(whole)
    done = onto(1, [done], [x for three in zip(whole, here, there) for x in three])
    crossed = zip(whole_crossed, here_crossed, there_crossed)
    sends = onto(2, [done], [x for three in crossed for x in three])
    return jnp.swapaxes(scatter_sum(sends, n_opg), 0, 1).astype(jnp.bfloat16)


def solution(mesh):
    n_opg, n_sec = mesh.shape[OPG], mesh.shape[SEC]
    placed = (
        P(SEC, None, None),
        P(OPG, SEC, None, None),
        P(OPG, SEC, None, None),
        P(OPG, SEC),
        P(OPG, SEC),
        P(),
    )
    return jax.shard_map(
        functools.partial(on_device, n_opg, n_sec),
        mesh=mesh,
        in_specs=placed,
        out_specs=P(OPG, SEC, None),
        check_vma=False,
    )
```

profile of v0, /device:TPU:0, one launch (start us, length us, event | category | flops | bytes accessed | tf_op | source)
XLA Modules:
  0.0 37.5 jit_solution(17971717147390155906)
XLA Ops:
  0.0 0.5 %collective-permute-start.4 = (bf16[2,384,384]{2,1,0:T(8,128)(2,1)}, bf16[2,384,384]{2,1,0:T(8,128)(2,1)S(1)}, u32[]{:S(2)}, u32[]{:S(2)}) collective-permute-start(bf16[2,384,384]{2,1,0:T(8,128)(2,1)} %refs_0_.1), channel_id=1, source_target_pairs={{0,1},{1,0},{2,3},{3,2},{4,5},{5,4},{6,7},{7,6},{8,9},{9,8},{10,11... | collective-permute-start | bytes 1769480 | tf_op jit(solution)/shard_map/ppermute | solution.py:20
  0.5 1.2 %fusion.1 = (bf16[1,384,384]{2,1,0:T(8,128)(2,1)S(1)}, bf16[1,384,384]{2,1,0:T(8,128)(2,1)S(1)}) fusion(bf16[2,384,384]{2,1,0:T(8,128)(2,1)} %refs_0_.1), kind=kLoop, calls=%fused_computation.8 | loop fusion | bytes 1179648 | tf_op jit(solution)/shard_map/slice | solution.py:214
  1.7 2.6 %collective-permute-start = (bf16[192,384]{1,0:T(8,128)(2,1)S(1)}, bf16[192,384]{1,0:T(8,128)(2,1)S(1)}, u32[]{:S(2)}, u32[]{:S(2)}) collective-permute-start(bf16[192,384]{1,0:T(8,128)(2,1)S(1)} %dynamic-slice_bitcast_fusion), channel_id=1, source_target_pairs={{0,2},{1,3},{2,0},{3,1},{4,6},{5,7},{6,4},{7,5},{8,10},{9,11},{10,... | collective-permute-start | bytes 442376 | tf_op jit(solution)/shard_map/ppermute | solution.py:20
  4.2 0.1 collective-permute-start.2
  4.3 0.7 %convert_bitcast_fusion = f32[2,8]{1,0:T(2,128)S(1)} fusion(s32[8,2]{0,1:T(2,128)} %param.9), kind=kLoop, calls=%fused_computation.7 | loop fusion | flops 16 | bytes 128 | tf_op jit(solution)/shard_map/convert_element_type | solution.py:224
  5.0 0.8 %select_reduce_fusion = f32[2,8]{1,0:T(2,128)S(1)} fusion(f32[64]{0:T(128)} %param.11, s32[2,8]{1,0:T(2,128)} %bitcast.11), kind=kLoop, calls=%fused_computation.4 | loop fusion | flops 3056 | bytes 384 | tf_op jit(solution)/shard_map/reduce_sum | solution.py:223
  5.9 0.0 copy-start
  5.9 0.0 copy-start.1
  5.9 1.7 %shard_map.64 = (s32[3,49]{1,0:T(4,128)S(1)}, f32[3,16]{1,0:T(4,128)S(1)}) custom-call(f32[4,8]{1,0:T(4,128)S(1)} %pad_maximum_fusion.meta), custom_call_target="tpu_custom_call" | custom-call | flops 20000000000 | tf_op jit(solution)/shard_map/pallas_call | solution.py:225
  7.6 1.3 %collective-permute-done.refs_2_ = bf16[192,384]{1,0:T(8,128)(2,1)S(1)} collective-permute-done((bf16[192,384]{1,0:T(8,128)(2,1)S(1)}, bf16[192,384]{1,0:T(8,128)(2,1)S(1)}, u32[]{:S(2)}, u32[]{:S(2)}) %collective-permute-start) | collective-permute-done | bytes 147488 | tf_op jit(solution)/shard_map/ppermute | solution.py:20
  9.0 1.9 %collective-permute-start.1 = (bf16[192,384]{1,0:T(8,128)(2,1)S(1)}, bf16[192,384]{1,0:T(8,128)(2,1)S(1)}, u32[]{:S(2)}, u32[]{:S(2)}) collective-permute-start(bf16[192,384]{1,0:T(8,128)(2,1)S(1)} %collective-permute-done.refs_2_), channel_id=1, source_target_pairs={{0,4},{4,0},{8,12},{12,8},{16,20},{20,16},{24,28},{28,24},{1,5},{5... | collective-permute-start | bytes 442376 | tf_op jit(solution)/shard_map/ppermute | solution.py:20
  10.9 0.0 collective-permute-done.4.refs_1_
  10.9 6.0 %shard_map.65.refs_0_ = f32[2,384,384]{2,1,0:T(8,128)S(1)} custom-call(s32[3,49]{1,0:T(4,128)S(1)} %get-tuple-element.24.plan, f32[3,16]{1,0:T(4,128)S(1)} %get-tuple-element.25.scale, bf16[8,2,384,384]{3,2,1,0:T(8,128)(2,1)S(1)} %bitcast.9, bf16[8,2,384,384]{3,2,1,0:T(8,128)(2,1)S(1)} %copy-done, bf16[2,384,384]{2,1,0:T(8,128)(2,1)S(1)} %copy-done.1, ...), custom_call_target="tpu_custom_call" | custom-call | flops 384 | tf_op jit(solution)/shard_map/pallas_call | solution.py:178
  16.9 0.0 collective-permute-done.3.refs_2_
  17.0 0.1 collective-permute-start.5
  17.0 0.5 %collective-permute-start.6 = (bf16[192,384]{1,0:T(8,128)(2,1)S(1)}, bf16[192,384]{1,0:T(8,128)(2,1)S(1)}, u32[]{:S(2)}, u32[]{:S(2)}) collective-permute-start(bf16[192,384]{1,0:T(8,128)(2,1)S(1)} %collective-permute-done.1.refs_3_), channel_id=1, source_target_pairs={{0,1},{1,0},{2,3},{3,2},{4,5},{5,4},{6,7},{7,6},{8,9},{9,8},{10,11... | collective-permute-start | bytes 442376 | tf_op jit(solution)/shard_map/ppermute | solution.py:20
  17.5 1.9 %shard_map.66.refs_0_ = f32[2,384,384]{2,1,0:T(8,128)S(1)} custom-call(s32[3,49]{1,0:T(4,128)S(1)} %get-tuple-element.24.plan, f32[3,16]{1,0:T(4,128)S(1)} %get-tuple-element.25.scale, bf16[8,2,384,384]{3,2,1,0:T(8,128)(2,1)S(1)} %bitcast.9, bf16[8,2,384,384]{3,2,1,0:T(8,128)(2,1)S(1)} %copy-done, f32[2,384,384]{2,1,0:T(8,128)S(1)} %shard_map.65.refs_0_, ...), custom_call_target="tpu_custom_call" | custom-call | flops 384 | tf_op jit(solution)/shard_map/pallas_call | solution.py:178
  19.4 1.9 %shard_map.67 = (f32[2,48,384]{2,1,0:T(8,128)S(1)}, bf16[2,48,384]{2,1,0:T(8,128)(2,1)S(1)}, bf16[2,48,384]{2,1,0:T(8,128)(2,1)S(1)}, bf16[2,48,384]{2,1,0:T(8,1...) custom-call(s32[3,49]{1,0:T(4,128)S(1)} %get-tuple-element.24.plan, ...), custom_call_target="tpu_custom_call" | custom-call | flops 384 | tf_op jit(solution)/shard_map/pallas_call | solution.py:178
  21.4 2.4 %collective-permute-start.10 = (bf16[2,48,384]{2,1,0:T(8,128)(2,1)S(1)}, bf16[2,48,384]{2,1,0:T(8,128)(2,1)S(1)}, u32[]{:S(2)}, u32[]{:S(2)}) collective-permute-start(bf16[2,48,384]{2,1,0:T(8,128)(2,1)S(1)} %get-tuple-element.36), channel_id=1, source_target_pairs={{0,12},{4,8},{8,4},{12,0},{16,28},{20,24},{24,20},{28,16},{1,13},{... | collective-permute-start | bytes 221192 | tf_op jit(solution)/shard_map/ppermute | solution.py:20
  23.8 1.3 %collective-permute-start.11 = (bf16[2,48,384]{2,1,0:T(8,128)(2,1)S(1)}, bf16[2,48,384]{2,1,0:T(8,128)(2,1)S(1)}, u32[]{:S(2)}, u32[]{:S(2)}) collective-permute-start(bf16[2,48,384]{2,1,0:T(8,128)(2,1)S(1)} %get-tuple-element.37), channel_id=1, source_target_pairs={{0,4},{4,0},{8,12},{12,8},{16,20},{20,16},{24,28},{28,24},{1,5},{5... | collective-permute-start | bytes 221192 | tf_op jit(solution)/shard_map/ppermute | solution.py:20
  25.1 0.3 collective-permute-start.12
  25.4 1.9 %collective-permute-start.7 = (bf16[2,48,384]{2,1,0:T(8,128)(2,1)S(1)}, bf16[2,48,384]{2,1,0:T(8,128)(2,1)S(1)}, u32[]{:S(2)}, u32[]{:S(2)}) collective-permute-start(bf16[2,48,384]{2,1,0:T(8,128)(2,1)S(1)} %get-tuple-element.32), channel_id=1, source_target_pairs={{0,12},{4,8},{8,4},{12,0},{16,28},{20,24},{24,20},{28,16},{1,13},{... | collective-permute-start | bytes 221192 | tf_op jit(solution)/shard_map/ppermute | solution.py:20
  27.3 1.3 %collective-permute-start.8 = (bf16[2,48,384]{2,1,0:T(8,128)(2,1)S(1)}, bf16[2,48,384]{2,1,0:T(8,128)(2,1)S(1)}, u32[]{:S(2)}, u32[]{:S(2)}) collective-permute-start(bf16[2,48,384]{2,1,0:T(8,128)(2,1)S(1)} %get-tuple-element.33), channel_id=1, source_target_pairs={{0,4},{4,0},{8,12},{12,8},{16,20},{20,16},{24,28},{28,24},{1,5},{5... | collective-permute-start | bytes 221192 | tf_op jit(solution)/shard_map/ppermute | solution.py:20
  28.6 0.3 collective-permute-start.9
  28.9 0.5 %collective-permute-done.11 = bf16[2,48,384]{2,1,0:T(8,128)(2,1)S(1)} collective-permute-done((bf16[2,48,384]{2,1,0:T(8,128)(2,1)S(1)}, bf16[2,48,384]{2,1,0:T(8,128)(2,1)S(1)}, u32[]{:S(2)}, u32[]{:S(2)}) %collective-permute-start.11) | collective-permute-done | bytes 73760 | tf_op jit(solution)/shard_map/ppermute | solution.py:20
  29.4 0.8 %collective-permute-done.12 = bf16[2,48,384]{2,1,0:T(8,128)(2,1)S(1)} collective-permute-done((bf16[2,48,384]{2,1,0:T(8,128)(2,1)S(1)}, bf16[2,48,384]{2,1,0:T(8,128)(2,1)S(1)}, u32[]{:S(2)}, u32[]{:S(2)}) %collective-permute-start.12) | collective-permute-done | bytes 73760 | tf_op jit(solution)/shard_map/ppermute | solution.py:20
  30.2 2.2 %collective-permute-start.13 = (bf16[2,48,384]{2,1,0:T(8,128)(2,1)S(1)}, bf16[2,48,384]{2,1,0:T(8,128)(2,1)S(1)}, u32[]{:S(2)}, u32[]{:S(2)}) collective-permute-start(bf16[2,48,384]{2,1,0:T(8,128)(2,1)S(1)} %add_convert_fusion.1), channel_id=1, source_target_pairs={{0,16},{4,20},{8,24},{12,28},{16,0},{20,4},{24,8},{28,12},{1,17},{... | collective-permute-start | bytes 221192 | tf_op jit(solution)/shard_map/ppermute | solution.py:20
  32.4 0.4 %collective-permute-done.8 = bf16[2,48,384]{2,1,0:T(8,128)(2,1)S(1)} collective-permute-done((bf16[2,48,384]{2,1,0:T(8,128)(2,1)S(1)}, bf16[2,48,384]{2,1,0:T(8,128)(2,1)S(1)}, u32[]{:S(2)}, u32[]{:S(2)}) %collective-permute-start.8) | collective-permute-done | bytes 73760 | tf_op jit(solution)/shard_map/ppermute | solution.py:20
  32.8 0.1 collective-permute-done.9
  32.9 3.8 %collective-permute-done.13 = bf16[2,48,384]{2,1,0:T(8,128)(2,1)S(1)} collective-permute-done((bf16[2,48,384]{2,1,0:T(8,128)(2,1)S(1)}, bf16[2,48,384]{2,1,0:T(8,128)(2,1)S(1)}, u32[]{:S(2)}, u32[]{:S(2)}) %collective-permute-start.13) | collective-permute-done | bytes 73760 | tf_op jit(solution)/shard_map/ppermute | solution.py:20
  36.7 0.1 fusion
  36.8 0.7 %copy.8 = bf16[48,2,384]{2,1,0:T(2,128)(2,1)} copy(bf16[48,2,384]{2,0,1:T(8,128)(2,1)S(1)} %fusion) | data formatting | bytes 147456 | tf_op jit(solution)/shard_map/convert_element_type | solution.py:252
  (17 shorter events, 0.1 us)
Async XLA Ops:
  0.0 10.9 %collective-permute-start.4 = (bf16[2,384,384]{2,1,0:T(8,128)(2,1)}, bf16[2,384,384]{2,1,0:T(8,128)(2,1)S(1)}, u32[]{:S(2)}, u32[]{:S(2)}) collective-permute-start(bf16[2,384,384]{2,1,0:T(8,128)(2,1)} %refs_0_.1), channel_id=1, source_target_pairs={{0,1},{1,0},{2,3},{3,2},{4,5},{5,4},{6,7},{7,6},{8,9},{9,8},{10,11... | collective-permute-start | bytes 1769480 | tf_op jit(solution)/shard_map/ppermute | solution.py:20
  0.5 10.4 %slice-start = ((s8[4718592]{0:T(1024)(128)(4,1)}), s8[524288]{0:T(1024)(128)(4,1)S(1)}, s32[]{:S(2)}) async-start(s8[4718592]{0:T(1024)(128)(4,1)} %bitcast.8), calls=%async_computation | async-start | bytes 1048576
  1.7 7.3 %collective-permute-start = (bf16[192,384]{1,0:T(8,128)(2,1)S(1)}, bf16[192,384]{1,0:T(8,128)(2,1)S(1)}, u32[]{:S(2)}, u32[]{:S(2)}) collective-permute-start(bf16[192,384]{1,0:T(8,128)(2,1)S(1)} %dynamic-slice_bitcast_fusion), channel_id=1, source_target_pairs={{0,2},{1,3},{2,0},{3,1},{4,6},{5,7},{6,4},{7,5},{8,10},{9,11},{10,... | collective-permute-start | bytes 442376 | tf_op jit(solution)/shard_map/ppermute | solution.py:20
  4.2 12.7 %collective-permute-start.2 = (bf16[1,384,384]{2,1,0:T(8,128)(2,1)S(1)}, bf16[1,384,384]{2,1,0:T(8,128)(2,1)S(1)}, u32[]{:S(2)}, u32[]{:S(2)}) collective-permute-start(bf16[1,384,384]{2,1,0:T(8,128)(2,1)S(1)} %get-tuple-element.39), channel_id=1, source_target_pairs={{0,2},{1,3},{2,0},{3,1},{4,6},{5,7},{6,4},{7,5},{8,10},{9,11},{10,... | collective-permute-start | bytes 884744 | tf_op jit(solution)/shard_map/ppermute | solution.py:20
  5.9 5.0 %slice-start.1 = ((s8[4718592]{0:T(1024)(128)(4,1)}), s8[4194304]{0:T(1024)(128)(4,1)S(1)}, s32[]{:S(2)}) async-start(s8[4718592]{0:T(1024)(128)(4,1)} %bitcast.8), calls=%async_computation.1 | async-start | bytes 8388608
  5.9 5.0 %copy-start = (bf16[8,2,384,384]{3,2,1,0:T(8,128)(2,1)S(1)}, bf16[8,2,384,384]{3,2,1,0:T(8,128)(2,1)}, u32[]{:S(2)}) copy-start(bf16[8,2,384,384]{3,2,1,0:T(8,128)(2,1)} %right.5) | copy-start | bytes 14155780
  5.9 5.0 %copy-start.1 = (bf16[2,384,384]{2,1,0:T(8,128)(2,1)S(1)}, bf16[2,384,384]{2,1,0:T(8,128)(2,1)}, u32[]{:S(2)}) copy-start(bf16[2,384,384]{2,1,0:T(8,128)(2,1)} %refs_0_.1) | copy-start | bytes 1769476
  9.0 8.0 %collective-permute-start.3 = (bf16[192,384]{1,0:T(8,128)(2,1)S(1)}, bf16[192,384]{1,0:T(8,128)(2,1)S(1)}, u32[]{:S(2)}, u32[]{:S(2)}) collective-permute-start(bf16[192,384]{1,0:T(8,128)(2,1)S(1)} %collective-permute-done.refs_2_), channel_id=1, source_target_pairs={{0,1},{1,0},{2,3},{3,2},{4,5},{5,4},{6,7},{7,6},{8,9},{9,8},{10,11... | collective-permute-start | bytes 442376 | tf_op jit(solution)/shard_map/ppermute | solution.py:20
  9.0 8.0 %collective-permute-start.1 = (bf16[192,384]{1,0:T(8,128)(2,1)S(1)}, bf16[192,384]{1,0:T(8,128)(2,1)S(1)}, u32[]{:S(2)}, u32[]{:S(2)}) collective-permute-start(bf16[192,384]{1,0:T(8,128)(2,1)S(1)} %collective-permute-done.refs_2_), channel_id=1, source_target_pairs={{0,4},{4,0},{8,12},{12,8},{16,20},{20,16},{24,28},{28,24},{1,5},{5... | collective-permute-start | bytes 442376 | tf_op jit(solution)/shard_map/ppermute | solution.py:20
  17.0 2.5 %collective-permute-start.5 = (bf16[1,384,384]{2,1,0:T(8,128)(2,1)S(1)}, bf16[1,384,384]{2,1,0:T(8,128)(2,1)S(1)}, u32[]{:S(2)}, u32[]{:S(2)}) collective-permute-start(bf16[1,384,384]{2,1,0:T(8,128)(2,1)S(1)} %collective-permute-done.2.refs_1_), channel_id=1, source_target_pairs={{0,1},{1,0},{2,3},{3,2},{4,5},{5,4},{6,7},{7,6},{8,9},{9,8},{10,11... | collective-permute-start | bytes 884744 | tf_op jit(solution)/shard_map/ppermute | solution.py:20
  17.0 2.4 %collective-permute-start.6 = (bf16[192,384]{1,0:T(8,128)(2,1)S(1)}, bf16[192,384]{1,0:T(8,128)(2,1)S(1)}, u32[]{:S(2)}, u32[]{:S(2)}) collective-permute-start(bf16[192,384]{1,0:T(8,128)(2,1)S(1)} %collective-permute-done.1.refs_3_), channel_id=1, source_target_pairs={{0,1},{1,0},{2,3},{3,2},{4,5},{5,4},{6,7},{7,6},{8,9},{9,8},{10,11... | collective-permute-start | bytes 442376 | tf_op jit(solution)/shard_map/ppermute | solution.py:20
  21.4 7.2 %collective-permute-start.10 = (bf16[2,48,384]{2,1,0:T(8,128)(2,1)S(1)}, bf16[2,48,384]{2,1,0:T(8,128)(2,1)S(1)}, u32[]{:S(2)}, u32[]{:S(2)}) collective-permute-start(bf16[2,48,384]{2,1,0:T(8,128)(2,1)S(1)} %get-tuple-element.36), channel_id=1, source_target_pairs={{0,12},{4,8},{8,4},{12,0},{16,28},{20,24},{24,20},{28,16},{1,13},{... | collective-permute-start | bytes 221192 | tf_op jit(solution)/shard_map/ppermute | solution.py:20
  23.8 5.6 %collective-permute-start.11 = (bf16[2,48,384]{2,1,0:T(8,128)(2,1)S(1)}, bf16[2,48,384]{2,1,0:T(8,128)(2,1)S(1)}, u32[]{:S(2)}, u32[]{:S(2)}) collective-permute-start(bf16[2,48,384]{2,1,0:T(8,128)(2,1)S(1)} %get-tuple-element.37), channel_id=1, source_target_pairs={{0,4},{4,0},{8,12},{12,8},{16,20},{20,16},{24,28},{28,24},{1,5},{5... | collective-permute-start | bytes 221192 | tf_op jit(solution)/shard_map/ppermute | solution.py:20
  25.1 5.1 %collective-permute-start.12 = (bf16[2,48,384]{2,1,0:T(8,128)(2,1)S(1)}, bf16[2,48,384]{2,1,0:T(8,128)(2,1)S(1)}, u32[]{:S(2)}, u32[]{:S(2)}) collective-permute-start(bf16[2,48,384]{2,1,0:T(8,128)(2,1)S(1)} %get-tuple-element.38), channel_id=1, source_target_pairs={{0,8},{4,12},{8,0},{12,4},{16,24},{20,28},{24,16},{28,20},{1,9},{5... | collective-permute-start | bytes 221192 | tf_op jit(solution)/shard_map/ppermute | solution.py:20
  25.4 7.1 %collective-permute-start.7 = (bf16[2,48,384]{2,1,0:T(8,128)(2,1)S(1)}, bf16[2,48,384]{2,1,0:T(8,128)(2,1)S(1)}, u32[]{:S(2)}, u32[]{:S(2)}) collective-permute-start(bf16[2,48,384]{2,1,0:T(8,128)(2,1)S(1)} %get-tuple-element.32), channel_id=1, source_target_pairs={{0,12},{4,8},{8,4},{12,0},{16,28},{20,24},{24,20},{28,16},{1,13},{... | collective-permute-start | bytes 221192 | tf_op jit(solution)/shard_map/ppermute | solution.py:20
  27.3 5.6 %collective-permute-start.8 = (bf16[2,48,384]{2,1,0:T(8,128)(2,1)S(1)}, bf16[2,48,384]{2,1,0:T(8,128)(2,1)S(1)}, u32[]{:S(2)}, u32[]{:S(2)}) collective-permute-start(bf16[2,48,384]{2,1,0:T(8,128)(2,1)S(1)} %get-tuple-element.33), channel_id=1, source_target_pairs={{0,4},{4,0},{8,12},{12,8},{16,20},{20,16},{24,28},{28,24},{1,5},{5... | collective-permute-start | bytes 221192 | tf_op jit(solution)/shard_map/ppermute | solution.py:20
  28.6 4.4 %collective-permute-start.9 = (bf16[2,48,384]{2,1,0:T(8,128)(2,1)S(1)}, bf16[2,48,384]{2,1,0:T(8,128)(2,1)S(1)}, u32[]{:S(2)}, u32[]{:S(2)}) collective-permute-start(bf16[2,48,384]{2,1,0:T(8,128)(2,1)S(1)} %get-tuple-element.34), channel_id=1, source_target_pairs={{0,8},{4,12},{8,0},{12,4},{16,24},{20,28},{24,16},{28,20},{1,9},{5... | collective-permute-start | bytes 221192 | tf_op jit(solution)/shard_map/ppermute | solution.py:20
  30.2 6.5 %collective-permute-start.13 = (bf16[2,48,384]{2,1,0:T(8,128)(2,1)S(1)}, bf16[2,48,384]{2,1,0:T(8,128)(2,1)S(1)}, u32[]{:S(2)}, u32[]{:S(2)}) collective-permute-start(bf16[2,48,384]{2,1,0:T(8,128)(2,1)S(1)} %add_convert_fusion.1), channel_id=1, source_target_pairs={{0,16},{4,20},{8,24},{12,28},{16,0},{20,4},{24,8},{28,12},{1,17},{... | collective-permute-start | bytes 221192 | tf_op jit(solution)/shard_map/ppermute | solution.py:20
where the time goes:
time: 37 us; the launch traced here: 37.5 us
  starting transfers between devices  15.4 us (42%)
  Pallas kernels  11.5 us (31%)
  waiting for transfers between devices  6.86 us (19%)
  local copies, waits for them, and re-layouts  1.9 us (5%)
  other arithmetic  1.64 us (4%)
    ppermute x14, starting transfers between devices, flip(): return lax.ppermute(x, axis, [(i, i ^ bit) for i in range(size)])  15.4 us
    pallas_call x3, Pallas kernels, products(): pl.pallas_call(functools.partial(products_kernel, kind, n_opg), out_shape...  9.83 us
    ppermute x14, waiting for transfers between devices, flip(): return lax.ppermute(x, axis, [(i, i ^ bit) for i in range(size)])  6.86 us
    pallas_call x1, Pallas kernels, on_device(): pl.pallas_call(functools.partial(plan_kernel, local), out_shape=(jax.Shap...  1.71 us
    slice x1, local copies, waits for them, and re-layouts, on_device(): whole = {0: psi[:local - 1]}  1.17 us
    reduce_sum x1, other arithmetic, on_device(): jnp.sum(jnp.where(coef_index.T[:, :, None] == table, sixj, 0.0), axis=2)  0.85 us
  transfers between devices with their start and end apart: 14, of which 6 were waited for; matrix products, arithmetic and copies ran while one was open for 7% of the time, Pallas kernels for 26%

commit v1 on v0

--- a/solution.py
+++ b/solution.py
@@ -144,12 +144,12 @@
     else:
         half = lax.rem(lax.axis_index(OPG), HALVES)
         rows = sb // HALVES
-        for i in range(len(pieces) // 3):
-            whole, here, there = pieces[3 * i : 3 * i + 3]
+        for i in range(len(pieces) // 2):
+            whole, halves = pieces[2 * i : 2 * i + 2]
             end = (i + 1) * local - 1
             psi[i * local : end] = whole[...]
-            psi[end, pl.ds(pl.multiple_of(half * rows, 16), rows), :] = here[...]
-            psi[end, pl.ds(pl.multiple_of((1 - half) * rows, 16), rows), :] = there[...]
+            psi[end, pl.ds(pl.multiple_of(half * rows, 16), rows), :] = halves[0]
+            psi[end, pl.ds(pl.multiple_of((1 - half) * rows, 16), rows), :] = halves[1]
     run(kind, plan, scale, left, right, psi, acc, even, odd)
     if last:
         me_opg = lax.axis_index(OPG)
@@ -181,7 +181,7 @@
         in_specs=[SMEM] * 2 + [VMEM] * (2 + len(totals) + len(pieces)),
         out_specs=jax.tree.map(lambda _: VMEM, out_shape),
         scratch_shapes=[
-            pltpu.VMEM((len(pieces) // (3 if kind else 1) * local, sb, sb), jnp.bfloat16),
+            pltpu.VMEM((len(pieces) // (2 if kind else 1) * local, sb, sb), jnp.bfloat16),
             pltpu.VMEM((sb, sb), jnp.bfloat16),
             pltpu.VMEM((sb, sb), jnp.bfloat16),
             *scratch,
@@ -210,8 +210,9 @@
 
     half = lax.rem(lax.axis_index(OPG), HALVES)
     cut = psi[local - 1].reshape(HALVES, sb // HALVES, sb)
-    here = {0: lax.dynamic_index_in_dim(cut, half, axis=0, keepdims=False)}
-    whole = {0: psi[: local - 1]}
+    ours = lax.dynamic_index_in_dim(cut, half, axis=0, keepdims=False)
+    ours, rest, psi = lax.optimization_barrier((ours, psi[: local - 1], psi))
+    here, whole = {0: ours}, {0: rest}
     for bit in bits_of(n_sec)[1:]:
         for held in (here, whole):
             held.update({r | bit: flip(x, SEC, n_sec, bit) for r, x in held.items()})
@@ -242,13 +243,13 @@
 
     here, plan, scale = lax.optimization_barrier((here, plan, scale))
     there = [flip(x, OPG, n_opg, 1) for x in here]
-    here_crossed = to_other_core(here)
     done = onto(0, [], [psi, partner])
-    there, whole, here_crossed, done = lax.optimization_barrier((there, whole, here_crossed, done))
-    there_crossed, whole_crossed = to_other_core(there), to_other_core(whole)
-    done = onto(1, [done], [x for three in zip(whole, here, there) for x in three])
-    crossed = zip(whole_crossed, here_crossed, there_crossed)
-    sends = onto(2, [done], [x for three in crossed for x in three])
+    here, there, whole, done = lax.optimization_barrier((here, there, whole, done))
+    whole_crossed = to_other_core(whole)
+    halves = [jnp.stack(two) for two in zip(here, there)]
+    halves_crossed = to_other_core(halves)
+    done = onto(1, [done], [x for two in zip(whole, halves) for x in two])
+    sends = onto(2, [done], [x for two in zip(whole_crossed, halves_crossed) for x in two])
     return jnp.swapaxes(scatter_sum(sends, n_opg), 0, 1).astype(jnp.bfloat16)
 
 

time: 37 us -> 37.7 us (1.019); the launches traced: 37.5 us -> 37.5 us
  starting transfers between devices: 15.4 us -> 16.1 us
    ppermute x14 -> x13, starting transfers between devices: 15.4 us -> 16.1 us  [flip(): return lax.ppermute(x, axis, [(i, i ^ bit) for i in range(size)])]
    ppermute x14 -> x13, waiting for transfers between devices: 6.86 us -> 6.53 us  [flip(): return lax.ppermute(x, axis, [(i, i ^ bit) for i in range(size)])]
  transfers between devices with their start and end apart: 14 -> 13, of which waited for: 6 -> 5; matrix products, arithmetic and copies ran while one was open for 7% -> 4% of each run, Pallas kernels for 26% -> 23%
where the time goes in v1:
time: 37.7 us; the launch traced here: 37.5 us
  starting transfers between devices  16.1 us (43%)
  Pallas kernels  11.2 us (30%)
  waiting for transfers between devices  6.53 us (17%)
  local copies, waits for them, and re-layouts  1.9 us (5%)
  other arithmetic  1.68 us (4%)
    ppermute x13, starting transfers between devices, flip(): return lax.ppermute(x, axis, [(i, i ^ bit) for i in range(size)])  16.1 us
    pallas_call x3, Pallas kernels, products(): pl.pallas_call(functools.partial(products_kernel, kind, n_opg), out_shape...  9.47 us
    ppermute x13, waiting for transfers between devices, flip(): return lax.ppermute(x, axis, [(i, i ^ bit) for i in range(size)])  6.53 us
    pallas_call x1, Pallas kernels, on_device(): pl.pallas_call(functools.partial(plan_kernel, local), out_shape=(jax.Shap...  1.71 us
    slice x1, local copies, waits for them, and re-layouts, on_device(): ours, rest, psi = lax.optimization_barrier((ours, psi[:local - 1], psi))  1.17 us
    reduce_sum x1, other arithmetic, on_device(): jnp.sum(jnp.where(coef_index.T[:, :, None] == table, sixj, 0.0), axis=2)  0.85 us
  transfers between devices with their start and end apart: 13, of which 5 were waited for; matrix products, arithmetic and copies ran while one was open for 4% of the time, Pallas kernels for 23%

profile of v1, /device:TPU:0, one launch (start us, length us, event | category | flops | bytes accessed | tf_op | source)
XLA Modules:
  0.0 37.5 jit_solution(7506369266497029905)
XLA Ops:
  0.0 1.2 %fusion.1 = (bf16[1,384,384]{2,1,0:T(8,128)(2,1)S(1)}, bf16[1,384,384]{2,1,0:T(8,128)(2,1)S(1)}) fusion(bf16[2,384,384]{2,1,0:T(8,128)(2,1)} %refs_0_), kind=kLoop, calls=%fused_computation.9 | loop fusion | bytes 1179648 | tf_op jit(solution)/shard_map/slice | solution.py:214
  1.2 3.0 %collective-permute-start = (bf16[192,384]{1,0:T(8,128)(2,1)S(1)}, bf16[192,384]{1,0:T(8,128)(2,1)S(1)}, u32[]{:S(2)}, u32[]{:S(2)}) collective-permute-start(bf16[192,384]{1,0:T(8,128)(2,1)S(1)} %dynamic-slice_bitcast_fusion), channel_id=1, source_target_pairs={{0,2},{1,3},{2,0},{3,1},{4,6},{5,7},{6,4},{7,5},{8,10},{9,11},{10,... | collective-permute-start | bytes 442376 | tf_op jit(solution)/shard_map/ppermute | solution.py:20
  4.2 0.1 collective-permute-start.2
  4.3 0.0 collective-permute-start.3
  4.3 0.7 %convert_bitcast_fusion = f32[2,8]{1,0:T(2,128)S(1)} fusion(s32[8,2]{0,1:T(2,128)} %param.9), kind=kLoop, calls=%fused_computation.8 | loop fusion | flops 16 | bytes 128 | tf_op jit(solution)/shard_map/convert_element_type | solution.py:225
  5.0 0.8 %select_reduce_fusion = f32[2,8]{1,0:T(2,128)S(1)} fusion(f32[64]{0:T(128)} %param.11, s32[2,8]{1,0:T(2,128)} %bitcast.15), kind=kLoop, calls=%fused_computation.5 | loop fusion | flops 3056 | bytes 384 | tf_op jit(solution)/shard_map/reduce_sum | solution.py:224
  5.9 0.0 copy-start
  5.9 0.0 copy-start.1
  5.9 1.7 %shard_map.64 = (s32[3,49]{1,0:T(4,128)S(1)}, f32[3,16]{1,0:T(4,128)S(1)}) custom-call(f32[4,8]{1,0:T(4,128)S(1)} %pad_maximum_fusion.1.meta), custom_call_target="tpu_custom_call" | custom-call | flops 20000000000 | tf_op jit(solution)/shard_map/pallas_call | solution.py:226
  7.6 1.3 %collective-permute-done = bf16[192,384]{1,0:T(8,128)(2,1)S(1)} collective-permute-done((bf16[192,384]{1,0:T(8,128)(2,1)S(1)}, bf16[192,384]{1,0:T(8,128)(2,1)S(1)}, u32[]{:S(2)}, u32[]{:S(2)}) %collective-permute-start) | collective-permute-done | bytes 147488 | tf_op jit(solution)/shard_map/ppermute | solution.py:20
  8.9 2.0 %collective-permute-start.1 = (bf16[192,384]{1,0:T(8,128)(2,1)S(1)}, bf16[192,384]{1,0:T(8,128)(2,1)S(1)}, u32[]{:S(2)}, u32[]{:S(2)}) collective-permute-start(bf16[192,384]{1,0:T(8,128)(2,1)S(1)} %collective-permute-done), channel_id=1, source_target_pairs={{0,4},{4,0},{8,12},{12,8},{16,20},{20,16},{24,28},{28,24},{1,5},{5... | collective-permute-start | bytes 442376 | tf_op jit(solution)/shard_map/ppermute | solution.py:20
  11.0 6.0 %shard_map.65.refs_0_ = f32[2,384,384]{2,1,0:T(8,128)S(1)} custom-call(s32[3,49]{1,0:T(4,128)S(1)} %get-tuple-element.28.plan, f32[3,16]{1,0:T(4,128)S(1)} %get-tuple-element.29.scale, bf16[8,2,384,384]{3,2,1,0:T(8,128)(2,1)S(1)} %bitcast.11, bf16[8,2,384,384]{3,2,1,0:T(8,128)(2,1)S(1)} %copy-done, bf16[2,384,384]{2,1,0:T(8,128)(2,1)S(1)} %copy-done.1, ...), custom_call_target="tpu_custom_call" | custom-call | flops 384 | tf_op jit(solution)/shard_map/pallas_call | solution.py:178
  17.0 0.0 collective-permute-done.1
  17.0 0.0 collective-permute-done.2.refs_1_
  17.1 0.1 collective-permute-start.5
  17.1 0.5 %collective-permute-start.4 = (bf16[1,384,384]{2,1,0:T(8,128)(2,1)S(1)}, bf16[1,384,384]{2,1,0:T(8,128)(2,1)S(1)}, u32[]{:S(2)}, u32[]{:S(2)}) collective-permute-start(bf16[1,384,384]{2,1,0:T(8,128)(2,1)S(1)} %collective-permute-done.2.refs_1_), channel_id=1, source_target_pairs={{0,1},{1,0},{2,3},{3,2},{4,5},{5,4},{6,7},{7,6},{8,9},{9,8},{10,11... | collective-permute-start | bytes 884744 | tf_op jit(solution)/shard_map/ppermute | solution.py:20
  17.6 0.7 %shard_map.66.refs_0_ = f32[2,384,384]{2,1,0:T(8,128)S(1)} custom-call(s32[3,49]{1,0:T(4,128)S(1)} %get-tuple-element.28.plan, f32[3,16]{1,0:T(4,128)S(1)} %get-tuple-element.29.scale, bf16[8,2,384,384]{3,2,1,0:T(8,128)(2,1)S(1)} %bitcast.11, bf16[8,2,384,384]{3,2,1,0:T(8,128)(2,1)S(1)} %copy-done, f32[2,384,384]{2,1,0:T(8,128)S(1)} %shard_map.65.refs_0_, ...), custom_call_target="tpu_custom_call" | custom-call | flops 384 | tf_op jit(solution)/shard_map/pallas_call | solution.py:178
  18.4 0.3 collective-permute-done.5.refs_2_
  18.7 0.4 %collective-permute-done.4.refs_1_ = bf16[1,384,384]{2,1,0:T(8,128)(2,1)S(1)} collective-permute-done((bf16[1,384,384]{2,1,0:T(8,128)(2,1)S(1)}, bf16[1,384,384]{2,1,0:T(8,128)(2,1)S(1)}, u32[]{:S(2)}, u32[]{:S(2)}) %collective-permute-start.4) | collective-permute-done | bytes 294944 | tf_op jit(solution)/shard_map/ppermute | solution.py:20
  19.1 2.7 %shard_map.67 = (f32[2,48,384]{2,1,0:T(8,128)S(1)}, bf16[2,48,384]{2,1,0:T(8,128)(2,1)S(1)}, bf16[2,48,384]{2,1,0:T(8,128)(2,1)S(1)}, bf16[2,48,384]{2,1,0:T(8,1...) custom-call(s32[3,49]{1,0:T(4,128)S(1)} %get-tuple-element.28.plan, ...), custom_call_target="tpu_custom_call" | custom-call | flops 384 | tf_op jit(solution)/shard_map/pallas_call | solution.py:178
  21.9 1.2 %collective-permute-start.9 = (bf16[2,48,384]{2,1,0:T(8,128)(2,1)S(1)}, bf16[2,48,384]{2,1,0:T(8,128)(2,1)S(1)}, u32[]{:S(2)}, u32[]{:S(2)}) collective-permute-start(bf16[2,48,384]{2,1,0:T(8,128)(2,1)S(1)} %get-tuple-element.42), channel_id=1, source_target_pairs={{0,12},{4,8},{8,4},{12,0},{16,28},{20,24},{24,20},{28,16},{1,13},{... | collective-permute-start | bytes 221192 | tf_op jit(solution)/shard_map/ppermute | solution.py:20
  23.1 1.4 %collective-permute-start.10 = (bf16[2,48,384]{2,1,0:T(8,128)(2,1)S(1)}, bf16[2,48,384]{2,1,0:T(8,128)(2,1)S(1)}, u32[]{:S(2)}, u32[]{:S(2)}) collective-permute-start(bf16[2,48,384]{2,1,0:T(8,128)(2,1)S(1)} %get-tuple-element.43), channel_id=1, source_target_pairs={{0,4},{4,0},{8,12},{12,8},{16,20},{20,16},{24,28},{28,24},{1,5},{5... | collective-permute-start | bytes 221192 | tf_op jit(solution)/shard_map/ppermute | solution.py:20
  24.5 0.9 %collective-permute-start.11 = (bf16[2,48,384]{2,1,0:T(8,128)(2,1)S(1)}, bf16[2,48,384]{2,1,0:T(8,128)(2,1)S(1)}, u32[]{:S(2)}, u32[]{:S(2)}) collective-permute-start(bf16[2,48,384]{2,1,0:T(8,128)(2,1)S(1)} %get-tuple-element.44), channel_id=1, source_target_pairs={{0,8},{4,12},{8,0},{12,4},{16,24},{20,28},{24,16},{28,20},{1,9},{5... | collective-permute-start | bytes 221192 | tf_op jit(solution)/shard_map/ppermute | solution.py:20
  25.4 1.1 %collective-permute-start.6 = (bf16[2,48,384]{2,1,0:T(8,128)(2,1)S(1)}, bf16[2,48,384]{2,1,0:T(8,128)(2,1)S(1)}, u32[]{:S(2)}, u32[]{:S(2)}) collective-permute-start(bf16[2,48,384]{2,1,0:T(8,128)(2,1)S(1)} %get-tuple-element.38), channel_id=1, source_target_pairs={{0,12},{4,8},{8,4},{12,0},{16,28},{20,24},{24,20},{28,16},{1,13},{... | collective-permute-start | bytes 221192 | tf_op jit(solution)/shard_map/ppermute | solution.py:20
  26.6 1.4 %collective-permute-start.7 = (bf16[2,48,384]{2,1,0:T(8,128)(2,1)S(1)}, bf16[2,48,384]{2,1,0:T(8,128)(2,1)S(1)}, u32[]{:S(2)}, u32[]{:S(2)}) collective-permute-start(bf16[2,48,384]{2,1,0:T(8,128)(2,1)S(1)} %get-tuple-element.39), channel_id=1, source_target_pairs={{0,4},{4,0},{8,12},{12,8},{16,20},{20,16},{24,28},{28,24},{1,5},{5... | collective-permute-start | bytes 221192 | tf_op jit(solution)/shard_map/ppermute | solution.py:20
  28.0 0.9 %collective-permute-start.8 = (bf16[2,48,384]{2,1,0:T(8,128)(2,1)S(1)}, bf16[2,48,384]{2,1,0:T(8,128)(2,1)S(1)}, u32[]{:S(2)}, u32[]{:S(2)}) collective-permute-start(bf16[2,48,384]{2,1,0:T(8,128)(2,1)S(1)} %get-tuple-element.40), channel_id=1, source_target_pairs={{0,8},{4,12},{8,0},{12,4},{16,24},{20,28},{24,16},{28,20},{1,9},{5... | collective-permute-start | bytes 221192 | tf_op jit(solution)/shard_map/ppermute | solution.py:20
  28.9 0.0 collective-permute-done.10
  29.0 3.3 %collective-permute-start.12 = (bf16[2,48,384]{2,1,0:T(8,128)(2,1)S(1)}, bf16[2,48,384]{2,1,0:T(8,128)(2,1)S(1)}, u32[]{:S(2)}, u32[]{:S(2)}) collective-permute-start(bf16[2,48,384]{2,1,0:T(8,128)(2,1)S(1)} %add_convert_fusion.1), channel_id=1, source_target_pairs={{0,16},{4,20},{8,24},{12,28},{16,0},{20,4},{24,8},{28,12},{1,17},{... | collective-permute-start | bytes 221192 | tf_op jit(solution)/shard_map/ppermute | solution.py:20
  32.3 0.8 %collective-permute-done.7 = bf16[2,48,384]{2,1,0:T(8,128)(2,1)S(1)} collective-permute-done((bf16[2,48,384]{2,1,0:T(8,128)(2,1)S(1)}, bf16[2,48,384]{2,1,0:T(8,128)(2,1)S(1)}, u32[]{:S(2)}, u32[]{:S(2)}) %collective-permute-start.7) | collective-permute-done | bytes 73760 | tf_op jit(solution)/shard_map/ppermute | solution.py:20
  33.1 3.7 %collective-permute-done.12 = bf16[2,48,384]{2,1,0:T(8,128)(2,1)S(1)} collective-permute-done((bf16[2,48,384]{2,1,0:T(8,128)(2,1)S(1)}, bf16[2,48,384]{2,1,0:T(8,128)(2,1)S(1)}, u32[]{:S(2)}, u32[]{:S(2)}) %collective-permute-start.12) | collective-permute-done | bytes 73760 | tf_op jit(solution)/shard_map/ppermute | solution.py:20
  36.8 0.1 fusion
  36.8 0.7 %copy.8 = bf16[48,2,384]{2,1,0:T(2,128)(2,1)} copy(bf16[48,2,384]{2,0,1:T(8,128)(2,1)S(1)} %fusion) | data formatting | bytes 147456 | tf_op jit(solution)/shard_map/convert_element_type | solution.py:253
  (16 shorter events, 0.1 us)
Async XLA Ops:
  0.0 11.0 %slice-start = ((s8[4718592]{0:T(1024)(128)(4,1)}), s8[524288]{0:T(1024)(128)(4,1)S(1)}, s32[]{:S(2)}) async-start(s8[4718592]{0:T(1024)(128)(4,1)} %bitcast.10), calls=%async_computation | async-start | bytes 1048576
  1.2 7.7 %collective-permute-start = (bf16[192,384]{1,0:T(8,128)(2,1)S(1)}, bf16[192,384]{1,0:T(8,128)(2,1)S(1)}, u32[]{:S(2)}, u32[]{:S(2)}) collective-permute-start(bf16[192,384]{1,0:T(8,128)(2,1)S(1)} %dynamic-slice_bitcast_fusion), channel_id=1, source_target_pairs={{0,2},{1,3},{2,0},{3,1},{4,6},{5,7},{6,4},{7,5},{8,10},{9,11},{10,... | collective-permute-start | bytes 442376 | tf_op jit(solution)/shard_map/ppermute | solution.py:20
  4.2 12.8 %collective-permute-start.2 = (bf16[1,384,384]{2,1,0:T(8,128)(2,1)S(1)}, bf16[1,384,384]{2,1,0:T(8,128)(2,1)S(1)}, u32[]{:S(2)}, u32[]{:S(2)}) collective-permute-start(bf16[1,384,384]{2,1,0:T(8,128)(2,1)S(1)} %get-tuple-element.31), channel_id=1, source_target_pairs={{0,2},{1,3},{2,0},{3,1},{4,6},{5,7},{6,4},{7,5},{8,10},{9,11},{10,... | collective-permute-start | bytes 884744 | tf_op jit(solution)/shard_map/ppermute | solution.py:20
  4.3 6.6 %collective-permute-start.3 = (bf16[2,384,384]{2,1,0:T(8,128)(2,1)}, bf16[2,384,384]{2,1,0:T(8,128)(2,1)S(1)}, u32[]{:S(2)}, u32[]{:S(2)}) collective-permute-start(bf16[2,384,384]{2,1,0:T(8,128)(2,1)} %refs_0_), channel_id=1, source_target_pairs={{0,1},{1,0},{2,3},{3,2},{4,5},{5,4},{6,7},{7,6},{8,9},{9,8},{10,11... | collective-permute-start | bytes 1769480 | tf_op jit(solution)/shard_map/ppermute | solution.py:20
  5.9 5.1 %slice-start.1 = ((s8[4718592]{0:T(1024)(128)(4,1)}), s8[4194304]{0:T(1024)(128)(4,1)S(1)}, s32[]{:S(2)}) async-start(s8[4718592]{0:T(1024)(128)(4,1)} %bitcast.10), calls=%async_computation.1 | async-start | bytes 8388608
  5.9 5.1 %copy-start = (bf16[8,2,384,384]{3,2,1,0:T(8,128)(2,1)S(1)}, bf16[8,2,384,384]{3,2,1,0:T(8,128)(2,1)}, u32[]{:S(2)}) copy-start(bf16[8,2,384,384]{3,2,1,0:T(8,128)(2,1)} %right.5) | copy-start | bytes 14155780
  5.9 5.1 %copy-start.1 = (bf16[2,384,384]{2,1,0:T(8,128)(2,1)S(1)}, bf16[2,384,384]{2,1,0:T(8,128)(2,1)}, u32[]{:S(2)}) copy-start(bf16[2,384,384]{2,1,0:T(8,128)(2,1)} %refs_0_) | copy-start | bytes 1769476
  8.9 8.1 %collective-permute-start.1 = (bf16[192,384]{1,0:T(8,128)(2,1)S(1)}, bf16[192,384]{1,0:T(8,128)(2,1)S(1)}, u32[]{:S(2)}, u32[]{:S(2)}) collective-permute-start(bf16[192,384]{1,0:T(8,128)(2,1)S(1)} %collective-permute-done), channel_id=1, source_target_pairs={{0,4},{4,0},{8,12},{12,8},{16,20},{20,16},{24,28},{28,24},{1,5},{5... | collective-permute-start | bytes 442376 | tf_op jit(solution)/shard_map/ppermute | solution.py:20
  17.1 1.6 %collective-permute-start.5 = (bf16[2,192,384]{2,1,0:T(8,128)(2,1)S(1)}, bf16[2,192,384]{2,1,0:T(8,128)(2,1)S(1)}, u32[]{:S(2)}, u32[]{:S(2)}) collective-permute-start(bf16[2,192,384]{2,1,0:T(8,128)(2,1)S(1)} %pad_maximum_fusion.refs_2_), channel_id=1, source_target_pairs={{0,1},{1,0},{2,3},{3,2},{4,5},{5,4},{6,7},{7,6},{8,9},{9,8},{10,11... | collective-permute-start | bytes 884744 | tf_op jit(solution)/shard_map/ppermute | solution.py:20
  17.1 2.0 %collective-permute-start.4 = (bf16[1,384,384]{2,1,0:T(8,128)(2,1)S(1)}, bf16[1,384,384]{2,1,0:T(8,128)(2,1)S(1)}, u32[]{:S(2)}, u32[]{:S(2)}) collective-permute-start(bf16[1,384,384]{2,1,0:T(8,128)(2,1)S(1)} %collective-permute-done.2.refs_1_), channel_id=1, source_target_pairs={{0,1},{1,0},{2,3},{3,2},{4,5},{5,4},{6,7},{7,6},{8,9},{9,8},{10,11... | collective-permute-start | bytes 884744 | tf_op jit(solution)/shard_map/ppermute | solution.py:20
  21.9 6.1 %collective-permute-start.9 = (bf16[2,48,384]{2,1,0:T(8,128)(2,1)S(1)}, bf16[2,48,384]{2,1,0:T(8,128)(2,1)S(1)}, u32[]{:S(2)}, u32[]{:S(2)}) collective-permute-start(bf16[2,48,384]{2,1,0:T(8,128)(2,1)S(1)} %get-tuple-element.42), channel_id=1, source_target_pairs={{0,12},{4,8},{8,4},{12,0},{16,28},{20,24},{24,20},{28,16},{1,13},{... | collective-permute-start | bytes 221192 | tf_op jit(solution)/shard_map/ppermute | solution.py:20
  23.1 5.9 %collective-permute-start.10 = (bf16[2,48,384]{2,1,0:T(8,128)(2,1)S(1)}, bf16[2,48,384]{2,1,0:T(8,128)(2,1)S(1)}, u32[]{:S(2)}, u32[]{:S(2)}) collective-permute-start(bf16[2,48,384]{2,1,0:T(8,128)(2,1)S(1)} %get-tuple-element.43), channel_id=1, source_target_pairs={{0,4},{4,0},{8,12},{12,8},{16,20},{20,16},{24,28},{28,24},{1,5},{5... | collective-permute-start | bytes 221192 | tf_op jit(solution)/shard_map/ppermute | solution.py:20
  24.5 4.4 %collective-permute-start.11 = (bf16[2,48,384]{2,1,0:T(8,128)(2,1)S(1)}, bf16[2,48,384]{2,1,0:T(8,128)(2,1)S(1)}, u32[]{:S(2)}, u32[]{:S(2)}) collective-permute-start(bf16[2,48,384]{2,1,0:T(8,128)(2,1)S(1)} %get-tuple-element.44), channel_id=1, source_target_pairs={{0,8},{4,12},{8,0},{12,4},{16,24},{20,28},{24,16},{28,20},{1,9},{5... | collective-permute-start | bytes 221192 | tf_op jit(solution)/shard_map/ppermute | solution.py:20
  25.4 6.9 %collective-permute-start.6 = (bf16[2,48,384]{2,1,0:T(8,128)(2,1)S(1)}, bf16[2,48,384]{2,1,0:T(8,128)(2,1)S(1)}, u32[]{:S(2)}, u32[]{:S(2)}) collective-permute-start(bf16[2,48,384]{2,1,0:T(8,128)(2,1)S(1)} %get-tuple-element.38), channel_id=1, source_target_pairs={{0,12},{4,8},{8,4},{12,0},{16,28},{20,24},{24,20},{28,16},{1,13},{... | collective-permute-start | bytes 221192 | tf_op jit(solution)/shard_map/ppermute | solution.py:20
  26.6 6.5 %collective-permute-start.7 = (bf16[2,48,384]{2,1,0:T(8,128)(2,1)S(1)}, bf16[2,48,384]{2,1,0:T(8,128)(2,1)S(1)}, u32[]{:S(2)}, u32[]{:S(2)}) collective-permute-start(bf16[2,48,384]{2,1,0:T(8,128)(2,1)S(1)} %get-tuple-element.39), channel_id=1, source_target_pairs={{0,4},{4,0},{8,12},{12,8},{16,20},{20,16},{24,28},{28,24},{1,5},{5... | collective-permute-start | bytes 221192 | tf_op jit(solution)/shard_map/ppermute | solution.py:20
  28.0 5.1 %collective-permute-start.8 = (bf16[2,48,384]{2,1,0:T(8,128)(2,1)S(1)}, bf16[2,48,384]{2,1,0:T(8,128)(2,1)S(1)}, u32[]{:S(2)}, u32[]{:S(2)}) collective-permute-start(bf16[2,48,384]{2,1,0:T(8,128)(2,1)S(1)} %get-tuple-element.40), channel_id=1, source_target_pairs={{0,8},{4,12},{8,0},{12,4},{16,24},{20,28},{24,16},{28,20},{1,9},{5... | collective-permute-start | bytes 221192 | tf_op jit(solution)/shard_map/ppermute | solution.py:20
  29.0 7.8 %collective-permute-start.12 = (bf16[2,48,384]{2,1,0:T(8,128)(2,1)S(1)}, bf16[2,48,384]{2,1,0:T(8,128)(2,1)S(1)}, u32[]{:S(2)}, u32[]{:S(2)}) collective-permute-start(bf16[2,48,384]{2,1,0:T(8,128)(2,1)S(1)} %add_convert_fusion.1), channel_id=1, source_target_pairs={{0,16},{4,20},{8,24},{12,28},{16,0},{20,4},{24,8},{28,12},{1,17},{... | collective-permute-start | bytes 221192 | tf_op jit(solution)/shard_map/ppermute | solution.py:20

commit v2 on v1

--- a/solution.py
+++ b/solution.py
@@ -27,7 +27,7 @@
 CLASSES = 3
 
 
-def make_plan(meta, plan, scale, pairs, local):
+def make_plan(source, plan, pairs, local):
     slots = local * pairs
     for kind in range(CLASSES):
         plan[kind, 3 * slots] = 0
@@ -35,7 +35,7 @@
 
     def sector(s):
         def one(p, carry):
-            src = meta[s, p].astype(jnp.int32)
+            src = source[s, p]
             r, j = lax.div(src, local) ^ me_sec, lax.rem(src, local)
             kind = jnp.where(r < NEAR, 0, 1 + lax.rem(r, 2))
             block = jnp.where(r < NEAR, r, lax.div(r, 2) - 1) * local + j
@@ -43,7 +43,6 @@
             plan[kind, n] = p
             plan[kind, slots + n] = s
             plan[kind, 2 * slots + n] = block
-            scale[kind, n] = meta[local + s, p]
             plan[kind, 3 * slots] = n + 1
             return carry
 
@@ -88,7 +87,7 @@
     return list(zip(cut, (p[:, low] + q[:, high], p[:, high] + r[:, high], q[:, low] + r[:, low])))
 
 
-def run(kind, plan, scale, left, right, psi, acc, even, odd):
+def run(kind, plan, coef, left, right, psi, acc, even, odd):
     pairs, local = left.shape[:2]
     slots = local * pairs
     count = plan[kind, 3 * slots]
@@ -97,7 +96,7 @@
         i = jnp.minimum(i, count - 1)
         p, s, block = [plan[kind, k * slots + i] for k in range(3)]
         for c, half in thirds(left.at[p, s], psi.at[block], False):
-            halves[:, c] = (half * scale[kind, i]).astype(jnp.bfloat16)
+            halves[:, c] = (half * coef[s, p]).astype(jnp.bfloat16)
 
     def second(i, halves):
         p, s = [plan[kind, k * slots + i] for k in range(2)]
@@ -122,11 +121,11 @@
             second(count - 1, even)
 
 
-def plan_kernel(local, meta, plan, scale):
-    make_plan(meta, plan, scale, meta.shape[1], local)
-
-
-def products_kernel(kind, n_opg, plan, scale, left, right, *refs):
+def plan_kernel(local, source, plan):
+    make_plan(source, plan, source.shape[1], local)
+
+
+def products_kernel(kind, n_opg, plan, coef, left, right, *refs):
     local, sb = left.shape[1:3]
     last = kind == CLASSES - 1
     outs = n_opg if last else 1
@@ -138,19 +137,12 @@
         pieces = pieces[1:]
     else:
         acc[...] = jnp.zeros_like(acc)
-    if kind == 0:
+    if len(pieces) == 1:
+        psi = pieces[0]
+    else:
         for i, piece in enumerate(pieces):
             psi[i * local : (i + 1) * local] = piece[...]
-    else:
-        half = lax.rem(lax.axis_index(OPG), HALVES)
-        rows = sb // HALVES
-        for i in range(len(pieces) // 2):
-            whole, halves = pieces[2 * i : 2 * i + 2]
-            end = (i + 1) * local - 1
-            psi[i * local : end] = whole[...]
-            psi[end, pl.ds(pl.multiple_of(half * rows, 16), rows), :] = halves[0]
-            psi[end, pl.ds(pl.multiple_of((1 - half) * rows, 16), rows), :] = halves[1]
-    run(kind, plan, scale, left, right, psi, acc, even, odd)
+    run(kind, plan, coef, left, right, psi, acc, even, odd)
     if last:
         me_opg = lax.axis_index(OPG)
         rows = sb // n_opg
@@ -163,7 +155,7 @@
 VMEM = pl.BlockSpec(memory_space=pltpu.VMEM)
 
 
-def products(kind, n_opg, plan, scale, left, right, totals, pieces):
+def products(kind, n_opg, plan, coef, left, right, totals, pieces):
     pairs, local, sb, _ = left.shape
     out_shape = jax.ShapeDtypeStruct((local, sb, sb), jnp.float32)
     scratch = []
@@ -181,14 +173,14 @@
         in_specs=[SMEM] * 2 + [VMEM] * (2 + len(totals) + len(pieces)),
         out_specs=jax.tree.map(lambda _: VMEM, out_shape),
         scratch_shapes=[
-            pltpu.VMEM((len(pieces) // (2 if kind else 1) * local, sb, sb), jnp.bfloat16),
+            pltpu.VMEM((len(pieces) * local, sb, sb), jnp.bfloat16),
             pltpu.VMEM((sb, sb), jnp.bfloat16),
             pltpu.VMEM((sb, sb), jnp.bfloat16),
             *scratch,
         ],
         compiler_params=pltpu.CompilerParams(vmem_limit_bytes=KERNEL_VMEM),
         cost_estimate=pl.CostEstimate(flops=sb, bytes_accessed=0, transcendentals=0),
-    )(plan, scale, left, right, *totals, *pieces)
+    )(plan, coef, left, right, *totals, *pieces)
 
 
 def scatter_sum(sends, n_opg):
@@ -220,36 +212,36 @@
     here, whole = [here[r] for r in far], [whole[r] for r in far]
     partner = flip(psi, SEC, n_sec, 1)
 
+    plan = pl.pallas_call(
+        functools.partial(plan_kernel, local),
+        out_shape=jax.ShapeDtypeStruct((CLASSES, 3 * local * pairs + 1), jnp.int32),
+        in_specs=[SMEM],
+        out_specs=SMEM,
+        compiler_params=pltpu.CompilerParams(vmem_limit_bytes=KERNEL_VMEM),
+        cost_estimate=pl.CostEstimate(flops=PLAN_FLOPS, bytes_accessed=0, transcendentals=0),
+    )(source.T)
+    plan, coef_index = lax.optimization_barrier((plan, coef_index))
     table = jnp.arange(sixj.shape[0], dtype=jnp.int32)
     coef = jnp.sum(jnp.where(coef_index.T[:, :, None] == table, sixj, 0.0), axis=2)
-    meta = jnp.concatenate([source.T.astype(jnp.float32), coef])
-    plan, scale = pl.pallas_call(
-        functools.partial(plan_kernel, local),
-        out_shape=(
-            jax.ShapeDtypeStruct((CLASSES, 3 * local * pairs + 1), jnp.int32),
-            jax.ShapeDtypeStruct((CLASSES, local * pairs), jnp.float32),
-        ),
-        in_specs=[SMEM],
-        out_specs=(SMEM, SMEM),
-        compiler_params=pltpu.CompilerParams(vmem_limit_bytes=KERNEL_VMEM),
-        cost_estimate=pl.CostEstimate(flops=PLAN_FLOPS, bytes_accessed=0, transcendentals=0),
-    )(meta)
 
     def onto(kind, totals, pieces):
-        return products(kind, n_opg, plan, scale, left_ops, right_ops, totals, pieces)
+        return products(kind, n_opg, plan, coef, left_ops, right_ops, totals, pieces)
 
     def to_other_core(pieces):
         return [flip(x, SEC, n_sec, 1) for x in pieces]
 
-    here, plan, scale = lax.optimization_barrier((here, plan, scale))
+    here, plan, coef = lax.optimization_barrier((here, plan, coef))
     there = [flip(x, OPG, n_opg, 1) for x in here]
     done = onto(0, [], [psi, partner])
     here, there, whole, done = lax.optimization_barrier((here, there, whole, done))
-    whole_crossed = to_other_core(whole)
-    halves = [jnp.stack(two) for two in zip(here, there)]
-    halves_crossed = to_other_core(halves)
-    done = onto(1, [done], [x for two in zip(whole, halves) for x in two])
-    sends = onto(2, [done], [x for two in zip(whole_crossed, halves_crossed) for x in two])
+    twins = []
+    for one, other, rest in zip(here, there, whole):
+        upper, lower = jnp.where(half == 0, one, other), jnp.where(half == 0, other, one)
+        rows = jnp.concatenate([rest.reshape(-1, sb), upper, lower])
+        twins.append(rows.reshape(local, sb, sb))
+    others = to_other_core(twins)
+    done = onto(1, [done], twins)
+    sends = onto(2, [done], others)
     return jnp.swapaxes(scatter_sum(sends, n_opg), 0, 1).astype(jnp.bfloat16)
 
 

time: 37.7 us -> 41.6 us (1.10)
  local copies, waits for them, and re-layouts: 1.9 us -> 6.58 us
  other arithmetic: 1.68 us -> 0.35 us
  waiting for transfers between devices: 6.53 us -> 7.18 us
    unnamed x8 -> x12, local copies, waits for them, and re-layouts: 0.02 us -> 4.69 us
    reduce_sum x1, other arithmetic: 0.85 us -> 0.16 us  [on_device(): jnp.sum(jnp.where(coef_index.T[:, :, None] == table, sixj, 0.0), axis=2)]
    convert_element_type x1 -> x0, other arithmetic: 0.68 us -> none  [on_device(): meta = jnp.concatenate([source.T.astype(jnp.float32), coef])]
    ppermute x13 -> x12, waiting for transfers between devices: 6.53 us -> 7.18 us  [flip(): return lax.ppermute(x, axis, [(i, i ^ bit) for i in range(size)])]
    ppermute x13 -> x12, starting transfers between devices: 16.1 us -> 15.8 us  [flip(): return lax.ppermute(x, axis, [(i, i ^ bit) for i in range(size)])]
  transfers between devices with their start and end apart: 13 -> 12, of which waited for: 5 -> 4; matrix products, arithmetic and copies ran while one was open for 4% -> 0% of each run, Pallas kernels for 23% -> 20%
where the time goes in v2:
time: 41.6 us; the launch traced here: 41.2 us
  starting transfers between devices  15.8 us (38%)
  Pallas kernels  11.1 us (27%)
  waiting for transfers between devices  7.18 us (17%)
  local copies, waits for them, and re-layouts  6.58 us (16%)
    ppermute x12, starting transfers between devices, flip(): return lax.ppermute(x, axis, [(i, i ^ bit) for i in range(size)])  15.8 us
    pallas_call x3, Pallas kernels, products(): pl.pallas_call(functools.partial(products_kernel, kind, n_opg), out_shape...  9.54 us
    ppermute x12, waiting for transfers between devices, flip(): return lax.ppermute(x, axis, [(i, i ^ bit) for i in range(size)])  7.18 us
    unnamed x12, local copies, waits for them, and re-layouts  4.69 us
    pallas_call x1, Pallas kernels, on_device(): pl.pallas_call(functools.partial(plan_kernel, local), out_shape=jax.Shape...  1.6 us
    slice x1, local copies, waits for them, and re-layouts, on_device(): ours, rest, psi = lax.optimization_barrier((ours, psi[:local - 1], psi))  1.17 us
  transfers between devices with their start and end apart: 12, of which 4 were waited for; matrix products, arithmetic and copies ran while one was open for 0% of the time, Pallas kernels for 20%

profile of v2, /device:TPU:0, one launch (start us, length us, event | category | flops | bytes accessed | tf_op | source)
XLA Modules:
  0.0 41.2 jit_solution(8729889264915534593)
XLA Ops:
  0.0 1.2 %fusion.1 = (bf16[1,384,384]{2,1,0:T(8,128)(2,1)S(1)}, bf16[1,384,384]{2,1,0:T(8,128)(2,1)S(1)}) fusion(bf16[2,384,384]{2,1,0:T(8,128)(2,1)} %refs_0_), kind=kLoop, calls=%fused_computation.9 | loop fusion | bytes 1179648 | tf_op jit(solution)/shard_map/slice | solution.py:206
  1.2 3.0 %collective-permute-start = (bf16[192,384]{1,0:T(8,128)(2,1)S(1)}, bf16[192,384]{1,0:T(8,128)(2,1)S(1)}, u32[]{:S(2)}, u32[]{:S(2)}) collective-permute-start(bf16[192,384]{1,0:T(8,128)(2,1)S(1)} %dynamic-slice_bitcast_fusion), channel_id=1, source_target_pairs={{0,2},{1,3},{2,0},{3,1},{4,6},{5,7},{6,4},{7,5},{8,10},{9,11},{10,... | collective-permute-start | bytes 442376 | tf_op jit(solution)/shard_map/ppermute | solution.py:20
  4.2 0.1 collective-permute-start.2
  4.3 0.0 collective-permute-start.3
  4.3 0.0 copy-start.4
  4.4 0.0 copy-start.5
  4.4 1.6 %shard_map.64.plan = s32[3,49]{1,0:T(4,128)S(1)} custom-call(s32[2,8]{1,0:T(2,128)S(1)} %bitcast.11), custom_call_target="tpu_custom_call" | custom-call | flops 20000000000 | tf_op jit(solution)/shard_map/pallas_call | solution.py:215
  6.0 0.2 select_reduce_fusion.coef
  6.1 2.8 %collective-permute-done = bf16[192,384]{1,0:T(8,128)(2,1)S(1)} collective-permute-done((bf16[192,384]{1,0:T(8,128)(2,1)S(1)}, bf16[192,384]{1,0:T(8,128)(2,1)S(1)}, u32[]{:S(2)}, u32[]{:S(2)}) %collective-permute-start) | collective-permute-done | bytes 147488 | tf_op jit(solution)/shard_map/ppermute | solution.py:20
  8.9 2.0 %collective-permute-start.1 = (bf16[192,384]{1,0:T(8,128)(2,1)S(1)}, bf16[192,384]{1,0:T(8,128)(2,1)S(1)}, u32[]{:S(2)}, u32[]{:S(2)}) collective-permute-start(bf16[192,384]{1,0:T(8,128)(2,1)S(1)} %collective-permute-done), channel_id=1, source_target_pairs={{0,4},{4,0},{8,12},{12,8},{16,20},{20,16},{24,28},{28,24},{1,5},{5... | collective-permute-start | bytes 442376 | tf_op jit(solution)/shard_map/ppermute | solution.py:20
  11.0 0.0 collective-permute-done.3.refs_1_
  11.0 2.3 %copy-done = bf16[8,2,384,384]{3,2,1,0:T(8,128)(2,1)S(1)} copy-done((bf16[8,2,384,384]{3,2,1,0:T(8,128)(2,1)S(1)}, bf16[8,2,384,384]{3,2,1,0:T(8,128)(2,1)}, u32[]{:S(2)}) %copy-start) | copy-done | bytes 4718616
  13.3 2.3 %copy-done.1 = bf16[8,2,384,384]{3,2,1,0:T(8,128)(2,1)S(1)} copy-done((bf16[8,2,384,384]{3,2,1,0:T(8,128)(2,1)S(1)}, bf16[8,2,384,384]{3,2,1,0:T(8,128)(2,1)}, u32[]{:S(2)}) %copy-start.1) | copy-done | bytes 4718616
  15.6 3.9 %shard_map.65.refs_0_ = f32[2,384,384]{2,1,0:T(8,128)S(1)} custom-call(s32[3,49]{1,0:T(4,128)S(1)} %shard_map.64.plan, f32[2,8]{1,0:T(2,128)S(1)} %select_reduce_fusion.coef, bf16[8,2,384,384]{3,2,1,0:T(8,128)(2,1)S(1)} %copy-done, bf16[8,2,384,384]{3,2,1,0:T(8,128)(2,1)S(1)} %copy-done.1, bf16[2,384,384]{2,1,0:T(8,128)(2,1)S(1)} %copy-done.2, ...), custom_call_target="tpu_custom_call" | custom-call | flops 384 | tf_op jit(solution)/shard_map/pallas_call | solution.py:170
  19.5 0.0 collective-permute-done.1
  19.6 0.1 pad_maximum_fusion
  19.7 0.1 collective-permute-start.4
  19.7 2.6 %shard_map.66.refs_0_ = f32[2,384,384]{2,1,0:T(8,128)S(1)} custom-call(s32[3,49]{1,0:T(4,128)S(1)} %shard_map.64.plan, f32[2,8]{1,0:T(2,128)S(1)} %select_reduce_fusion.coef, bf16[8,2,384,384]{3,2,1,0:T(8,128)(2,1)S(1)} %copy-done, bf16[8,2,384,384]{3,2,1,0:T(8,128)(2,1)S(1)} %copy-done.1, f32[2,384,384]{2,1,0:T(8,128)S(1)} %shard_map.65.refs_0_, ...), custom_call_target="tpu_custom_call" | custom-call | flops 384 | tf_op jit(solution)/shard_map/pallas_call | solution.py:170
  22.4 3.0 %shard_map.67 = (f32[2,48,384]{2,1,0:T(8,128)S(1)}, bf16[2,48,384]{2,1,0:T(8,128)(2,1)S(1)}, bf16[2,48,384]{2,1,0:T(8,128)(2,1)S(1)}, bf16[2,48,384]{2,1,0:T(8,1...) custom-call(s32[3,49]{1,0:T(4,128)S(1)} %shard_map.64.plan, ...), custom_call_target="tpu_custom_call" | custom-call | flops 384 | tf_op jit(solution)/shard_map/pallas_call | solution.py:170
  25.4 1.6 %collective-permute-start.8 = (bf16[2,48,384]{2,1,0:T(8,128)(2,1)S(1)}, bf16[2,48,384]{2,1,0:T(8,128)(2,1)S(1)}, u32[]{:S(2)}, u32[]{:S(2)}) collective-permute-start(bf16[2,48,384]{2,1,0:T(8,128)(2,1)S(1)} %get-tuple-element.42), channel_id=1, source_target_pairs={{0,12},{4,8},{8,4},{12,0},{16,28},{20,24},{24,20},{28,16},{1,13},{... | collective-permute-start | bytes 221192 | tf_op jit(solution)/shard_map/ppermute | solution.py:20
  27.0 1.7 %collective-permute-start.9 = (bf16[2,48,384]{2,1,0:T(8,128)(2,1)S(1)}, bf16[2,48,384]{2,1,0:T(8,128)(2,1)S(1)}, u32[]{:S(2)}, u32[]{:S(2)}) collective-permute-start(bf16[2,48,384]{2,1,0:T(8,128)(2,1)S(1)} %get-tuple-element.43), channel_id=1, source_target_pairs={{0,4},{4,0},{8,12},{12,8},{16,20},{20,16},{24,28},{28,24},{1,5},{5... | collective-permute-start | bytes 221192 | tf_op jit(solution)/shard_map/ppermute | solution.py:20
  28.7 0.3 collective-permute-start.10
  29.0 1.6 %collective-permute-start.5 = (bf16[2,48,384]{2,1,0:T(8,128)(2,1)S(1)}, bf16[2,48,384]{2,1,0:T(8,128)(2,1)S(1)}, u32[]{:S(2)}, u32[]{:S(2)}) collective-permute-start(bf16[2,48,384]{2,1,0:T(8,128)(2,1)S(1)} %get-tuple-element.38), channel_id=1, source_target_pairs={{0,12},{4,8},{8,4},{12,0},{16,28},{20,24},{24,20},{28,16},{1,13},{... | collective-permute-start | bytes 221192 | tf_op jit(solution)/shard_map/ppermute | solution.py:20
  30.5 1.7 %collective-permute-start.6 = (bf16[2,48,384]{2,1,0:T(8,128)(2,1)S(1)}, bf16[2,48,384]{2,1,0:T(8,128)(2,1)S(1)}, u32[]{:S(2)}, u32[]{:S(2)}) collective-permute-start(bf16[2,48,384]{2,1,0:T(8,128)(2,1)S(1)} %get-tuple-element.39), channel_id=1, source_target_pairs={{0,4},{4,0},{8,12},{12,8},{16,20},{20,16},{24,28},{28,24},{1,5},{5... | collective-permute-start | bytes 221192 | tf_op jit(solution)/shard_map/ppermute | solution.py:20
  32.2 1.1 %collective-permute-start.7 = (bf16[2,48,384]{2,1,0:T(8,128)(2,1)S(1)}, bf16[2,48,384]{2,1,0:T(8,128)(2,1)S(1)}, u32[]{:S(2)}, u32[]{:S(2)}) collective-permute-start(bf16[2,48,384]{2,1,0:T(8,128)(2,1)S(1)} %get-tuple-element.40), channel_id=1, source_target_pairs={{0,8},{4,12},{8,0},{12,4},{16,24},{20,28},{24,16},{28,20},{1,9},{5... | collective-permute-start | bytes 221192 | tf_op jit(solution)/shard_map/ppermute | solution.py:20
  33.3 0.3 collective-permute-done.10
  33.6 2.8 %collective-permute-start.11 = (bf16[2,48,384]{2,1,0:T(8,128)(2,1)S(1)}, bf16[2,48,384]{2,1,0:T(8,128)(2,1)S(1)}, u32[]{:S(2)}, u32[]{:S(2)}) collective-permute-start(bf16[2,48,384]{2,1,0:T(8,128)(2,1)S(1)} %add_convert_fusion.1), channel_id=1, source_target_pairs={{0,16},{4,20},{8,24},{12,28},{16,0},{20,4},{24,8},{28,12},{1,17},{... | collective-permute-start | bytes 221192 | tf_op jit(solution)/shard_map/ppermute | solution.py:20
  36.4 0.0 collective-permute-done.6
  36.4 0.1 collective-permute-done.7
  36.5 3.9 %collective-permute-done.11 = bf16[2,48,384]{2,1,0:T(8,128)(2,1)S(1)} collective-permute-done((bf16[2,48,384]{2,1,0:T(8,128)(2,1)S(1)}, bf16[2,48,384]{2,1,0:T(8,128)(2,1)S(1)}, u32[]{:S(2)}, u32[]{:S(2)}) %collective-permute-start.11) | collective-permute-done | bytes 73760 | tf_op jit(solution)/shard_map/ppermute | solution.py:20
  40.5 0.1 fusion
  40.5 0.7 %copy.8 = bf16[48,2,384]{2,1,0:T(2,128)(2,1)} copy(bf16[48,2,384]{2,0,1:T(8,128)(2,1)S(1)} %fusion) | data formatting | bytes 147456 | tf_op jit(solution)/shard_map/convert_element_type | solution.py:245
  (16 shorter events, 0.1 us)
Async XLA Ops:
  0.0 4.3 %copy-start.2 = (bf16[2,384,384]{2,1,0:T(8,128)(2,1)S(1)}, bf16[2,384,384]{2,1,0:T(8,128)(2,1)}, u32[]{:S(2)}) copy-start(bf16[2,384,384]{2,1,0:T(8,128)(2,1)} %refs_0_) | copy-start | bytes 1769476
  0.0 4.3 %copy-start.3 = (s32[8,2]{0,1:T(2,128)S(1)}, s32[8,2]{0,1:T(2,128)}, u32[]{:S(2)}) copy-start(s32[8,2]{0,1:T(2,128)} %param.9) | copy-start | bytes 196
  1.2 7.7 %collective-permute-start = (bf16[192,384]{1,0:T(8,128)(2,1)S(1)}, bf16[192,384]{1,0:T(8,128)(2,1)S(1)}, u32[]{:S(2)}, u32[]{:S(2)}) collective-permute-start(bf16[192,384]{1,0:T(8,128)(2,1)S(1)} %dynamic-slice_bitcast_fusion), channel_id=1, source_target_pairs={{0,2},{1,3},{2,0},{3,1},{4,6},{5,7},{6,4},{7,5},{8,10},{9,11},{10,... | collective-permute-start | bytes 442376 | tf_op jit(solution)/shard_map/ppermute | solution.py:20
  4.2 15.3 %collective-permute-start.2 = (bf16[1,384,384]{2,1,0:T(8,128)(2,1)S(1)}, bf16[1,384,384]{2,1,0:T(8,128)(2,1)S(1)}, u32[]{:S(2)}, u32[]{:S(2)}) collective-permute-start(bf16[1,384,384]{2,1,0:T(8,128)(2,1)S(1)} %get-tuple-element.31), channel_id=1, source_target_pairs={{0,2},{1,3},{2,0},{3,1},{4,6},{5,7},{6,4},{7,5},{8,10},{9,11},{10,... | collective-permute-start | bytes 884744 | tf_op jit(solution)/shard_map/ppermute | solution.py:20
  4.3 6.6 %collective-permute-start.3 = (bf16[2,384,384]{2,1,0:T(8,128)(2,1)S(1)}, bf16[2,384,384]{2,1,0:T(8,128)(2,1)S(1)}, u32[]{:S(2)}, u32[]{:S(2)}) collective-permute-start(bf16[2,384,384]{2,1,0:T(8,128)(2,1)S(1)} %copy-done.2), channel_id=1, source_target_pairs={{0,1},{1,0},{2,3},{3,2},{4,5},{5,4},{6,7},{7,6},{8,9},{9,8},{10,11... | collective-permute-start | bytes 1769480 | tf_op jit(solution)/shard_map/ppermute | solution.py:20
  4.3 1.6 %copy-start.4 = (s32[8,2]{0,1:T(2,128)S(1)}, s32[8,2]{0,1:T(2,128)}, u32[]{:S(2)}) copy-start(s32[8,2]{0,1:T(2,128)} %param.10) | copy-start | bytes 196
  4.4 1.6 %copy-start.5 = (f32[64]{0:T(128)S(1)}, f32[64]{0:T(128)}, u32[]{:S(2)}) copy-start(f32[64]{0:T(128)} %param.11) | copy-start | bytes 772
  8.9 10.6 %collective-permute-start.1 = (bf16[192,384]{1,0:T(8,128)(2,1)S(1)}, bf16[192,384]{1,0:T(8,128)(2,1)S(1)}, u32[]{:S(2)}, u32[]{:S(2)}) collective-permute-start(bf16[192,384]{1,0:T(8,128)(2,1)S(1)} %collective-permute-done), channel_id=1, source_target_pairs={{0,4},{4,0},{8,12},{12,8},{16,20},{20,16},{24,28},{28,24},{1,5},{5... | collective-permute-start | bytes 442376 | tf_op jit(solution)/shard_map/ppermute | solution.py:20
  11.0 2.3 %copy-start = (bf16[8,2,384,384]{3,2,1,0:T(8,128)(2,1)S(1)}, bf16[8,2,384,384]{3,2,1,0:T(8,128)(2,1)}, u32[]{:S(2)}) copy-start(bf16[8,2,384,384]{3,2,1,0:T(8,128)(2,1)} %left.5) | copy-start | bytes 14155780
  13.3 2.3 %copy-start.1 = (bf16[8,2,384,384]{3,2,1,0:T(8,128)(2,1)S(1)}, bf16[8,2,384,384]{3,2,1,0:T(8,128)(2,1)}, u32[]{:S(2)}) copy-start(bf16[8,2,384,384]{3,2,1,0:T(8,128)(2,1)} %right.5) | copy-start | bytes 14155780
  19.7 2.7 %collective-permute-start.4 = (bf16[2,384,384]{2,1,0:T(8,128)(2,1)S(1)}, bf16[2,384,384]{2,1,0:T(8,128)(2,1)S(1)}, u32[]{:S(2)}, u32[]{:S(2)}) collective-permute-start(bf16[2,384,384]{2,1,0:T(8,128)(2,1)S(1)} %bitcast.9), channel_id=1, source_target_pairs={{0,1},{1,0},{2,3},{3,2},{4,5},{5,4},{6,7},{7,6},{8,9},{9,8},{10,11... | collective-permute-start | bytes 1769480 | tf_op jit(solution)/shard_map/ppermute | solution.py:20
  25.4 6.8 %collective-permute-start.8 = (bf16[2,48,384]{2,1,0:T(8,128)(2,1)S(1)}, bf16[2,48,384]{2,1,0:T(8,128)(2,1)S(1)}, u32[]{:S(2)}, u32[]{:S(2)}) collective-permute-start(bf16[2,48,384]{2,1,0:T(8,128)(2,1)S(1)} %get-tuple-element.42), channel_id=1, source_target_pairs={{0,12},{4,8},{8,4},{12,0},{16,28},{20,24},{24,20},{28,16},{1,13},{... | collective-permute-start | bytes 221192 | tf_op jit(solution)/shard_map/ppermute | solution.py:20
  27.0 6.2 %collective-permute-start.9 = (bf16[2,48,384]{2,1,0:T(8,128)(2,1)S(1)}, bf16[2,48,384]{2,1,0:T(8,128)(2,1)S(1)}, u32[]{:S(2)}, u32[]{:S(2)}) collective-permute-start(bf16[2,48,384]{2,1,0:T(8,128)(2,1)S(1)} %get-tuple-element.43), channel_id=1, source_target_pairs={{0,4},{4,0},{8,12},{12,8},{16,20},{20,16},{24,28},{28,24},{1,5},{5... | collective-permute-start | bytes 221192 | tf_op jit(solution)/shard_map/ppermute | solution.py:20
  28.7 4.9 %collective-permute-start.10 = (bf16[2,48,384]{2,1,0:T(8,128)(2,1)S(1)}, bf16[2,48,384]{2,1,0:T(8,128)(2,1)S(1)}, u32[]{:S(2)}, u32[]{:S(2)}) collective-permute-start(bf16[2,48,384]{2,1,0:T(8,128)(2,1)S(1)} %get-tuple-element.44), channel_id=1, source_target_pairs={{0,8},{4,12},{8,0},{12,4},{16,24},{20,28},{24,16},{28,20},{1,9},{5... | collective-permute-start | bytes 221192 | tf_op jit(solution)/shard_map/ppermute | solution.py:20
  29.0 7.4 %collective-permute-start.5 = (bf16[2,48,384]{2,1,0:T(8,128)(2,1)S(1)}, bf16[2,48,384]{2,1,0:T(8,128)(2,1)S(1)}, u32[]{:S(2)}, u32[]{:S(2)}) collective-permute-start(bf16[2,48,384]{2,1,0:T(8,128)(2,1)S(1)} %get-tuple-element.38), channel_id=1, source_target_pairs={{0,12},{4,8},{8,4},{12,0},{16,28},{20,24},{24,20},{28,16},{1,13},{... | collective-permute-start | bytes 221192 | tf_op jit(solution)/shard_map/ppermute | solution.py:20
  30.5 5.9 %collective-permute-start.6 = (bf16[2,48,384]{2,1,0:T(8,128)(2,1)S(1)}, bf16[2,48,384]{2,1,0:T(8,128)(2,1)S(1)}, u32[]{:S(2)}, u32[]{:S(2)}) collective-permute-start(bf16[2,48,384]{2,1,0:T(8,128)(2,1)S(1)} %get-tuple-element.39), channel_id=1, source_target_pairs={{0,4},{4,0},{8,12},{12,8},{16,20},{20,16},{24,28},{28,24},{1,5},{5... | collective-permute-start | bytes 221192 | tf_op jit(solution)/shard_map/ppermute | solution.py:20
  32.2 4.4 %collective-permute-start.7 = (bf16[2,48,384]{2,1,0:T(8,128)(2,1)S(1)}, bf16[2,48,384]{2,1,0:T(8,128)(2,1)S(1)}, u32[]{:S(2)}, u32[]{:S(2)}) collective-permute-start(bf16[2,48,384]{2,1,0:T(8,128)(2,1)S(1)} %get-tuple-element.40), channel_id=1, source_target_pairs={{0,8},{4,12},{8,0},{12,4},{16,24},{20,28},{24,16},{28,20},{1,9},{5... | collective-permute-start | bytes 221192 | tf_op jit(solution)/shard_map/ppermute | solution.py:20
  33.6 6.9 %collective-permute-start.11 = (bf16[2,48,384]{2,1,0:T(8,128)(2,1)S(1)}, bf16[2,48,384]{2,1,0:T(8,128)(2,1)S(1)}, u32[]{:S(2)}, u32[]{:S(2)}) collective-permute-start(bf16[2,48,384]{2,1,0:T(8,128)(2,1)S(1)} %add_convert_fusion.1), channel_id=1, source_target_pairs={{0,16},{4,20},{8,24},{12,28},{16,0},{20,4},{24,8},{28,12},{1,17},{... | collective-permute-start | bytes 221192 | tf_op jit(solution)/shard_map/ppermute | solution.py:20

commit v3 on v2

--- a/solution.py
+++ b/solution.py
@@ -14,6 +14,8 @@
 NEAR = 2
 KERNEL_VMEM = 24_000_000
 PLAN_FLOPS = 20_000_000_000
+PLAN_VMEM = 49_000_000
+NEAR_VMEM = 44_000_000
 
 
 def flip(x, axis, size, bit):
@@ -87,7 +89,7 @@
     return list(zip(cut, (p[:, low] + q[:, high], p[:, high] + r[:, high], q[:, low] + r[:, low])))
 
 
-def run(kind, plan, coef, left, right, psi, acc, even, odd):
+def run(kind, plan, coef, left, right, psi, acc, even, odd, ready):
     pairs, local = left.shape[:2]
     slots = local * pairs
     count = plan[kind, 3 * slots]
@@ -105,6 +107,8 @@
 
     def two(j, carry):
         i = 2 * j
+        ready(i)
+        ready(i + 1)
         first(i + 1, odd)
         second(i, even)
         first(i + 2, even)
@@ -118,31 +122,65 @@
 
         @pl.when(lax.rem(count, 2) == 1)
         def _():
+            ready(count - 1)
             second(count - 1, even)
 
 
-def plan_kernel(local, source, plan):
-    make_plan(source, plan, source.shape[1], local)
-
-
-def products_kernel(kind, n_opg, plan, coef, left, right, *refs):
+def plan_kernel(source, left, plan, left_here, sem):
+    pairs, local = left.shape[:2]
+    copies = [
+        pltpu.make_async_copy(left.at[p], left_here.at[p], sem.at[p]) for p in range(pairs)
+    ]
+    for copy in copies:
+        copy.start()
+    make_plan(source, plan, pairs, local)
+    for copy in copies:
+        copy.wait()
+
+
+def near_kernel(plan, coef, left, right, own, partner, acc, right_here, psi, even, odd, sem):
+    pairs, local = right.shape[:2]
+    slots = pairs * local
+
+    def copy(kind, i):
+        p, s = plan[kind, i], plan[kind, slots + i]
+        return pltpu.make_async_copy(
+            right.at[p, s], right_here.at[p, s], sem.at[p * local + s]
+        )
+
+    def each(kind, act):
+        def one(i, carry):
+            act(kind, i)
+            return carry
+
+        lax.fori_loop(0, plan[kind, 3 * slots], one, 0)
+
+    for kind in range(CLASSES):
+        each(kind, lambda kind, i: copy(kind, i).start())
+    acc[...] = jnp.zeros_like(acc)
+    psi[:local] = own[...]
+    psi[local:] = partner[...]
+    run(
+        0, plan, coef, left, right_here, psi, acc, even, odd, lambda i: copy(0, i).wait()
+    )
+    for kind in range(1, CLASSES):
+        each(kind, lambda kind, i: copy(kind, i).wait())
+
+
+def products_kernel(kind, n_opg, plan, coef, left, right, total, *refs):
     local, sb = left.shape[1:3]
     last = kind == CLASSES - 1
     outs = n_opg if last else 1
     pieces, refs = refs[: -outs - 3 - last], refs[-outs - 3 - last :]
     psi, even, odd = refs[outs : outs + 3]
     acc = refs[-1] if last else refs[0]
-    if kind:
-        acc[...] = pieces[0][...]
-        pieces = pieces[1:]
-    else:
-        acc[...] = jnp.zeros_like(acc)
+    acc[...] = total[...]
     if len(pieces) == 1:
         psi = pieces[0]
     else:
         for i, piece in enumerate(pieces):
             psi[i * local : (i + 1) * local] = piece[...]
-    run(kind, plan, coef, left, right, psi, acc, even, odd)
+    run(kind, plan, coef, left, right, psi, acc, even, odd, lambda i: None)
     if last:
         me_opg = lax.axis_index(OPG)
         rows = sb // n_opg
@@ -153,11 +191,52 @@
 
 SMEM = pl.BlockSpec(memory_space=pltpu.SMEM)
 VMEM = pl.BlockSpec(memory_space=pltpu.VMEM)
-
-
-def products(kind, n_opg, plan, coef, left, right, totals, pieces):
+HBM = pl.BlockSpec(memory_space=pltpu.HBM)
+
+
+def halves(sb):
+    return [pltpu.VMEM((sb, sb), jnp.bfloat16), pltpu.VMEM((sb, sb), jnp.bfloat16)]
+
+
+def lists(source, left):
+    pairs, local = left.shape[:2]
+    return pl.pallas_call(
+        plan_kernel,
+        out_shape=(
+            jax.ShapeDtypeStruct((CLASSES, 3 * local * pairs + 1), jnp.int32),
+            jax.ShapeDtypeStruct(left.shape, left.dtype),
+        ),
+        in_specs=[SMEM, HBM],
+        out_specs=(SMEM, VMEM),
+        scratch_shapes=[pltpu.SemaphoreType.DMA((pairs,))],
+        compiler_params=pltpu.CompilerParams(vmem_limit_bytes=PLAN_VMEM),
+        cost_estimate=pl.CostEstimate(flops=PLAN_FLOPS, bytes_accessed=0, transcendentals=0),
+    )(source, left)
+
+
+def near_products(plan, coef, left, right, own, partner):
+    pairs, local, sb, _ = right.shape
+    return pl.pallas_call(
+        near_kernel,
+        out_shape=(
+            jax.ShapeDtypeStruct((local, sb, sb), jnp.float32),
+            jax.ShapeDtypeStruct(right.shape, right.dtype),
+        ),
+        in_specs=[SMEM, SMEM, VMEM, HBM, VMEM, VMEM],
+        out_specs=(VMEM, VMEM),
+        scratch_shapes=[
+            pltpu.VMEM((NEAR * local, sb, sb), jnp.bfloat16),
+            *halves(sb),
+            pltpu.SemaphoreType.DMA((pairs * local,)),
+        ],
+        compiler_params=pltpu.CompilerParams(vmem_limit_bytes=NEAR_VMEM),
+        cost_estimate=pl.CostEstimate(flops=sb, bytes_accessed=0, transcendentals=0),
+    )(plan, coef, left, right, own, partner)
+
+
+def products(kind, n_opg, plan, coef, left, right, total, pieces):
     pairs, local, sb, _ = left.shape
-    out_shape = jax.ShapeDtypeStruct((local, sb, sb), jnp.float32)
+    out_shape = jax.ShapeDtypeStruct(total.shape, total.dtype)
     scratch = []
     if kind == CLASSES - 1:
         scratch = [pltpu.VMEM(out_shape.shape, out_shape.dtype)]
@@ -170,17 +249,16 @@
     return pl.pallas_call(
         functools.partial(products_kernel, kind, n_opg),
         out_shape=out_shape,
-        in_specs=[SMEM] * 2 + [VMEM] * (2 + len(totals) + len(pieces)),
+        in_specs=[SMEM] * 2 + [VMEM] * (3 + len(pieces)),
         out_specs=jax.tree.map(lambda _: VMEM, out_shape),
         scratch_shapes=[
             pltpu.VMEM((len(pieces) * local, sb, sb), jnp.bfloat16),
-            pltpu.VMEM((sb, sb), jnp.bfloat16),
-            pltpu.VMEM((sb, sb), jnp.bfloat16),
+            *halves(sb),
             *scratch,
         ],
         compiler_params=pltpu.CompilerParams(vmem_limit_bytes=KERNEL_VMEM),
         cost_estimate=pl.CostEstimate(flops=sb, bytes_accessed=0, transcendentals=0),
-    )(plan, coef, left, right, *totals, *pieces)
+    )(plan, coef, left, right, total, *pieces)
 
 
 def scatter_sum(sends, n_opg):
@@ -198,7 +276,6 @@
 
 def on_device(n_opg, n_sec, psi, left_ops, right_ops, source, coef_index, sixj):
     local, sb, _ = psi.shape
-    pairs = left_ops.shape[0]
 
     half = lax.rem(lax.axis_index(OPG), HALVES)
     cut = psi[local - 1].reshape(HALVES, sb // HALVES, sb)
@@ -212,27 +289,17 @@
     here, whole = [here[r] for r in far], [whole[r] for r in far]
     partner = flip(psi, SEC, n_sec, 1)
 
-    plan = pl.pallas_call(
-        functools.partial(plan_kernel, local),
-        out_shape=jax.ShapeDtypeStruct((CLASSES, 3 * local * pairs + 1), jnp.int32),
-        in_specs=[SMEM],
-        out_specs=SMEM,
-        compiler_params=pltpu.CompilerParams(vmem_limit_bytes=KERNEL_VMEM),
-        cost_estimate=pl.CostEstimate(flops=PLAN_FLOPS, bytes_accessed=0, transcendentals=0),
-    )(source.T)
-    plan, coef_index = lax.optimization_barrier((plan, coef_index))
+    plan, left = lists(source.T, left_ops)
+    plan, left, coef_index = lax.optimization_barrier((plan, left, coef_index))
     table = jnp.arange(sixj.shape[0], dtype=jnp.int32)
     coef = jnp.sum(jnp.where(coef_index.T[:, :, None] == table, sixj, 0.0), axis=2)
 
-    def onto(kind, totals, pieces):
-        return products(kind, n_opg, plan, coef, left_ops, right_ops, totals, pieces)
-
     def to_other_core(pieces):
         return [flip(x, SEC, n_sec, 1) for x in pieces]
 
     here, plan, coef = lax.optimization_barrier((here, plan, coef))
     there = [flip(x, OPG, n_opg, 1) for x in here]
-    done = onto(0, [], [psi, partner])
+    done, right = near_products(plan, coef, left, right_ops, psi, partner)
     here, there, whole, done = lax.optimization_barrier((here, there, whole, done))
     twins = []
     for one, other, rest in zip(here, there, whole):
@@ -240,8 +307,8 @@
         rows = jnp.concatenate([rest.reshape(-1, sb), upper, lower])
         twins.append(rows.reshape(local, sb, sb))
     others = to_other_core(twins)
-    done = onto(1, [done], twins)
-    sends = onto(2, [done], others)
+    done = products(1, n_opg, plan, coef, left, right, done, twins)
+    sends = products(2, n_opg, plan, coef, left, right, done, others)
     return jnp.swapaxes(scatter_sum(sends, n_opg), 0, 1).astype(jnp.bfloat16)
 
 

time: 41.6 us -> 41.1 us (0.988)
  waiting for transfers between devices: 7.18 us -> 4.21 us
  Pallas kernels: 11.1 us -> 13.9 us
    pallas_call x1 -> x2, Pallas kernels: 1.6 us -> 8.26 us  [the longest x1 4.71 us: near_products(): pl.pallas_call(near_kernel, out_shape=(jax.ShapeDtypeStruct((local, sb, s...]
    pallas_call x3 -> x2, Pallas kernels: 9.54 us -> 5.6 us  [products(): pl.pallas_call(functools.partial(products_kernel, kind, n_opg), out_shape...]
    ppermute x12, waiting for transfers between devices: 7.18 us -> 4.21 us  [flip(): return lax.ppermute(x, axis, [(i, i ^ bit) for i in range(size)])]
  transfers between devices with their start and end apart: 12 -> 12, of which waited for: 4 -> 2; matrix products, arithmetic and copies ran while one was open for 0% -> 0% of each run, Pallas kernels for 20% -> 29%
where the time goes in v3:
time: 41.1 us
  starting transfers between devices  16.2 us (39%)
  Pallas kernels  13.9 us (34%)
  local copies, waits for them, and re-layouts  6.35 us (15%)
  waiting for transfers between devices  4.21 us (10%)
    ppermute x12, starting transfers between devices, flip(): return lax.ppermute(x, axis, [(i, i ^ bit) for i in range(size)])  16.2 us
    pallas_call x2, Pallas kernels, products(): pl.pallas_call(functools.partial(products_kernel, kind, n_opg), out_shape...  5.6 us
    pallas_call x1, Pallas kernels, near_products(): pl.pallas_call(near_kernel, out_shape=(jax.ShapeDtypeStruct((local, sb, s...  4.71 us
    unnamed x12, local copies, waits for them, and re-layouts  4.47 us
    ppermute x12, waiting for transfers between devices, flip(): return lax.ppermute(x, axis, [(i, i ^ bit) for i in range(size)])  4.21 us
    pallas_call x1, Pallas kernels, lists(): pl.pallas_call(plan_kernel, out_shape=(jax.ShapeDtypeStruct((CLASSES, 3 *...  3.55 us
    slice x1, local copies, waits for them, and re-layouts, on_device(): ours, rest, psi = lax.optimization_barrier((ours, psi[:local - 1], psi))  1.17 us
  transfers between devices with their start and end apart: 12, of which 2 were waited for; matrix products, arithmetic and copies ran while one was open for 0% of the time, Pallas kernels for 29%

profile of v3, /device:TPU:0, one launch (start us, length us, event | category | flops | bytes accessed | tf_op | source)
XLA Modules:
  0.0 41.1 jit_solution(13038972346434033474)
XLA Ops:
  0.0 1.2 %fusion.1 = (bf16[1,384,384]{2,1,0:T(8,128)(2,1)S(1)}, bf16[1,384,384]{2,1,0:T(8,128)(2,1)S(1)}) fusion(bf16[2,384,384]{2,1,0:T(8,128)(2,1)} %own), kind=kLoop, calls=%fused_computation.9 | loop fusion | bytes 1179648 | tf_op jit(solution)/shard_map/slice | solution.py:283
  1.2 3.0 %collective-permute-start = (bf16[192,384]{1,0:T(8,128)(2,1)S(1)}, bf16[192,384]{1,0:T(8,128)(2,1)S(1)}, u32[]{:S(2)}, u32[]{:S(2)}) collective-permute-start(bf16[192,384]{1,0:T(8,128)(2,1)S(1)} %dynamic-slice_bitcast_fusion), channel_id=1, source_target_pairs={{0,2},{1,3},{2,0},{3,1},{4,6},{5,7},{6,4},{7,5},{8,10},{9,11},{10,... | collective-permute-start | bytes 442376 | tf_op jit(solution)/shard_map/ppermute | solution.py:22
  4.2 0.1 collective-permute-start.3
  4.3 0.0 copy-start.4
  4.4 0.0 copy-start.5
  4.4 3.5 %shard_map.64 = (s32[3,49]{1,0:T(4,128)S(1)}, bf16[8,2,384,384]{3,2,1,0:T(8,128)(2,1)S(1)}) custom-call(s32[2,8]{1,0:T(2,128)S(1)} %bitcast.11, bf16[8,2,384,384]{3,2,1,0:T(8,128)(2,1)} %left.1), custom_call_target="tpu_custom_call" | custom-call | flops 20000000000 | tf_op jit(solution)/shard_map/pallas_call | solution.py:203
  7.9 2.1 %copy-done = bf16[8,2,384,384]{3,2,1,0:T(8,128)(2,1)} copy-done((bf16[8,2,384,384]{3,2,1,0:T(8,128)(2,1)}, bf16[8,2,384,384]{3,2,1,0:T(8,128)(2,1)S(1)}, u32[]{:S(2)}) %copy-start) | copy-done | bytes 4718616
  10.0 0.2 select_reduce_fusion.coef
  10.2 0.0 collective-permute-done
  10.2 1.9 %collective-permute-start.2 = (bf16[192,384]{1,0:T(8,128)(2,1)S(1)}, bf16[192,384]{1,0:T(8,128)(2,1)S(1)}, u32[]{:S(2)}, u32[]{:S(2)}) collective-permute-start(bf16[192,384]{1,0:T(8,128)(2,1)S(1)} %collective-permute-done), channel_id=1, source_target_pairs={{0,4},{4,0},{8,12},{12,8},{16,20},{20,16},{24,28},{28,24},{1,5},{5... | collective-permute-start | bytes 442376 | tf_op jit(solution)/shard_map/ppermute | solution.py:22
  12.1 0.0 collective-permute-done.1.partner
  12.1 2.3 %copy-done.1 = bf16[8,2,384,384]{3,2,1,0:T(8,128)(2,1)S(1)} copy-done((bf16[8,2,384,384]{3,2,1,0:T(8,128)(2,1)S(1)}, bf16[8,2,384,384]{3,2,1,0:T(8,128)(2,1)}, u32[]{:S(2)}) %copy-start.1) | copy-done | bytes 4718616
  14.5 4.7 %shard_map.65 = (f32[2,384,384]{2,1,0:T(8,128)S(1)}, bf16[8,2,384,384]{3,2,1,0:T(8,128)(2,1)S(1)}) custom-call(s32[3,49]{1,0:T(4,128)S(1)} %get-tuple-element.35.plan, f32[2,8]{1,0:T(2,128)S(1)} %select_reduce_fusion.coef, bf16[8,2,384,384]{3,2,1,0:T(8,128)(2,1)S(1)} %copy-done.1, bf16[8,2,384,384]{3,2,1,0:T(8,128)(2,1)} %right.1, ...), custom_call_target="tpu_custom_call" | custom-call | flops 384 | tf_op jit(solution)/shard_map/pallas_call | solution.py:219
  19.2 0.0 collective-permute-done.2
  19.2 0.1 pad_maximum_fusion
  19.3 1.9 %collective-permute-start.4 = (bf16[2,384,384]{2,1,0:T(8,128)(2,1)S(1)}, bf16[2,384,384]{2,1,0:T(8,128)(2,1)S(1)}, u32[]{:S(2)}, u32[]{:S(2)}) collective-permute-start(bf16[2,384,384]{2,1,0:T(8,128)(2,1)S(1)} %bitcast.9), channel_id=1, source_target_pairs={{0,1},{1,0},{2,3},{3,2},{4,5},{5,4},{6,7},{7,6},{8,9},{9,8},{10,11... | collective-permute-start | bytes 1769480 | tf_op jit(solution)/shard_map/ppermute | solution.py:22
  21.2 3.7 %shard_map.66.total = f32[2,384,384]{2,1,0:T(8,128)S(1)} custom-call(s32[3,49]{1,0:T(4,128)S(1)} %get-tuple-element.35.plan, f32[2,8]{1,0:T(2,128)S(1)} %select_reduce_fusion.coef, bf16[8,2,384,384]{3,2,1,0:T(8,128)(2,1)S(1)} %copy-done.1, bf16[8,2,384,384]{3,2,1,0:T(8,128)(2,1)S(1)} %get-tuple-element.39.right, f32[2,384,384]{2,1,0:T(8,128)S(1)} %get-tuple-element.43.total, ...), custom_call_target="tpu_custom_call" | custom-call | flops 384 | tf_op jit(solution)/shard_map/pallas_call | solution.py:249
  24.9 0.0 collective-permute-done.4.refs_0_
  24.9 1.9 %shard_map.67 = (f32[2,48,384]{2,1,0:T(8,128)S(1)}, bf16[2,48,384]{2,1,0:T(8,128)(2,1)S(1)}, bf16[2,48,384]{2,1,0:T(8,128)(2,1)S(1)}, bf16[2,48,384]{2,1,0:T(8,1...) custom-call(s32[3,49]{1,0:T(4,128)S(1)} %get-tuple-element.35.plan, ...), custom_call_target="tpu_custom_call" | custom-call | flops 384 | tf_op jit(solution)/shard_map/pallas_call | solution.py:249
  26.8 0.1 collective-permute-start.8
  26.9 1.4 %collective-permute-start.9 = (bf16[2,48,384]{2,1,0:T(8,128)(2,1)S(1)}, bf16[2,48,384]{2,1,0:T(8,128)(2,1)S(1)}, u32[]{:S(2)}, u32[]{:S(2)}) collective-permute-start(bf16[2,48,384]{2,1,0:T(8,128)(2,1)S(1)} %get-tuple-element.53), channel_id=1, source_target_pairs={{0,4},{4,0},{8,12},{12,8},{16,20},{20,16},{24,28},{28,24},{1,5},{5... | collective-permute-start | bytes 221192 | tf_op jit(solution)/shard_map/ppermute | solution.py:22
  28.3 2.1 %collective-permute-start.10 = (bf16[2,48,384]{2,1,0:T(8,128)(2,1)S(1)}, bf16[2,48,384]{2,1,0:T(8,128)(2,1)S(1)}, u32[]{:S(2)}, u32[]{:S(2)}) collective-permute-start(bf16[2,48,384]{2,1,0:T(8,128)(2,1)S(1)} %get-tuple-element.54), channel_id=1, source_target_pairs={{0,8},{4,12},{8,0},{12,4},{16,24},{20,28},{24,16},{28,20},{1,9},{5... | collective-permute-start | bytes 221192 | tf_op jit(solution)/shard_map/ppermute | solution.py:22
  30.4 0.1 collective-permute-start.5
  30.4 1.4 %collective-permute-start.6 = (bf16[2,48,384]{2,1,0:T(8,128)(2,1)S(1)}, bf16[2,48,384]{2,1,0:T(8,128)(2,1)S(1)}, u32[]{:S(2)}, u32[]{:S(2)}) collective-permute-start(bf16[2,48,384]{2,1,0:T(8,128)(2,1)S(1)} %get-tuple-element.49), channel_id=1, source_target_pairs={{0,4},{4,0},{8,12},{12,8},{16,20},{20,16},{24,28},{28,24},{1,5},{5... | collective-permute-start | bytes 221192 | tf_op jit(solution)/shard_map/ppermute | solution.py:22
  31.8 0.8 %collective-permute-done.8 = bf16[2,48,384]{2,1,0:T(8,128)(2,1)S(1)} collective-permute-done((bf16[2,48,384]{2,1,0:T(8,128)(2,1)S(1)}, bf16[2,48,384]{2,1,0:T(8,128)(2,1)S(1)}, u32[]{:S(2)}, u32[]{:S(2)}) %collective-permute-start.8) | collective-permute-done | bytes 73760 | tf_op jit(solution)/shard_map/ppermute | solution.py:22
  32.6 1.2 %collective-permute-start.7 = (bf16[2,48,384]{2,1,0:T(8,128)(2,1)S(1)}, bf16[2,48,384]{2,1,0:T(8,128)(2,1)S(1)}, u32[]{:S(2)}, u32[]{:S(2)}) collective-permute-start(bf16[2,48,384]{2,1,0:T(8,128)(2,1)S(1)} %get-tuple-element.50), channel_id=1, source_target_pairs={{0,8},{4,12},{8,0},{12,4},{16,24},{20,28},{24,16},{28,20},{1,9},{5... | collective-permute-start | bytes 221192 | tf_op jit(solution)/shard_map/ppermute | solution.py:22
  33.9 3.1 %collective-permute-start.11 = (bf16[2,48,384]{2,1,0:T(8,128)(2,1)S(1)}, bf16[2,48,384]{2,1,0:T(8,128)(2,1)S(1)}, u32[]{:S(2)}, u32[]{:S(2)}) collective-permute-start(bf16[2,48,384]{2,1,0:T(8,128)(2,1)S(1)} %add_convert_fusion.1), channel_id=1, source_target_pairs={{0,16},{4,20},{8,24},{12,28},{16,0},{20,4},{24,8},{28,12},{1,17},{... | collective-permute-start | bytes 221192 | tf_op jit(solution)/shard_map/ppermute | solution.py:22
  37.0 0.0 collective-permute-done.5
  37.0 0.0 collective-permute-done.7
  37.0 3.4 %collective-permute-done.11 = bf16[2,48,384]{2,1,0:T(8,128)(2,1)S(1)} collective-permute-done((bf16[2,48,384]{2,1,0:T(8,128)(2,1)S(1)}, bf16[2,48,384]{2,1,0:T(8,128)(2,1)S(1)}, u32[]{:S(2)}, u32[]{:S(2)}) %collective-permute-start.11) | collective-permute-done | bytes 73760 | tf_op jit(solution)/shard_map/ppermute | solution.py:22
  40.3 0.1 fusion
  40.4 0.7 %copy.8 = bf16[48,2,384]{2,1,0:T(2,128)(2,1)} copy(bf16[48,2,384]{2,0,1:T(8,128)(2,1)S(1)} %fusion) | data formatting | bytes 147456 | tf_op jit(solution)/shard_map/convert_element_type | solution.py:312
  (16 shorter events, 0.1 us)
Async XLA Ops:
  0.0 4.3 %copy-start.2 = (bf16[2,384,384]{2,1,0:T(8,128)(2,1)S(1)}, bf16[2,384,384]{2,1,0:T(8,128)(2,1)}, u32[]{:S(2)}) copy-start(bf16[2,384,384]{2,1,0:T(8,128)(2,1)} %own) | copy-start | bytes 1769476
  0.0 4.3 %copy-start.3 = (s32[8,2]{0,1:T(2,128)S(1)}, s32[8,2]{0,1:T(2,128)}, u32[]{:S(2)}) copy-start(s32[8,2]{0,1:T(2,128)} %param.9) | copy-start | bytes 196
  1.2 9.0 %collective-permute-start = (bf16[192,384]{1,0:T(8,128)(2,1)S(1)}, bf16[192,384]{1,0:T(8,128)(2,1)S(1)}, u32[]{:S(2)}, u32[]{:S(2)}) collective-permute-start(bf16[192,384]{1,0:T(8,128)(2,1)S(1)} %dynamic-slice_bitcast_fusion), channel_id=1, source_target_pairs={{0,2},{1,3},{2,0},{3,1},{4,6},{5,7},{6,4},{7,5},{8,10},{9,11},{10,... | collective-permute-start | bytes 442376 | tf_op jit(solution)/shard_map/ppermute | solution.py:22
  4.2 14.9 %collective-permute-start.3 = (bf16[1,384,384]{2,1,0:T(8,128)(2,1)S(1)}, bf16[1,384,384]{2,1,0:T(8,128)(2,1)S(1)}, u32[]{:S(2)}, u32[]{:S(2)}) collective-permute-start(bf16[1,384,384]{2,1,0:T(8,128)(2,1)S(1)} %get-tuple-element.41), channel_id=1, source_target_pairs={{0,2},{1,3},{2,0},{3,1},{4,6},{5,7},{6,4},{7,5},{8,10},{9,11},{10,... | collective-permute-start | bytes 884744 | tf_op jit(solution)/shard_map/ppermute | solution.py:22
  4.3 7.8 %collective-permute-start.1 = (bf16[2,384,384]{2,1,0:T(8,128)(2,1)S(1)}, bf16[2,384,384]{2,1,0:T(8,128)(2,1)S(1)}, u32[]{:S(2)}, u32[]{:S(2)}) collective-permute-start(bf16[2,384,384]{2,1,0:T(8,128)(2,1)S(1)} %copy-done.2), channel_id=1, source_target_pairs={{0,1},{1,0},{2,3},{3,2},{4,5},{5,4},{6,7},{7,6},{8,9},{9,8},{10,11... | collective-permute-start | bytes 1769480 | tf_op jit(solution)/shard_map/ppermute | solution.py:22
  4.3 5.7 %copy-start.4 = (s32[8,2]{0,1:T(2,128)S(1)}, s32[8,2]{0,1:T(2,128)}, u32[]{:S(2)}) copy-start(s32[8,2]{0,1:T(2,128)} %param.10) | copy-start | bytes 196
  4.4 5.7 %copy-start.5 = (f32[64]{0:T(128)S(1)}, f32[64]{0:T(128)}, u32[]{:S(2)}) copy-start(f32[64]{0:T(128)} %param.11) | copy-start | bytes 772
  7.9 2.1 %copy-start = (bf16[8,2,384,384]{3,2,1,0:T(8,128)(2,1)}, bf16[8,2,384,384]{3,2,1,0:T(8,128)(2,1)S(1)}, u32[]{:S(2)}) copy-start(bf16[8,2,384,384]{3,2,1,0:T(8,128)(2,1)S(1)} %get-tuple-element.37.left) | copy-start | bytes 14155780
  10.2 9.0 %collective-permute-start.2 = (bf16[192,384]{1,0:T(8,128)(2,1)S(1)}, bf16[192,384]{1,0:T(8,128)(2,1)S(1)}, u32[]{:S(2)}, u32[]{:S(2)}) collective-permute-start(bf16[192,384]{1,0:T(8,128)(2,1)S(1)} %collective-permute-done), channel_id=1, source_target_pairs={{0,4},{4,0},{8,12},{12,8},{16,20},{20,16},{24,28},{28,24},{1,5},{5... | collective-permute-start | bytes 442376 | tf_op jit(solution)/shard_map/ppermute | solution.py:22
  12.1 2.3 %copy-start.1 = (bf16[8,2,384,384]{3,2,1,0:T(8,128)(2,1)S(1)}, bf16[8,2,384,384]{3,2,1,0:T(8,128)(2,1)}, u32[]{:S(2)}) copy-start(bf16[8,2,384,384]{3,2,1,0:T(8,128)(2,1)} %copy-done) | copy-start | bytes 14155780
  19.3 5.6 %collective-permute-start.4 = (bf16[2,384,384]{2,1,0:T(8,128)(2,1)S(1)}, bf16[2,384,384]{2,1,0:T(8,128)(2,1)S(1)}, u32[]{:S(2)}, u32[]{:S(2)}) collective-permute-start(bf16[2,384,384]{2,1,0:T(8,128)(2,1)S(1)} %bitcast.9), channel_id=1, source_target_pairs={{0,1},{1,0},{2,3},{3,2},{4,5},{5,4},{6,7},{7,6},{8,9},{9,8},{10,11... | collective-permute-start | bytes 1769480 | tf_op jit(solution)/shard_map/ppermute | solution.py:22
  26.8 5.8 %collective-permute-start.8 = (bf16[2,48,384]{2,1,0:T(8,128)(2,1)S(1)}, bf16[2,48,384]{2,1,0:T(8,128)(2,1)S(1)}, u32[]{:S(2)}, u32[]{:S(2)}) collective-permute-start(bf16[2,48,384]{2,1,0:T(8,128)(2,1)S(1)} %get-tuple-element.52), channel_id=1, source_target_pairs={{0,12},{4,8},{8,4},{12,0},{16,28},{20,24},{24,20},{28,16},{1,13},{... | collective-permute-start | bytes 221192 | tf_op jit(solution)/shard_map/ppermute | solution.py:22
  26.9 7.0 %collective-permute-start.9 = (bf16[2,48,384]{2,1,0:T(8,128)(2,1)S(1)}, bf16[2,48,384]{2,1,0:T(8,128)(2,1)S(1)}, u32[]{:S(2)}, u32[]{:S(2)}) collective-permute-start(bf16[2,48,384]{2,1,0:T(8,128)(2,1)S(1)} %get-tuple-element.53), channel_id=1, source_target_pairs={{0,4},{4,0},{8,12},{12,8},{16,20},{20,16},{24,28},{28,24},{1,5},{5... | collective-permute-start | bytes 221192 | tf_op jit(solution)/shard_map/ppermute | solution.py:22
  28.3 5.6 %collective-permute-start.10 = (bf16[2,48,384]{2,1,0:T(8,128)(2,1)S(1)}, bf16[2,48,384]{2,1,0:T(8,128)(2,1)S(1)}, u32[]{:S(2)}, u32[]{:S(2)}) collective-permute-start(bf16[2,48,384]{2,1,0:T(8,128)(2,1)S(1)} %get-tuple-element.54), channel_id=1, source_target_pairs={{0,8},{4,12},{8,0},{12,4},{16,24},{20,28},{24,16},{28,20},{1,9},{5... | collective-permute-start | bytes 221192 | tf_op jit(solution)/shard_map/ppermute | solution.py:22
  30.4 6.6 %collective-permute-start.5 = (bf16[2,48,384]{2,1,0:T(8,128)(2,1)S(1)}, bf16[2,48,384]{2,1,0:T(8,128)(2,1)S(1)}, u32[]{:S(2)}, u32[]{:S(2)}) collective-permute-start(bf16[2,48,384]{2,1,0:T(8,128)(2,1)S(1)} %get-tuple-element.48), channel_id=1, source_target_pairs={{0,12},{4,8},{8,4},{12,0},{16,28},{20,24},{24,20},{28,16},{1,13},{... | collective-permute-start | bytes 221192 | tf_op jit(solution)/shard_map/ppermute | solution.py:22
  30.4 6.5 %collective-permute-start.6 = (bf16[2,48,384]{2,1,0:T(8,128)(2,1)S(1)}, bf16[2,48,384]{2,1,0:T(8,128)(2,1)S(1)}, u32[]{:S(2)}, u32[]{:S(2)}) collective-permute-start(bf16[2,48,384]{2,1,0:T(8,128)(2,1)S(1)} %get-tuple-element.49), channel_id=1, source_target_pairs={{0,4},{4,0},{8,12},{12,8},{16,20},{20,16},{24,28},{28,24},{1,5},{5... | collective-permute-start | bytes 221192 | tf_op jit(solution)/shard_map/ppermute | solution.py:22
  32.6 4.4 %collective-permute-start.7 = (bf16[2,48,384]{2,1,0:T(8,128)(2,1)S(1)}, bf16[2,48,384]{2,1,0:T(8,128)(2,1)S(1)}, u32[]{:S(2)}, u32[]{:S(2)}) collective-permute-start(bf16[2,48,384]{2,1,0:T(8,128)(2,1)S(1)} %get-tuple-element.50), channel_id=1, source_target_pairs={{0,8},{4,12},{8,0},{12,4},{16,24},{20,28},{24,16},{28,20},{1,9},{5... | collective-permute-start | bytes 221192 | tf_op jit(solution)/shard_map/ppermute | solution.py:22
  33.9 6.4 %collective-permute-start.11 = (bf16[2,48,384]{2,1,0:T(8,128)(2,1)S(1)}, bf16[2,48,384]{2,1,0:T(8,128)(2,1)S(1)}, u32[]{:S(2)}, u32[]{:S(2)}) collective-permute-start(bf16[2,48,384]{2,1,0:T(8,128)(2,1)S(1)} %add_convert_fusion.1), channel_id=1, source_target_pairs={{0,16},{4,20},{8,24},{12,28},{16,0},{20,4},{24,8},{28,12},{1,17},{... | collective-permute-start | bytes 221192 | tf_op jit(solution)/shard_map/ppermute | solution.py:22

commit v4 on v1

--- a/solution.py
+++ b/solution.py
@@ -13,7 +13,7 @@
 HALVES = 2
 NEAR = 2
 KERNEL_VMEM = 24_000_000
-PLAN_FLOPS = 20_000_000_000
+PLAN_FLOPS = 200_000_000_000
 
 
 def flip(x, axis, size, bit):

time: 37.7 us -> 40.3 us (1.069)
  local copies, waits for them, and re-layouts: 1.9 us -> 3.19 us
  Pallas kernels: 11.2 us -> 12.3 us
  other arithmetic: 1.68 us -> 2.58 us
  waiting for transfers between devices: 6.53 us -> 5.89 us
    pallas_call x3, Pallas kernels: 9.47 us -> 10.6 us  [products(): pl.pallas_call(functools.partial(products_kernel, kind, n_opg), out_shape...]
    another operation x1, other arithmetic: 0.04 us -> 0.95 us  [on_device(): halves = [jnp.stack(two) for two in zip(here, there)]]
    slice x1, local copies, waits for them, and re-layouts: 1.17 us -> 1.82 us  [on_device(): ours, rest, psi = lax.optimization_barrier((ours, psi[:local - 1], psi))]
    squeeze x1, local copies, waits for them, and re-layouts: 0.02 us -> 0.67 us  [on_device(): ours = lax.dynamic_index_in_dim(cut, half, axis=0, keepdims=False)]
    ppermute x13, waiting for transfers between devices: 6.53 us -> 5.89 us  [flip(): return lax.ppermute(x, axis, [(i, i ^ bit) for i in range(size)])]
  transfers between devices with their start and end apart: 13 -> 13, of which waited for: 5 -> 4; matrix products, arithmetic and copies ran while one was open for 4% -> 4% of each run, Pallas kernels for 23% -> 24%
where the time goes in v4:
time: 40.3 us; the launch traced here: 39.8 us
  starting transfers between devices  15.7 us (39%)
  Pallas kernels  12.3 us (31%)
  waiting for transfers between devices  5.89 us (15%)
  local copies, waits for them, and re-layouts  3.19 us (8%)
  other arithmetic  2.58 us (6%)
    ppermute x13, starting transfers between devices, flip(): return lax.ppermute(x, axis, [(i, i ^ bit) for i in range(size)])  15.7 us
    pallas_call x3, Pallas kernels, products(): pl.pallas_call(functools.partial(products_kernel, kind, n_opg), out_shape...  10.6 us
    ppermute x13, waiting for transfers between devices, flip(): return lax.ppermute(x, axis, [(i, i ^ bit) for i in range(size)])  5.89 us
    slice x1, local copies, waits for them, and re-layouts, on_device(): ours, rest, psi = lax.optimization_barrier((ours, psi[:local - 1], psi))  1.82 us
    pallas_call x1, Pallas kernels, on_device(): pl.pallas_call(functools.partial(plan_kernel, local), out_shape=(jax.Shap...  1.71 us
    another operation x1, other arithmetic, on_device(): halves = [jnp.stack(two) for two in zip(here, there)]  0.95 us
    reduce_sum x1, other arithmetic, on_device(): jnp.sum(jnp.where(coef_index.T[:, :, None] == table, sixj, 0.0), axis=2)  0.85 us
  transfers between devices with their start and end apart: 13, of which 4 were waited for; matrix products, arithmetic and copies ran while one was open for 4% of the time, Pallas kernels for 24%

profile of v4, /device:TPU:0, one launch (start us, length us, event | category | flops | bytes accessed | tf_op | source)
XLA Modules:
  0.0 39.8 jit_solution(14634793296269439897)
XLA Ops:
  0.0 1.8 %fusion.1 = (bf16[1,384,384]{2,1,0:T(8,128)(2,1)}, bf16[1,384,384]{2,1,0:T(8,128)(2,1)S(1)}) fusion(bf16[2,384,384]{2,1,0:T(8,128)(2,1)} %refs_0_), kind=kLoop, calls=%fused_computation.9 | loop fusion | bytes 1179648 | tf_op jit(solution)/shard_map/slice | solution.py:214
  1.8 0.7 %dynamic-slice_bitcast_fusion = bf16[192,384]{1,0:T(8,128)(2,1)} fusion(bf16[2,192,384]{2,1,0:T(8,128)(2,1)S(1)} %bitcast.10, s32[]{:T(128)S(6)} %select_n.8), kind=kLoop, calls=%fused_computation.3 | loop fusion | bytes 294916 | tf_op jit(solution)/shard_map/jit(dynamic_index_in_dim)/squeeze | solution.py:213
  2.5 3.0 %collective-permute-start = (bf16[192,384]{1,0:T(8,128)(2,1)}, bf16[192,384]{1,0:T(8,128)(2,1)}, u32[]{:S(2)}, u32[]{:S(2)}) collective-permute-start(bf16[192,384]{1,0:T(8,128)(2,1)} %dynamic-slice_bitcast_fusion), channel_id=1, source_target_pairs={{0,2},{1,3},{2,0},{3,1},{4,6},{5,7},{6,4},{7,5},{8,10},{9,11},{10,... | collective-permute-start | bytes 442376 | tf_op jit(solution)/shard_map/ppermute | solution.py:20
  5.5 0.0 collective-permute-start.2
  5.5 0.0 collective-permute-start.3
  5.5 0.7 %convert_bitcast_fusion = f32[2,8]{1,0:T(2,128)S(1)} fusion(s32[8,2]{0,1:T(2,128)} %param.9), kind=kLoop, calls=%fused_computation.8 | loop fusion | flops 16 | bytes 128 | tf_op jit(solution)/shard_map/convert_element_type | solution.py:225
  6.2 0.8 %select_reduce_fusion = f32[2,8]{1,0:T(2,128)S(1)} fusion(f32[64]{0:T(128)} %param.11, s32[2,8]{1,0:T(2,128)} %bitcast.12), kind=kLoop, calls=%fused_computation.5 | loop fusion | flops 3056 | bytes 384 | tf_op jit(solution)/shard_map/reduce_sum | solution.py:224
  7.0 0.0 copy-start.1
  7.1 0.0 copy-start.2
  7.1 1.7 %shard_map.64 = (s32[3,49]{1,0:T(4,128)S(1)}, f32[3,16]{1,0:T(4,128)S(1)}) custom-call(f32[4,8]{1,0:T(4,128)S(1)} %pad_maximum_fusion.1.meta), custom_call_target="tpu_custom_call" | custom-call | flops 199999995904 | tf_op jit(solution)/shard_map/pallas_call | solution.py:226
  8.8 1.7 %collective-permute-done = bf16[192,384]{1,0:T(8,128)(2,1)} collective-permute-done((bf16[192,384]{1,0:T(8,128)(2,1)}, bf16[192,384]{1,0:T(8,128)(2,1)}, u32[]{:S(2)}, u32[]{:S(2)}) %collective-permute-start) | collective-permute-done | bytes 147488 | tf_op jit(solution)/shard_map/ppermute | solution.py:20
  10.4 2.0 %collective-permute-start.1 = (bf16[192,384]{1,0:T(8,128)(2,1)}, bf16[192,384]{1,0:T(8,128)(2,1)S(1)}, u32[]{:S(2)}, u32[]{:S(2)}) collective-permute-start(bf16[192,384]{1,0:T(8,128)(2,1)} %collective-permute-done), channel_id=1, source_target_pairs={{0,4},{4,0},{8,12},{12,8},{16,20},{20,16},{24,28},{28,24},{1,5},{5... | collective-permute-start | bytes 442376 | tf_op jit(solution)/shard_map/ppermute | solution.py:20
  12.5 3.6 %shard_map.65.refs_0_ = f32[2,384,384]{2,1,0:T(8,128)S(1)} custom-call(s32[3,49]{1,0:T(4,128)S(1)} %get-tuple-element.28.plan, f32[3,16]{1,0:T(4,128)S(1)} %get-tuple-element.29.scale, bf16[8,2,384,384]{3,2,1,0:T(8,128)(2,1)S(1)} %copy-done, bf16[8,2,384,384]{3,2,1,0:T(8,128)(2,1)S(1)} %copy-done.1, bf16[2,384,384]{2,1,0:T(8,128)(2,1)S(1)} %copy-done.2, ...), custom_call_target="tpu_custom_call" | custom-call | flops 384 | tf_op jit(solution)/shard_map/pallas_call | solution.py:178
  16.1 0.0 collective-permute-done.1
  16.1 0.9 %pad_maximum_fusion.refs_2_ = bf16[2,192,384]{2,1,0:T(8,128)(2,1)S(1)} fusion(bf16[1,192,384]{2,1,0:T(8,128)(2,1)S(1)} %bitcast.11, bf16[1,192,384]{2,1,0:T(8,128)(2,1)} %bitcast.4), kind=kLoop, calls=%fused_computation | loop fusion | flops 147456 | bytes 589824 | tf_op jit(solution)/shard_map/stack | solution.py:249
  17.1 0.6 %collective-permute-start.5 = (bf16[2,192,384]{2,1,0:T(8,128)(2,1)S(1)}, bf16[2,192,384]{2,1,0:T(8,128)(2,1)S(1)}, u32[]{:S(2)}, u32[]{:S(2)}) collective-permute-start(bf16[2,192,384]{2,1,0:T(8,128)(2,1)S(1)} %pad_maximum_fusion.refs_2_), channel_id=1, source_target_pairs={{0,1},{1,0},{2,3},{3,2},{4,5},{5,4},{6,7},{7,6},{8,9},{9,8},{10,11... | collective-permute-start | bytes 884744 | tf_op jit(solution)/shard_map/ppermute | solution.py:20
  17.6 0.1 collective-permute-start.4
  17.7 4.2 %shard_map.66.refs_0_ = f32[2,384,384]{2,1,0:T(8,128)S(1)} custom-call(s32[3,49]{1,0:T(4,128)S(1)} %get-tuple-element.28.plan, f32[3,16]{1,0:T(4,128)S(1)} %get-tuple-element.29.scale, bf16[8,2,384,384]{3,2,1,0:T(8,128)(2,1)S(1)} %copy-done, bf16[8,2,384,384]{3,2,1,0:T(8,128)(2,1)S(1)} %copy-done.1, f32[2,384,384]{2,1,0:T(8,128)S(1)} %shard_map.65.refs_0_, ...), custom_call_target="tpu_custom_call" | custom-call | flops 384 | tf_op jit(solution)/shard_map/pallas_call | solution.py:178
  21.9 0.0 collective-permute-done.5.refs_2_
  22.0 2.8 %shard_map.67 = (f32[2,48,384]{2,1,0:T(8,128)S(1)}, bf16[2,48,384]{2,1,0:T(8,128)(2,1)S(1)}, bf16[2,48,384]{2,1,0:T(8,128)(2,1)S(1)}, bf16[2,48,384]{2,1,0:T(8,1...) custom-call(s32[3,49]{1,0:T(4,128)S(1)} %get-tuple-element.28.plan, ...), custom_call_target="tpu_custom_call" | custom-call | flops 384 | tf_op jit(solution)/shard_map/pallas_call | solution.py:178
  24.7 1.8 %collective-permute-start.9 = (bf16[2,48,384]{2,1,0:T(8,128)(2,1)S(1)}, bf16[2,48,384]{2,1,0:T(8,128)(2,1)S(1)}, u32[]{:S(2)}, u32[]{:S(2)}) collective-permute-start(bf16[2,48,384]{2,1,0:T(8,128)(2,1)S(1)} %get-tuple-element.42), channel_id=1, source_target_pairs={{0,12},{4,8},{8,4},{12,0},{16,28},{20,24},{24,20},{28,16},{1,13},{... | collective-permute-start | bytes 221192 | tf_op jit(solution)/shard_map/ppermute | solution.py:20
  26.5 1.3 %collective-permute-start.10 = (bf16[2,48,384]{2,1,0:T(8,128)(2,1)S(1)}, bf16[2,48,384]{2,1,0:T(8,128)(2,1)S(1)}, u32[]{:S(2)}, u32[]{:S(2)}) collective-permute-start(bf16[2,48,384]{2,1,0:T(8,128)(2,1)S(1)} %get-tuple-element.43), channel_id=1, source_target_pairs={{0,4},{4,0},{8,12},{12,8},{16,20},{20,16},{24,28},{28,24},{1,5},{5... | collective-permute-start | bytes 221192 | tf_op jit(solution)/shard_map/ppermute | solution.py:20
  27.8 0.5 %collective-permute-start.11 = (bf16[2,48,384]{2,1,0:T(8,128)(2,1)S(1)}, bf16[2,48,384]{2,1,0:T(8,128)(2,1)S(1)}, u32[]{:S(2)}, u32[]{:S(2)}) collective-permute-start(bf16[2,48,384]{2,1,0:T(8,128)(2,1)S(1)} %get-tuple-element.44), channel_id=1, source_target_pairs={{0,8},{4,12},{8,0},{12,4},{16,24},{20,28},{24,16},{28,20},{1,9},{5... | collective-permute-start | bytes 221192 | tf_op jit(solution)/shard_map/ppermute | solution.py:20
  28.3 1.7 %collective-permute-start.6 = (bf16[2,48,384]{2,1,0:T(8,128)(2,1)S(1)}, bf16[2,48,384]{2,1,0:T(8,128)(2,1)S(1)}, u32[]{:S(2)}, u32[]{:S(2)}) collective-permute-start(bf16[2,48,384]{2,1,0:T(8,128)(2,1)S(1)} %get-tuple-element.38), channel_id=1, source_target_pairs={{0,12},{4,8},{8,4},{12,0},{16,28},{20,24},{24,20},{28,16},{1,13},{... | collective-permute-start | bytes 221192 | tf_op jit(solution)/shard_map/ppermute | solution.py:20
  30.0 1.3 %collective-permute-start.7 = (bf16[2,48,384]{2,1,0:T(8,128)(2,1)S(1)}, bf16[2,48,384]{2,1,0:T(8,128)(2,1)S(1)}, u32[]{:S(2)}, u32[]{:S(2)}) collective-permute-start(bf16[2,48,384]{2,1,0:T(8,128)(2,1)S(1)} %get-tuple-element.39), channel_id=1, source_target_pairs={{0,4},{4,0},{8,12},{12,8},{16,20},{20,16},{24,28},{28,24},{1,5},{5... | collective-permute-start | bytes 221192 | tf_op jit(solution)/shard_map/ppermute | solution.py:20
  31.3 1.0 %collective-permute-start.8 = (bf16[2,48,384]{2,1,0:T(8,128)(2,1)S(1)}, bf16[2,48,384]{2,1,0:T(8,128)(2,1)S(1)}, u32[]{:S(2)}, u32[]{:S(2)}) collective-permute-start(bf16[2,48,384]{2,1,0:T(8,128)(2,1)S(1)} %get-tuple-element.40), channel_id=1, source_target_pairs={{0,8},{4,12},{8,0},{12,4},{16,24},{20,28},{24,16},{28,20},{1,9},{5... | collective-permute-start | bytes 221192 | tf_op jit(solution)/shard_map/ppermute | solution.py:20
  32.3 0.4 %collective-permute-done.11 = bf16[2,48,384]{2,1,0:T(8,128)(2,1)S(1)} collective-permute-done((bf16[2,48,384]{2,1,0:T(8,128)(2,1)S(1)}, bf16[2,48,384]{2,1,0:T(8,128)(2,1)S(1)}, u32[]{:S(2)}, u32[]{:S(2)}) %collective-permute-start.11) | collective-permute-done | bytes 73760 | tf_op jit(solution)/shard_map/ppermute | solution.py:20
  32.8 2.5 %collective-permute-start.12 = (bf16[2,48,384]{2,1,0:T(8,128)(2,1)S(1)}, bf16[2,48,384]{2,1,0:T(8,128)(2,1)S(1)}, u32[]{:S(2)}, u32[]{:S(2)}) collective-permute-start(bf16[2,48,384]{2,1,0:T(8,128)(2,1)S(1)} %add_convert_fusion.1), channel_id=1, source_target_pairs={{0,16},{4,20},{8,24},{12,28},{16,0},{20,4},{24,8},{28,12},{1,17},{... | collective-permute-start | bytes 221192 | tf_op jit(solution)/shard_map/ppermute | solution.py:20
  35.3 0.4 collective-permute-done.8
  35.6 3.4 %collective-permute-done.12 = bf16[2,48,384]{2,1,0:T(8,128)(2,1)S(1)} collective-permute-done((bf16[2,48,384]{2,1,0:T(8,128)(2,1)S(1)}, bf16[2,48,384]{2,1,0:T(8,128)(2,1)S(1)}, u32[]{:S(2)}, u32[]{:S(2)}) %collective-permute-start.12) | collective-permute-done | bytes 73760 | tf_op jit(solution)/shard_map/ppermute | solution.py:20
  39.0 0.1 fusion
  39.1 0.7 %copy.8 = bf16[48,2,384]{2,1,0:T(2,128)(2,1)} copy(bf16[48,2,384]{2,0,1:T(8,128)(2,1)S(1)} %fusion) | data formatting | bytes 147456 | tf_op jit(solution)/shard_map/convert_element_type | solution.py:253
  (13 shorter events, 0.1 us)
Async XLA Ops:
  2.5 8.0 %collective-permute-start = (bf16[192,384]{1,0:T(8,128)(2,1)}, bf16[192,384]{1,0:T(8,128)(2,1)}, u32[]{:S(2)}, u32[]{:S(2)}) collective-permute-start(bf16[192,384]{1,0:T(8,128)(2,1)} %dynamic-slice_bitcast_fusion), channel_id=1, source_target_pairs={{0,2},{1,3},{2,0},{3,1},{4,6},{5,7},{6,4},{7,5},{8,10},{9,11},{10,... | collective-permute-start | bytes 442376 | tf_op jit(solution)/shard_map/ppermute | solution.py:20
  5.5 10.6 %collective-permute-start.2 = (bf16[1,384,384]{2,1,0:T(8,128)(2,1)}, bf16[1,384,384]{2,1,0:T(8,128)(2,1)}, u32[]{:S(2)}, u32[]{:S(2)}) collective-permute-start(bf16[1,384,384]{2,1,0:T(8,128)(2,1)} %get-tuple-element.31), channel_id=1, source_target_pairs={{0,2},{1,3},{2,0},{3,1},{4,6},{5,7},{6,4},{7,5},{8,10},{9,11},{10,... | collective-permute-start | bytes 884744 | tf_op jit(solution)/shard_map/ppermute | solution.py:20
  5.5 7.0 %collective-permute-start.3 = (bf16[2,384,384]{2,1,0:T(8,128)(2,1)}, bf16[2,384,384]{2,1,0:T(8,128)(2,1)}, u32[]{:S(2)}, u32[]{:S(2)}) collective-permute-start(bf16[2,384,384]{2,1,0:T(8,128)(2,1)} %refs_0_), channel_id=1, source_target_pairs={{0,1},{1,0},{2,3},{3,2},{4,5},{5,4},{6,7},{7,6},{8,9},{9,8},{10,11... | collective-permute-start | bytes 1769480 | tf_op jit(solution)/shard_map/ppermute | solution.py:20
  7.0 5.4 %copy-start = (bf16[8,2,384,384]{3,2,1,0:T(8,128)(2,1)S(1)}, bf16[8,2,384,384]{3,2,1,0:T(8,128)(2,1)}, u32[]{:S(2)}) copy-start(bf16[8,2,384,384]{3,2,1,0:T(8,128)(2,1)} %left.5) | copy-start | bytes 14155780
  7.0 5.4 %copy-start.1 = (bf16[8,2,384,384]{3,2,1,0:T(8,128)(2,1)S(1)}, bf16[8,2,384,384]{3,2,1,0:T(8,128)(2,1)}, u32[]{:S(2)}) copy-start(bf16[8,2,384,384]{3,2,1,0:T(8,128)(2,1)} %right.5) | copy-start | bytes 14155780
  7.1 5.4 %copy-start.2 = (bf16[2,384,384]{2,1,0:T(8,128)(2,1)S(1)}, bf16[2,384,384]{2,1,0:T(8,128)(2,1)}, u32[]{:S(2)}) copy-start(bf16[2,384,384]{2,1,0:T(8,128)(2,1)} %refs_0_) | copy-start | bytes 1769476
  10.4 5.6 %collective-permute-start.1 = (bf16[192,384]{1,0:T(8,128)(2,1)}, bf16[192,384]{1,0:T(8,128)(2,1)S(1)}, u32[]{:S(2)}, u32[]{:S(2)}) collective-permute-start(bf16[192,384]{1,0:T(8,128)(2,1)} %collective-permute-done), channel_id=1, source_target_pairs={{0,4},{4,0},{8,12},{12,8},{16,20},{20,16},{24,28},{28,24},{1,5},{5... | collective-permute-start | bytes 442376 | tf_op jit(solution)/shard_map/ppermute | solution.py:20
  17.1 4.9 %collective-permute-start.5 = (bf16[2,192,384]{2,1,0:T(8,128)(2,1)S(1)}, bf16[2,192,384]{2,1,0:T(8,128)(2,1)S(1)}, u32[]{:S(2)}, u32[]{:S(2)}) collective-permute-start(bf16[2,192,384]{2,1,0:T(8,128)(2,1)S(1)} %pad_maximum_fusion.refs_2_), channel_id=1, source_target_pairs={{0,1},{1,0},{2,3},{3,2},{4,5},{5,4},{6,7},{7,6},{8,9},{9,8},{10,11... | collective-permute-start | bytes 884744 | tf_op jit(solution)/shard_map/ppermute | solution.py:20
  17.6 4.3 %collective-permute-start.4 = (bf16[1,384,384]{2,1,0:T(8,128)(2,1)}, bf16[1,384,384]{2,1,0:T(8,128)(2,1)S(1)}, u32[]{:S(2)}, u32[]{:S(2)}) collective-permute-start(bf16[1,384,384]{2,1,0:T(8,128)(2,1)} %collective-permute-done.2.refs_1_), channel_id=1, source_target_pairs={{0,1},{1,0},{2,3},{3,2},{4,5},{5,4},{6,7},{7,6},{8,9},{9,8},{10,11... | collective-permute-start | bytes 884744 | tf_op jit(solution)/shard_map/ppermute | solution.py:20
  24.7 6.5 %collective-permute-start.9 = (bf16[2,48,384]{2,1,0:T(8,128)(2,1)S(1)}, bf16[2,48,384]{2,1,0:T(8,128)(2,1)S(1)}, u32[]{:S(2)}, u32[]{:S(2)}) collective-permute-start(bf16[2,48,384]{2,1,0:T(8,128)(2,1)S(1)} %get-tuple-element.42), channel_id=1, source_target_pairs={{0,12},{4,8},{8,4},{12,0},{16,28},{20,24},{24,20},{28,16},{1,13},{... | collective-permute-start | bytes 221192 | tf_op jit(solution)/shard_map/ppermute | solution.py:20
  26.5 5.8 %collective-permute-start.10 = (bf16[2,48,384]{2,1,0:T(8,128)(2,1)S(1)}, bf16[2,48,384]{2,1,0:T(8,128)(2,1)S(1)}, u32[]{:S(2)}, u32[]{:S(2)}) collective-permute-start(bf16[2,48,384]{2,1,0:T(8,128)(2,1)S(1)} %get-tuple-element.43), channel_id=1, source_target_pairs={{0,4},{4,0},{8,12},{12,8},{16,20},{20,16},{24,28},{28,24},{1,5},{5... | collective-permute-start | bytes 221192 | tf_op jit(solution)/shard_map/ppermute | solution.py:20
  27.8 4.9 %collective-permute-start.11 = (bf16[2,48,384]{2,1,0:T(8,128)(2,1)S(1)}, bf16[2,48,384]{2,1,0:T(8,128)(2,1)S(1)}, u32[]{:S(2)}, u32[]{:S(2)}) collective-permute-start(bf16[2,48,384]{2,1,0:T(8,128)(2,1)S(1)} %get-tuple-element.44), channel_id=1, source_target_pairs={{0,8},{4,12},{8,0},{12,4},{16,24},{20,28},{24,16},{28,20},{1,9},{5... | collective-permute-start | bytes 221192 | tf_op jit(solution)/shard_map/ppermute | solution.py:20
  28.3 7.0 %collective-permute-start.6 = (bf16[2,48,384]{2,1,0:T(8,128)(2,1)S(1)}, bf16[2,48,384]{2,1,0:T(8,128)(2,1)S(1)}, u32[]{:S(2)}, u32[]{:S(2)}) collective-permute-start(bf16[2,48,384]{2,1,0:T(8,128)(2,1)S(1)} %get-tuple-element.38), channel_id=1, source_target_pairs={{0,12},{4,8},{8,4},{12,0},{16,28},{20,24},{24,20},{28,16},{1,13},{... | collective-permute-start | bytes 221192 | tf_op jit(solution)/shard_map/ppermute | solution.py:20
  30.0 5.3 %collective-permute-start.7 = (bf16[2,48,384]{2,1,0:T(8,128)(2,1)S(1)}, bf16[2,48,384]{2,1,0:T(8,128)(2,1)S(1)}, u32[]{:S(2)}, u32[]{:S(2)}) collective-permute-start(bf16[2,48,384]{2,1,0:T(8,128)(2,1)S(1)} %get-tuple-element.39), channel_id=1, source_target_pairs={{0,4},{4,0},{8,12},{12,8},{16,20},{20,16},{24,28},{28,24},{1,5},{5... | collective-permute-start | bytes 221192 | tf_op jit(solution)/shard_map/ppermute | solution.py:20
  31.3 4.4 %collective-permute-start.8 = (bf16[2,48,384]{2,1,0:T(8,128)(2,1)S(1)}, bf16[2,48,384]{2,1,0:T(8,128)(2,1)S(1)}, u32[]{:S(2)}, u32[]{:S(2)}) collective-permute-start(bf16[2,48,384]{2,1,0:T(8,128)(2,1)S(1)} %get-tuple-element.40), channel_id=1, source_target_pairs={{0,8},{4,12},{8,0},{12,4},{16,24},{20,28},{24,16},{28,20},{1,9},{5... | collective-permute-start | bytes 221192 | tf_op jit(solution)/shard_map/ppermute | solution.py:20
  32.8 6.3 %collective-permute-start.12 = (bf16[2,48,384]{2,1,0:T(8,128)(2,1)S(1)}, bf16[2,48,384]{2,1,0:T(8,128)(2,1)S(1)}, u32[]{:S(2)}, u32[]{:S(2)}) collective-permute-start(bf16[2,48,384]{2,1,0:T(8,128)(2,1)S(1)} %add_convert_fusion.1), channel_id=1, source_target_pairs={{0,16},{4,20},{8,24},{12,28},{16,0},{20,4},{24,8},{28,12},{1,17},{... | collective-permute-start | bytes 221192 | tf_op jit(solution)/shard_map/ppermute | solution.py:20

commit v5 on v2

--- a/solution.py
+++ b/solution.py
@@ -13,7 +13,7 @@
 HALVES = 2
 NEAR = 2
 KERNEL_VMEM = 24_000_000
-PLAN_FLOPS = 20_000_000_000
+PLAN_FLOPS = 5_000_000_000
 
 
 def flip(x, axis, size, bit):

time: 41.6 us -> 41.4 us (level)
  starting transfers between devices: 15.8 us -> 14.8 us
  waiting for transfers between devices: 7.18 us -> 7.95 us
    ppermute x12, starting transfers between devices: 15.8 us -> 14.8 us  [flip(): return lax.ppermute(x, axis, [(i, i ^ bit) for i in range(size)])]
    ppermute x12, waiting for transfers between devices: 7.18 us -> 7.95 us  [flip(): return lax.ppermute(x, axis, [(i, i ^ bit) for i in range(size)])]
  transfers between devices with their start and end apart: 12 -> 12, of which waited for: 4 -> 4; matrix products, arithmetic and copies ran while one was open for 0% -> 0% of each run, Pallas kernels for 20% -> 23%
where the time goes in v5:
time: 41.4 us; the launch traced here: 41.1 us
  starting transfers between devices  14.8 us (36%)
  Pallas kernels  11.3 us (27%)
  waiting for transfers between devices  7.95 us (19%)
  local copies, waits for them, and re-layouts  6.58 us (16%)
    ppermute x12, starting transfers between devices, flip(): return lax.ppermute(x, axis, [(i, i ^ bit) for i in range(size)])  14.8 us
    pallas_call x3, Pallas kernels, products(): pl.pallas_call(functools.partial(products_kernel, kind, n_opg), out_shape...  9.66 us
    ppermute x12, waiting for transfers between devices, flip(): return lax.ppermute(x, axis, [(i, i ^ bit) for i in range(size)])  7.95 us
    unnamed x12, local copies, waits for them, and re-layouts  4.69 us
    pallas_call x1, Pallas kernels, on_device(): pl.pallas_call(functools.partial(plan_kernel, local), out_shape=jax.Shape...  1.6 us
    slice x1, local copies, waits for them, and re-layouts, on_device(): ours, rest, psi = lax.optimization_barrier((ours, psi[:local - 1], psi))  1.17 us
  transfers between devices with their start and end apart: 12, of which 4 were waited for; matrix products, arithmetic and copies ran while one was open for 0% of the time, Pallas kernels for 23%

profile of v5, /device:TPU:0, one launch (start us, length us, event | category | flops | bytes accessed | tf_op | source)
XLA Modules:
  0.0 41.1 jit_solution(8729889264915534593)
XLA Ops:
  0.0 1.2 %fusion.1 = (bf16[1,384,384]{2,1,0:T(8,128)(2,1)S(1)}, bf16[1,384,384]{2,1,0:T(8,128)(2,1)S(1)}) fusion(bf16[2,384,384]{2,1,0:T(8,128)(2,1)} %refs_0_), kind=kLoop, calls=%fused_computation.9 | loop fusion | bytes 1179648 | tf_op jit(solution)/shard_map/slice | solution.py:206
  1.2 3.0 %collective-permute-start = (bf16[192,384]{1,0:T(8,128)(2,1)S(1)}, bf16[192,384]{1,0:T(8,128)(2,1)S(1)}, u32[]{:S(2)}, u32[]{:S(2)}) collective-permute-start(bf16[192,384]{1,0:T(8,128)(2,1)S(1)} %dynamic-slice_bitcast_fusion), channel_id=1, source_target_pairs={{0,2},{1,3},{2,0},{3,1},{4,6},{5,7},{6,4},{7,5},{8,10},{9,11},{10,... | collective-permute-start | bytes 442376 | tf_op jit(solution)/shard_map/ppermute | solution.py:20
  4.2 0.1 collective-permute-start.2
  4.3 0.0 collective-permute-start.3
  4.3 0.0 copy-start.4
  4.4 0.0 copy-start.5
  4.4 1.6 %shard_map.64.plan = s32[3,49]{1,0:T(4,128)S(1)} custom-call(s32[2,8]{1,0:T(2,128)S(1)} %bitcast.11), custom_call_target="tpu_custom_call" | custom-call | flops 5000000000 | tf_op jit(solution)/shard_map/pallas_call | solution.py:215
  6.0 0.2 select_reduce_fusion.coef
  6.1 2.8 %collective-permute-done = bf16[192,384]{1,0:T(8,128)(2,1)S(1)} collective-permute-done((bf16[192,384]{1,0:T(8,128)(2,1)S(1)}, bf16[192,384]{1,0:T(8,128)(2,1)S(1)}, u32[]{:S(2)}, u32[]{:S(2)}) %collective-permute-start) | collective-permute-done | bytes 147488 | tf_op jit(solution)/shard_map/ppermute | solution.py:20
  8.9 2.0 %collective-permute-start.1 = (bf16[192,384]{1,0:T(8,128)(2,1)S(1)}, bf16[192,384]{1,0:T(8,128)(2,1)S(1)}, u32[]{:S(2)}, u32[]{:S(2)}) collective-permute-start(bf16[192,384]{1,0:T(8,128)(2,1)S(1)} %collective-permute-done), channel_id=1, source_target_pairs={{0,4},{4,0},{8,12},{12,8},{16,20},{20,16},{24,28},{28,24},{1,5},{5... | collective-permute-start | bytes 442376 | tf_op jit(solution)/shard_map/ppermute | solution.py:20
  11.0 2.3 %copy-done = bf16[8,2,384,384]{3,2,1,0:T(8,128)(2,1)S(1)} copy-done((bf16[8,2,384,384]{3,2,1,0:T(8,128)(2,1)S(1)}, bf16[8,2,384,384]{3,2,1,0:T(8,128)(2,1)}, u32[]{:S(2)}) %copy-start) | copy-done | bytes 4718616
  13.3 2.3 %copy-done.1 = bf16[8,2,384,384]{3,2,1,0:T(8,128)(2,1)S(1)} copy-done((bf16[8,2,384,384]{3,2,1,0:T(8,128)(2,1)S(1)}, bf16[8,2,384,384]{3,2,1,0:T(8,128)(2,1)}, u32[]{:S(2)}) %copy-start.1) | copy-done | bytes 4718616
  15.6 5.2 %shard_map.65.refs_0_ = f32[2,384,384]{2,1,0:T(8,128)S(1)} custom-call(s32[3,49]{1,0:T(4,128)S(1)} %shard_map.64.plan, f32[2,8]{1,0:T(2,128)S(1)} %select_reduce_fusion.coef, bf16[8,2,384,384]{3,2,1,0:T(8,128)(2,1)S(1)} %copy-done, bf16[8,2,384,384]{3,2,1,0:T(8,128)(2,1)S(1)} %copy-done.1, bf16[2,384,384]{2,1,0:T(8,128)(2,1)S(1)} %copy-done.2, ...), custom_call_target="tpu_custom_call" | custom-call | flops 384 | tf_op jit(solution)/shard_map/pallas_call | solution.py:170
  20.8 0.0 collective-permute-done.1
  20.9 0.1 pad_maximum_fusion
  20.9 0.1 collective-permute-start.4
  21.0 2.6 %shard_map.66.refs_0_ = f32[2,384,384]{2,1,0:T(8,128)S(1)} custom-call(s32[3,49]{1,0:T(4,128)S(1)} %shard_map.64.plan, f32[2,8]{1,0:T(2,128)S(1)} %select_reduce_fusion.coef, bf16[8,2,384,384]{3,2,1,0:T(8,128)(2,1)S(1)} %copy-done, bf16[8,2,384,384]{3,2,1,0:T(8,128)(2,1)S(1)} %copy-done.1, f32[2,384,384]{2,1,0:T(8,128)S(1)} %shard_map.65.refs_0_, ...), custom_call_target="tpu_custom_call" | custom-call | flops 384 | tf_op jit(solution)/shard_map/pallas_call | solution.py:170
  23.7 1.9 %shard_map.67 = (f32[2,48,384]{2,1,0:T(8,128)S(1)}, bf16[2,48,384]{2,1,0:T(8,128)(2,1)S(1)}, bf16[2,48,384]{2,1,0:T(8,128)(2,1)S(1)}, bf16[2,48,384]{2,1,0:T(8,1...) custom-call(s32[3,49]{1,0:T(4,128)S(1)} %shard_map.64.plan, ...), custom_call_target="tpu_custom_call" | custom-call | flops 384 | tf_op jit(solution)/shard_map/pallas_call | solution.py:170
  25.5 2.1 %collective-permute-start.8 = (bf16[2,48,384]{2,1,0:T(8,128)(2,1)S(1)}, bf16[2,48,384]{2,1,0:T(8,128)(2,1)S(1)}, u32[]{:S(2)}, u32[]{:S(2)}) collective-permute-start(bf16[2,48,384]{2,1,0:T(8,128)(2,1)S(1)} %get-tuple-element.42), channel_id=1, source_target_pairs={{0,12},{4,8},{8,4},{12,0},{16,28},{20,24},{24,20},{28,16},{1,13},{... | collective-permute-start | bytes 221192 | tf_op jit(solution)/shard_map/ppermute | solution.py:20
  27.7 0.9 %collective-permute-start.9 = (bf16[2,48,384]{2,1,0:T(8,128)(2,1)S(1)}, bf16[2,48,384]{2,1,0:T(8,128)(2,1)S(1)}, u32[]{:S(2)}, u32[]{:S(2)}) collective-permute-start(bf16[2,48,384]{2,1,0:T(8,128)(2,1)S(1)} %get-tuple-element.43), channel_id=1, source_target_pairs={{0,4},{4,0},{8,12},{12,8},{16,20},{20,16},{24,28},{28,24},{1,5},{5... | collective-permute-start | bytes 221192 | tf_op jit(solution)/shard_map/ppermute | solution.py:20
  28.5 0.6 %collective-permute-start.10 = (bf16[2,48,384]{2,1,0:T(8,128)(2,1)S(1)}, bf16[2,48,384]{2,1,0:T(8,128)(2,1)S(1)}, u32[]{:S(2)}, u32[]{:S(2)}) collective-permute-start(bf16[2,48,384]{2,1,0:T(8,128)(2,1)S(1)} %get-tuple-element.44), channel_id=1, source_target_pairs={{0,8},{4,12},{8,0},{12,4},{16,24},{20,28},{24,16},{28,20},{1,9},{5... | collective-permute-start | bytes 221192 | tf_op jit(solution)/shard_map/ppermute | solution.py:20
  29.1 2.1 %collective-permute-start.5 = (bf16[2,48,384]{2,1,0:T(8,128)(2,1)S(1)}, bf16[2,48,384]{2,1,0:T(8,128)(2,1)S(1)}, u32[]{:S(2)}, u32[]{:S(2)}) collective-permute-start(bf16[2,48,384]{2,1,0:T(8,128)(2,1)S(1)} %get-tuple-element.38), channel_id=1, source_target_pairs={{0,12},{4,8},{8,4},{12,0},{16,28},{20,24},{24,20},{28,16},{1,13},{... | collective-permute-start | bytes 221192 | tf_op jit(solution)/shard_map/ppermute | solution.py:20
  31.2 0.9 %collective-permute-start.6 = (bf16[2,48,384]{2,1,0:T(8,128)(2,1)S(1)}, bf16[2,48,384]{2,1,0:T(8,128)(2,1)S(1)}, u32[]{:S(2)}, u32[]{:S(2)}) collective-permute-start(bf16[2,48,384]{2,1,0:T(8,128)(2,1)S(1)} %get-tuple-element.39), channel_id=1, source_target_pairs={{0,4},{4,0},{8,12},{12,8},{16,20},{20,16},{24,28},{28,24},{1,5},{5... | collective-permute-start | bytes 221192 | tf_op jit(solution)/shard_map/ppermute | solution.py:20
  32.0 0.0 collective-permute-done.8
  32.0 0.6 %collective-permute-start.7 = (bf16[2,48,384]{2,1,0:T(8,128)(2,1)S(1)}, bf16[2,48,384]{2,1,0:T(8,128)(2,1)S(1)}, u32[]{:S(2)}, u32[]{:S(2)}) collective-permute-start(bf16[2,48,384]{2,1,0:T(8,128)(2,1)S(1)} %get-tuple-element.40), channel_id=1, source_target_pairs={{0,8},{4,12},{8,0},{12,4},{16,24},{20,28},{24,16},{28,20},{1,9},{5... | collective-permute-start | bytes 221192 | tf_op jit(solution)/shard_map/ppermute | solution.py:20
  32.6 0.9 %collective-permute-done.9 = bf16[2,48,384]{2,1,0:T(8,128)(2,1)S(1)} collective-permute-done((bf16[2,48,384]{2,1,0:T(8,128)(2,1)S(1)}, bf16[2,48,384]{2,1,0:T(8,128)(2,1)S(1)}, u32[]{:S(2)}, u32[]{:S(2)}) %collective-permute-start.9) | collective-permute-done | bytes 73760 | tf_op jit(solution)/shard_map/ppermute | solution.py:20
  33.5 0.0 collective-permute-done.10
  33.6 2.6 %collective-permute-start.11 = (bf16[2,48,384]{2,1,0:T(8,128)(2,1)S(1)}, bf16[2,48,384]{2,1,0:T(8,128)(2,1)S(1)}, u32[]{:S(2)}, u32[]{:S(2)}) collective-permute-start(bf16[2,48,384]{2,1,0:T(8,128)(2,1)S(1)} %add_convert_fusion.1), channel_id=1, source_target_pairs={{0,16},{4,20},{8,24},{12,28},{16,0},{20,4},{24,8},{28,12},{1,17},{... | collective-permute-start | bytes 221192 | tf_op jit(solution)/shard_map/ppermute | solution.py:20
  36.1 1.1 %collective-permute-done.6 = bf16[2,48,384]{2,1,0:T(8,128)(2,1)S(1)} collective-permute-done((bf16[2,48,384]{2,1,0:T(8,128)(2,1)S(1)}, bf16[2,48,384]{2,1,0:T(8,128)(2,1)S(1)}, u32[]{:S(2)}, u32[]{:S(2)}) %collective-permute-start.6) | collective-permute-done | bytes 73760 | tf_op jit(solution)/shard_map/ppermute | solution.py:20
  37.3 3.1 %collective-permute-done.11 = bf16[2,48,384]{2,1,0:T(8,128)(2,1)S(1)} collective-permute-done((bf16[2,48,384]{2,1,0:T(8,128)(2,1)S(1)}, bf16[2,48,384]{2,1,0:T(8,128)(2,1)S(1)}, u32[]{:S(2)}, u32[]{:S(2)}) %collective-permute-start.11) | collective-permute-done | bytes 73760 | tf_op jit(solution)/shard_map/ppermute | solution.py:20
  40.4 0.1 fusion
  40.4 0.7 %copy.8 = bf16[48,2,384]{2,1,0:T(2,128)(2,1)} copy(bf16[48,2,384]{2,0,1:T(8,128)(2,1)S(1)} %fusion) | data formatting | bytes 147456 | tf_op jit(solution)/shard_map/convert_element_type | solution.py:245
  (16 shorter events, 0.1 us)
Async XLA Ops:
  0.0 4.3 %copy-start.2 = (bf16[2,384,384]{2,1,0:T(8,128)(2,1)S(1)}, bf16[2,384,384]{2,1,0:T(8,128)(2,1)}, u32[]{:S(2)}) copy-start(bf16[2,384,384]{2,1,0:T(8,128)(2,1)} %refs_0_) | copy-start | bytes 1769476
  0.0 4.3 %copy-start.3 = (s32[8,2]{0,1:T(2,128)S(1)}, s32[8,2]{0,1:T(2,128)}, u32[]{:S(2)}) copy-start(s32[8,2]{0,1:T(2,128)} %param.9) | copy-start | bytes 196
  1.2 7.7 %collective-permute-start = (bf16[192,384]{1,0:T(8,128)(2,1)S(1)}, bf16[192,384]{1,0:T(8,128)(2,1)S(1)}, u32[]{:S(2)}, u32[]{:S(2)}) collective-permute-start(bf16[192,384]{1,0:T(8,128)(2,1)S(1)} %dynamic-slice_bitcast_fusion), channel_id=1, source_target_pairs={{0,2},{1,3},{2,0},{3,1},{4,6},{5,7},{6,4},{7,5},{8,10},{9,11},{10,... | collective-permute-start | bytes 442376 | tf_op jit(solution)/shard_map/ppermute | solution.py:20
  4.2 16.6 %collective-permute-start.2 = (bf16[1,384,384]{2,1,0:T(8,128)(2,1)S(1)}, bf16[1,384,384]{2,1,0:T(8,128)(2,1)S(1)}, u32[]{:S(2)}, u32[]{:S(2)}) collective-permute-start(bf16[1,384,384]{2,1,0:T(8,128)(2,1)S(1)} %get-tuple-element.31), channel_id=1, source_target_pairs={{0,2},{1,3},{2,0},{3,1},{4,6},{5,7},{6,4},{7,5},{8,10},{9,11},{10,... | collective-permute-start | bytes 884744 | tf_op jit(solution)/shard_map/ppermute | solution.py:20
  4.3 6.6 %collective-permute-start.3 = (bf16[2,384,384]{2,1,0:T(8,128)(2,1)S(1)}, bf16[2,384,384]{2,1,0:T(8,128)(2,1)S(1)}, u32[]{:S(2)}, u32[]{:S(2)}) collective-permute-start(bf16[2,384,384]{2,1,0:T(8,128)(2,1)S(1)} %copy-done.2), channel_id=1, source_target_pairs={{0,1},{1,0},{2,3},{3,2},{4,5},{5,4},{6,7},{7,6},{8,9},{9,8},{10,11... | collective-permute-start | bytes 1769480 | tf_op jit(solution)/shard_map/ppermute | solution.py:20
  4.3 1.6 %copy-start.4 = (s32[8,2]{0,1:T(2,128)S(1)}, s32[8,2]{0,1:T(2,128)}, u32[]{:S(2)}) copy-start(s32[8,2]{0,1:T(2,128)} %param.10) | copy-start | bytes 196
  4.4 1.6 %copy-start.5 = (f32[64]{0:T(128)S(1)}, f32[64]{0:T(128)}, u32[]{:S(2)}) copy-start(f32[64]{0:T(128)} %param.11) | copy-start | bytes 772
  8.9 11.9 %collective-permute-start.1 = (bf16[192,384]{1,0:T(8,128)(2,1)S(1)}, bf16[192,384]{1,0:T(8,128)(2,1)S(1)}, u32[]{:S(2)}, u32[]{:S(2)}) collective-permute-start(bf16[192,384]{1,0:T(8,128)(2,1)S(1)} %collective-permute-done), channel_id=1, source_target_pairs={{0,4},{4,0},{8,12},{12,8},{16,20},{20,16},{24,28},{28,24},{1,5},{5... | collective-permute-start | bytes 442376 | tf_op jit(solution)/shard_map/ppermute | solution.py:20
  11.0 2.3 %copy-start = (bf16[8,2,384,384]{3,2,1,0:T(8,128)(2,1)S(1)}, bf16[8,2,384,384]{3,2,1,0:T(8,128)(2,1)}, u32[]{:S(2)}) copy-start(bf16[8,2,384,384]{3,2,1,0:T(8,128)(2,1)} %left.5) | copy-start | bytes 14155780
  13.3 2.3 %copy-start.1 = (bf16[8,2,384,384]{3,2,1,0:T(8,128)(2,1)S(1)}, bf16[8,2,384,384]{3,2,1,0:T(8,128)(2,1)}, u32[]{:S(2)}) copy-start(bf16[8,2,384,384]{3,2,1,0:T(8,128)(2,1)} %right.5) | copy-start | bytes 14155780
  20.9 2.7 %collective-permute-start.4 = (bf16[2,384,384]{2,1,0:T(8,128)(2,1)S(1)}, bf16[2,384,384]{2,1,0:T(8,128)(2,1)S(1)}, u32[]{:S(2)}, u32[]{:S(2)}) collective-permute-start(bf16[2,384,384]{2,1,0:T(8,128)(2,1)S(1)} %bitcast.9), channel_id=1, source_target_pairs={{0,1},{1,0},{2,3},{3,2},{4,5},{5,4},{6,7},{7,6},{8,9},{9,8},{10,11... | collective-permute-start | bytes 1769480 | tf_op jit(solution)/shard_map/ppermute | solution.py:20
  25.5 6.5 %collective-permute-start.8 = (bf16[2,48,384]{2,1,0:T(8,128)(2,1)S(1)}, bf16[2,48,384]{2,1,0:T(8,128)(2,1)S(1)}, u32[]{:S(2)}, u32[]{:S(2)}) collective-permute-start(bf16[2,48,384]{2,1,0:T(8,128)(2,1)S(1)} %get-tuple-element.42), channel_id=1, source_target_pairs={{0,12},{4,8},{8,4},{12,0},{16,28},{20,24},{24,20},{28,16},{1,13},{... | collective-permute-start | bytes 221192 | tf_op jit(solution)/shard_map/ppermute | solution.py:20
  27.7 5.8 %collective-permute-start.9 = (bf16[2,48,384]{2,1,0:T(8,128)(2,1)S(1)}, bf16[2,48,384]{2,1,0:T(8,128)(2,1)S(1)}, u32[]{:S(2)}, u32[]{:S(2)}) collective-permute-start(bf16[2,48,384]{2,1,0:T(8,128)(2,1)S(1)} %get-tuple-element.43), channel_id=1, source_target_pairs={{0,4},{4,0},{8,12},{12,8},{16,20},{20,16},{24,28},{28,24},{1,5},{5... | collective-permute-start | bytes 221192 | tf_op jit(solution)/shard_map/ppermute | solution.py:20
  28.5 5.0 %collective-permute-start.10 = (bf16[2,48,384]{2,1,0:T(8,128)(2,1)S(1)}, bf16[2,48,384]{2,1,0:T(8,128)(2,1)S(1)}, u32[]{:S(2)}, u32[]{:S(2)}) collective-permute-start(bf16[2,48,384]{2,1,0:T(8,128)(2,1)S(1)} %get-tuple-element.44), channel_id=1, source_target_pairs={{0,8},{4,12},{8,0},{12,4},{16,24},{20,28},{24,16},{28,20},{1,9},{5... | collective-permute-start | bytes 221192 | tf_op jit(solution)/shard_map/ppermute | solution.py:20
  29.1 7.0 %collective-permute-start.5 = (bf16[2,48,384]{2,1,0:T(8,128)(2,1)S(1)}, bf16[2,48,384]{2,1,0:T(8,128)(2,1)S(1)}, u32[]{:S(2)}, u32[]{:S(2)}) collective-permute-start(bf16[2,48,384]{2,1,0:T(8,128)(2,1)S(1)} %get-tuple-element.38), channel_id=1, source_target_pairs={{0,12},{4,8},{8,4},{12,0},{16,28},{20,24},{24,20},{28,16},{1,13},{... | collective-permute-start | bytes 221192 | tf_op jit(solution)/shard_map/ppermute | solution.py:20
  31.2 6.1 %collective-permute-start.6 = (bf16[2,48,384]{2,1,0:T(8,128)(2,1)S(1)}, bf16[2,48,384]{2,1,0:T(8,128)(2,1)S(1)}, u32[]{:S(2)}, u32[]{:S(2)}) collective-permute-start(bf16[2,48,384]{2,1,0:T(8,128)(2,1)S(1)} %get-tuple-element.39), channel_id=1, source_target_pairs={{0,4},{4,0},{8,12},{12,8},{16,20},{20,16},{24,28},{28,24},{1,5},{5... | collective-permute-start | bytes 221192 | tf_op jit(solution)/shard_map/ppermute | solution.py:20
  32.0 5.3 %collective-permute-start.7 = (bf16[2,48,384]{2,1,0:T(8,128)(2,1)S(1)}, bf16[2,48,384]{2,1,0:T(8,128)(2,1)S(1)}, u32[]{:S(2)}, u32[]{:S(2)}) collective-permute-start(bf16[2,48,384]{2,1,0:T(8,128)(2,1)S(1)} %get-tuple-element.40), channel_id=1, source_target_pairs={{0,8},{4,12},{8,0},{12,4},{16,24},{20,28},{24,16},{28,20},{1,9},{5... | collective-permute-start | bytes 221192 | tf_op jit(solution)/shard_map/ppermute | solution.py:20
  33.6 6.8 %collective-permute-start.11 = (bf16[2,48,384]{2,1,0:T(8,128)(2,1)S(1)}, bf16[2,48,384]{2,1,0:T(8,128)(2,1)S(1)}, u32[]{:S(2)}, u32[]{:S(2)}) collective-permute-start(bf16[2,48,384]{2,1,0:T(8,128)(2,1)S(1)} %add_convert_fusion.1), channel_id=1, source_target_pairs={{0,16},{4,20},{8,24},{12,28},{16,0},{20,4},{24,8},{28,12},{1,17},{... | collective-permute-start | bytes 221192 | tf_op jit(solution)/shard_map/ppermute | solution.py:20

commit v6 on v2

--- a/solution.py
+++ b/solution.py
@@ -137,11 +137,18 @@
         pieces = pieces[1:]
     else:
         acc[...] = jnp.zeros_like(acc)
-    if len(pieces) == 1:
-        psi = pieces[0]
-    else:
+    if kind == 0:
         for i, piece in enumerate(pieces):
             psi[i * local : (i + 1) * local] = piece[...]
+    else:
+        half = lax.rem(lax.axis_index(OPG), HALVES)
+        rows = sb // HALVES
+        for i in range(len(pieces) // 2):
+            whole, halves = pieces[2 * i : 2 * i + 2]
+            end = (i + 1) * local - 1
+            psi[i * local : end] = whole[...]
+            psi[end, pl.ds(pl.multiple_of(half * rows, 16), rows), :] = halves[0]
+            psi[end, pl.ds(pl.multiple_of((1 - half) * rows, 16), rows), :] = halves[1]
     run(kind, plan, coef, left, right, psi, acc, even, odd)
     if last:
         me_opg = lax.axis_index(OPG)
@@ -173,7 +180,7 @@
         in_specs=[SMEM] * 2 + [VMEM] * (2 + len(totals) + len(pieces)),
         out_specs=jax.tree.map(lambda _: VMEM, out_shape),
         scratch_shapes=[
-            pltpu.VMEM((len(pieces) * local, sb, sb), jnp.bfloat16),
+            pltpu.VMEM((len(pieces) // (2 if kind else 1) * local, sb, sb), jnp.bfloat16),
             pltpu.VMEM((sb, sb), jnp.bfloat16),
             pltpu.VMEM((sb, sb), jnp.bfloat16),
             *scratch,
@@ -234,14 +241,11 @@
     there = [flip(x, OPG, n_opg, 1) for x in here]
     done = onto(0, [], [psi, partner])
     here, there, whole, done = lax.optimization_barrier((here, there, whole, done))
-    twins = []
-    for one, other, rest in zip(here, there, whole):
-        upper, lower = jnp.where(half == 0, one, other), jnp.where(half == 0, other, one)
-        rows = jnp.concatenate([rest.reshape(-1, sb), upper, lower])
-        twins.append(rows.reshape(local, sb, sb))
-    others = to_other_core(twins)
-    done = onto(1, [done], twins)
-    sends = onto(2, [done], others)
+    whole_crossed = to_other_core(whole)
+    halves = [jnp.stack(two) for two in zip(here, there)]
+    halves_crossed = to_other_core(halves)
+    done = onto(1, [done], [x for two in zip(whole, halves) for x in two])
+    sends = onto(2, [done], [x for two in zip(whole_crossed, halves_crossed) for x in two])
     return jnp.swapaxes(scatter_sum(sends, n_opg), 0, 1).astype(jnp.bfloat16)
 
 

time: 41.6 us -> 36.8 us (0.88); the launches traced: 41.2 us -> 37 us
  local copies, waits for them, and re-layouts: 6.58 us -> 2.58 us
    unnamed x12 -> x14, local copies, waits for them, and re-layouts: 4.69 us -> 0.7 us
    ppermute x12 -> x13, starting transfers between devices: 15.8 us -> 15.4 us  [flip(): return lax.ppermute(x, axis, [(i, i ^ bit) for i in range(size)])]
    ppermute x12 -> x13, waiting for transfers between devices: 7.18 us -> 7.25 us  [flip(): return lax.ppermute(x, axis, [(i, i ^ bit) for i in range(size)])]
  transfers between devices with their start and end apart: 12 -> 13, of which waited for: 4 -> 4; matrix products, arithmetic and copies ran while one was open for 0% -> 1% of each run, Pallas kernels for 20% -> 24%
where the time goes in v6:
time: 36.8 us; the launch traced here: 37 us
  starting transfers between devices  15.4 us (42%)
  Pallas kernels  11.3 us (31%)
  waiting for transfers between devices  7.25 us (20%)
  local copies, waits for them, and re-layouts  2.58 us (7%)
    ppermute x13, starting transfers between devices, flip(): return lax.ppermute(x, axis, [(i, i ^ bit) for i in range(size)])  15.4 us
    pallas_call x3, Pallas kernels, products(): pl.pallas_call(functools.partial(products_kernel, kind, n_opg), out_shape...  9.69 us
    ppermute x13, waiting for transfers between devices, flip(): return lax.ppermute(x, axis, [(i, i ^ bit) for i in range(size)])  7.25 us
    pallas_call x1, Pallas kernels, on_device(): pl.pallas_call(functools.partial(plan_kernel, local), out_shape=jax.Shape...  1.6 us
    slice x1, local copies, waits for them, and re-layouts, on_device(): ours, rest, psi = lax.optimization_barrier((ours, psi[:local - 1], psi))  1.17 us
  transfers between devices with their start and end apart: 13, of which 4 were waited for; matrix products, arithmetic and copies ran while one was open for 1% of the time, Pallas kernels for 24%

profile of v6, /device:TPU:0, one launch (start us, length us, event | category | flops | bytes accessed | tf_op | source)
XLA Modules:
  0.0 37.0 jit_solution(1580298332135837842)
XLA Ops:
  0.0 1.2 %fusion.1 = (bf16[1,384,384]{2,1,0:T(8,128)(2,1)S(1)}, bf16[1,384,384]{2,1,0:T(8,128)(2,1)S(1)}) fusion(bf16[2,384,384]{2,1,0:T(8,128)(2,1)} %refs_0_), kind=kLoop, calls=%fused_computation.7 | loop fusion | bytes 1179648 | tf_op jit(solution)/shard_map/slice | solution.py:213
  1.2 3.0 %collective-permute-start = (bf16[192,384]{1,0:T(8,128)(2,1)S(1)}, bf16[192,384]{1,0:T(8,128)(2,1)S(1)}, u32[]{:S(2)}, u32[]{:S(2)}) collective-permute-start(bf16[192,384]{1,0:T(8,128)(2,1)S(1)} %dynamic-slice_bitcast_fusion), channel_id=1, source_target_pairs={{0,2},{1,3},{2,0},{3,1},{4,6},{5,7},{6,4},{7,5},{8,10},{9,11},{10,... | collective-permute-start | bytes 442376 | tf_op jit(solution)/shard_map/ppermute | solution.py:20
  4.2 0.1 collective-permute-start.2
  4.3 0.0 collective-permute-start.3
  4.3 0.7 %copy-done.2 = s32[8,2]{0,1:T(2,128)S(1)} copy-done((s32[8,2]{0,1:T(2,128)S(1)}, s32[8,2]{0,1:T(2,128)}, u32[]{:S(2)}) %copy-start.2) | copy-done | bytes 88
  5.0 1.6 %shard_map.64.plan = s32[3,49]{1,0:T(4,128)S(1)} custom-call(s32[2,8]{1,0:T(2,128)S(1)} %bitcast.11), custom_call_target="tpu_custom_call" | custom-call | flops 20000000000 | tf_op jit(solution)/shard_map/pallas_call | solution.py:222
  6.7 0.2 select_reduce_fusion.coef
  6.8 2.1 %collective-permute-done = bf16[192,384]{1,0:T(8,128)(2,1)S(1)} collective-permute-done((bf16[192,384]{1,0:T(8,128)(2,1)S(1)}, bf16[192,384]{1,0:T(8,128)(2,1)S(1)}, u32[]{:S(2)}, u32[]{:S(2)}) %collective-permute-start) | collective-permute-done | bytes 147488 | tf_op jit(solution)/shard_map/ppermute | solution.py:20
  8.9 2.0 %collective-permute-start.1 = (bf16[192,384]{1,0:T(8,128)(2,1)S(1)}, bf16[192,384]{1,0:T(8,128)(2,1)S(1)}, u32[]{:S(2)}, u32[]{:S(2)}) collective-permute-start(bf16[192,384]{1,0:T(8,128)(2,1)S(1)} %collective-permute-done), channel_id=1, source_target_pairs={{0,4},{4,0},{8,12},{12,8},{16,20},{20,16},{24,28},{28,24},{1,5},{5... | collective-permute-start | bytes 442376 | tf_op jit(solution)/shard_map/ppermute | solution.py:20
  10.9 0.0 collective-permute-done.3.refs_1_
  11.0 3.9 %shard_map.65.refs_0_ = f32[2,384,384]{2,1,0:T(8,128)S(1)} custom-call(s32[3,49]{1,0:T(4,128)S(1)} %shard_map.64.plan, f32[2,8]{1,0:T(2,128)S(1)} %select_reduce_fusion.coef, bf16[8,2,384,384]{3,2,1,0:T(8,128)(2,1)S(1)} %bitcast.10, bf16[8,2,384,384]{3,2,1,0:T(8,128)(2,1)S(1)} %copy-done, bf16[2,384,384]{2,1,0:T(8,128)(2,1)S(1)} %copy-done.1, ...), custom_call_target="tpu_custom_call" | custom-call | flops 384 | tf_op jit(solution)/shard_map/pallas_call | solution.py:177
  14.9 0.0 collective-permute-done.1
  14.9 0.0 collective-permute-done.2.refs_1_
  15.0 0.1 collective-permute-start.5
  15.0 0.5 %collective-permute-start.4 = (bf16[1,384,384]{2,1,0:T(8,128)(2,1)S(1)}, bf16[1,384,384]{2,1,0:T(8,128)(2,1)S(1)}, u32[]{:S(2)}, u32[]{:S(2)}) collective-permute-start(bf16[1,384,384]{2,1,0:T(8,128)(2,1)S(1)} %collective-permute-done.2.refs_1_), channel_id=1, source_target_pairs={{0,1},{1,0},{2,3},{3,2},{4,5},{5,4},{6,7},{7,6},{8,9},{9,8},{10,11... | collective-permute-start | bytes 884744 | tf_op jit(solution)/shard_map/ppermute | solution.py:20
  15.5 3.5 %shard_map.66.refs_0_ = f32[2,384,384]{2,1,0:T(8,128)S(1)} custom-call(s32[3,49]{1,0:T(4,128)S(1)} %shard_map.64.plan, f32[2,8]{1,0:T(2,128)S(1)} %select_reduce_fusion.coef, bf16[8,2,384,384]{3,2,1,0:T(8,128)(2,1)S(1)} %bitcast.10, bf16[8,2,384,384]{3,2,1,0:T(8,128)(2,1)S(1)} %copy-done, f32[2,384,384]{2,1,0:T(8,128)S(1)} %shard_map.65.refs_0_, ...), custom_call_target="tpu_custom_call" | custom-call | flops 384 | tf_op jit(solution)/shard_map/pallas_call | solution.py:177
  19.1 0.0 collective-permute-done.5.refs_2_
  19.1 2.3 %shard_map.67 = (f32[2,48,384]{2,1,0:T(8,128)S(1)}, bf16[2,48,384]{2,1,0:T(8,128)(2,1)S(1)}, bf16[2,48,384]{2,1,0:T(8,128)(2,1)S(1)}, bf16[2,48,384]{2,1,0:T(8,1...) custom-call(s32[3,49]{1,0:T(4,128)S(1)} %shard_map.64.plan, ...), custom_call_target="tpu_custom_call" | custom-call | flops 384 | tf_op jit(solution)/shard_map/pallas_call | solution.py:177
  21.4 3.1 %collective-permute-start.9 = (bf16[2,48,384]{2,1,0:T(8,128)(2,1)S(1)}, bf16[2,48,384]{2,1,0:T(8,128)(2,1)S(1)}, u32[]{:S(2)}, u32[]{:S(2)}) collective-permute-start(bf16[2,48,384]{2,1,0:T(8,128)(2,1)S(1)} %get-tuple-element.42), channel_id=1, source_target_pairs={{0,12},{4,8},{8,4},{12,0},{16,28},{20,24},{24,20},{28,16},{1,13},{... | collective-permute-start | bytes 221192 | tf_op jit(solution)/shard_map/ppermute | solution.py:20
  24.4 0.0 collective-permute-start.10
  24.5 0.6 %collective-permute-start.11 = (bf16[2,48,384]{2,1,0:T(8,128)(2,1)S(1)}, bf16[2,48,384]{2,1,0:T(8,128)(2,1)S(1)}, u32[]{:S(2)}, u32[]{:S(2)}) collective-permute-start(bf16[2,48,384]{2,1,0:T(8,128)(2,1)S(1)} %get-tuple-element.44), channel_id=1, source_target_pairs={{0,8},{4,12},{8,0},{12,4},{16,24},{20,28},{24,16},{28,20},{1,9},{5... | collective-permute-start | bytes 221192 | tf_op jit(solution)/shard_map/ppermute | solution.py:20
  25.1 2.8 %collective-permute-start.6 = (bf16[2,48,384]{2,1,0:T(8,128)(2,1)S(1)}, bf16[2,48,384]{2,1,0:T(8,128)(2,1)S(1)}, u32[]{:S(2)}, u32[]{:S(2)}) collective-permute-start(bf16[2,48,384]{2,1,0:T(8,128)(2,1)S(1)} %get-tuple-element.38), channel_id=1, source_target_pairs={{0,12},{4,8},{8,4},{12,0},{16,28},{20,24},{24,20},{28,16},{1,13},{... | collective-permute-start | bytes 221192 | tf_op jit(solution)/shard_map/ppermute | solution.py:20
  27.9 0.0 collective-permute-start.7
  28.0 0.0 collective-permute-done.9
  28.0 0.6 %collective-permute-start.8 = (bf16[2,48,384]{2,1,0:T(8,128)(2,1)S(1)}, bf16[2,48,384]{2,1,0:T(8,128)(2,1)S(1)}, u32[]{:S(2)}, u32[]{:S(2)}) collective-permute-start(bf16[2,48,384]{2,1,0:T(8,128)(2,1)S(1)} %get-tuple-element.40), channel_id=1, source_target_pairs={{0,8},{4,12},{8,0},{12,4},{16,24},{20,28},{24,16},{28,20},{1,9},{5... | collective-permute-start | bytes 221192 | tf_op jit(solution)/shard_map/ppermute | solution.py:20
  28.6 1.4 %collective-permute-done.10 = bf16[2,48,384]{2,1,0:T(8,128)(2,1)S(1)} collective-permute-done((bf16[2,48,384]{2,1,0:T(8,128)(2,1)S(1)}, bf16[2,48,384]{2,1,0:T(8,128)(2,1)S(1)}, u32[]{:S(2)}, u32[]{:S(2)}) %collective-permute-start.10) | collective-permute-done | bytes 73760 | tf_op jit(solution)/shard_map/ppermute | solution.py:20
  30.0 0.0 collective-permute-done.11
  30.0 2.5 %collective-permute-start.12 = (bf16[2,48,384]{2,1,0:T(8,128)(2,1)S(1)}, bf16[2,48,384]{2,1,0:T(8,128)(2,1)S(1)}, u32[]{:S(2)}, u32[]{:S(2)}) collective-permute-start(bf16[2,48,384]{2,1,0:T(8,128)(2,1)S(1)} %add_convert_fusion.1), channel_id=1, source_target_pairs={{0,16},{4,20},{8,24},{12,28},{16,0},{20,4},{24,8},{28,12},{1,17},{... | collective-permute-start | bytes 221192 | tf_op jit(solution)/shard_map/ppermute | solution.py:20
  32.6 0.1 collective-permute-done.7
  32.6 3.7 %collective-permute-done.12 = bf16[2,48,384]{2,1,0:T(8,128)(2,1)S(1)} collective-permute-done((bf16[2,48,384]{2,1,0:T(8,128)(2,1)S(1)}, bf16[2,48,384]{2,1,0:T(8,128)(2,1)S(1)}, u32[]{:S(2)}, u32[]{:S(2)}) %collective-permute-start.12) | collective-permute-done | bytes 73760 | tf_op jit(solution)/shard_map/ppermute | solution.py:20
  36.3 0.1 fusion
  36.3 0.7 %copy.8 = bf16[48,2,384]{2,1,0:T(2,128)(2,1)} copy(bf16[48,2,384]{2,0,1:T(8,128)(2,1)S(1)} %fusion) | data formatting | bytes 147456 | tf_op jit(solution)/shard_map/convert_element_type | solution.py:249
  (20 shorter events, 0.1 us)
Async XLA Ops:
  0.0 11.0 %slice-start = ((s8[4718592]{0:T(1024)(128)(4,1)}), s8[524288]{0:T(1024)(128)(4,1)S(1)}, s32[]{:S(2)}) async-start(s8[4718592]{0:T(1024)(128)(4,1)} %bitcast.9), calls=%async_computation | async-start | bytes 1048576
  1.2 7.7 %collective-permute-start = (bf16[192,384]{1,0:T(8,128)(2,1)S(1)}, bf16[192,384]{1,0:T(8,128)(2,1)S(1)}, u32[]{:S(2)}, u32[]{:S(2)}) collective-permute-start(bf16[192,384]{1,0:T(8,128)(2,1)S(1)} %dynamic-slice_bitcast_fusion), channel_id=1, source_target_pairs={{0,2},{1,3},{2,0},{3,1},{4,6},{5,7},{6,4},{7,5},{8,10},{9,11},{10,... | collective-permute-start | bytes 442376 | tf_op jit(solution)/shard_map/ppermute | solution.py:20
  4.2 10.7 %collective-permute-start.2 = (bf16[1,384,384]{2,1,0:T(8,128)(2,1)S(1)}, bf16[1,384,384]{2,1,0:T(8,128)(2,1)S(1)}, u32[]{:S(2)}, u32[]{:S(2)}) collective-permute-start(bf16[1,384,384]{2,1,0:T(8,128)(2,1)S(1)} %get-tuple-element.31), channel_id=1, source_target_pairs={{0,2},{1,3},{2,0},{3,1},{4,6},{5,7},{6,4},{7,5},{8,10},{9,11},{10,... | collective-permute-start | bytes 884744 | tf_op jit(solution)/shard_map/ppermute | solution.py:20
  4.3 6.6 %collective-permute-start.3 = (bf16[2,384,384]{2,1,0:T(8,128)(2,1)}, bf16[2,384,384]{2,1,0:T(8,128)(2,1)S(1)}, u32[]{:S(2)}, u32[]{:S(2)}) collective-permute-start(bf16[2,384,384]{2,1,0:T(8,128)(2,1)} %refs_0_), channel_id=1, source_target_pairs={{0,1},{1,0},{2,3},{3,2},{4,5},{5,4},{6,7},{7,6},{8,9},{9,8},{10,11... | collective-permute-start | bytes 1769480 | tf_op jit(solution)/shard_map/ppermute | solution.py:20
  4.3 0.7 %copy-start.2 = (s32[8,2]{0,1:T(2,128)S(1)}, s32[8,2]{0,1:T(2,128)}, u32[]{:S(2)}) copy-start(s32[8,2]{0,1:T(2,128)} %param.9) | copy-start | bytes 196
  5.0 1.6 %copy-start.3 = (s32[8,2]{0,1:T(2,128)S(1)}, s32[8,2]{0,1:T(2,128)}, u32[]{:S(2)}) copy-start(s32[8,2]{0,1:T(2,128)} %param.10) | copy-start | bytes 196
  5.0 1.6 %copy-start.4 = (f32[64]{0:T(128)S(1)}, f32[64]{0:T(128)}, u32[]{:S(2)}) copy-start(f32[64]{0:T(128)} %param.11) | copy-start | bytes 772
  5.0 5.9 %slice-start.1 = ((s8[4718592]{0:T(1024)(128)(4,1)}), s8[4194304]{0:T(1024)(128)(4,1)S(1)}, s32[]{:S(2)}) async-start(s8[4718592]{0:T(1024)(128)(4,1)} %bitcast.9), calls=%async_computation.1 | async-start | bytes 8388608
  5.0 6.0 %copy-start = (bf16[8,2,384,384]{3,2,1,0:T(8,128)(2,1)S(1)}, bf16[8,2,384,384]{3,2,1,0:T(8,128)(2,1)}, u32[]{:S(2)}) copy-start(bf16[8,2,384,384]{3,2,1,0:T(8,128)(2,1)} %right.5) | copy-start | bytes 14155780
  5.0 6.0 %copy-start.1 = (bf16[2,384,384]{2,1,0:T(8,128)(2,1)S(1)}, bf16[2,384,384]{2,1,0:T(8,128)(2,1)}, u32[]{:S(2)}) copy-start(bf16[2,384,384]{2,1,0:T(8,128)(2,1)} %refs_0_) | copy-start | bytes 1769476
  8.9 6.0 %collective-permute-start.1 = (bf16[192,384]{1,0:T(8,128)(2,1)S(1)}, bf16[192,384]{1,0:T(8,128)(2,1)S(1)}, u32[]{:S(2)}, u32[]{:S(2)}) collective-permute-start(bf16[192,384]{1,0:T(8,128)(2,1)S(1)} %collective-permute-done), channel_id=1, source_target_pairs={{0,4},{4,0},{8,12},{12,8},{16,20},{20,16},{24,28},{28,24},{1,5},{5... | collective-permute-start | bytes 442376 | tf_op jit(solution)/shard_map/ppermute | solution.py:20
  15.0 4.1 %collective-permute-start.5 = (bf16[2,192,384]{2,1,0:T(8,128)(2,1)S(1)}, bf16[2,192,384]{2,1,0:T(8,128)(2,1)S(1)}, u32[]{:S(2)}, u32[]{:S(2)}) collective-permute-start(bf16[2,192,384]{2,1,0:T(8,128)(2,1)S(1)} %pad_maximum_fusion.refs_2_), channel_id=1, source_target_pairs={{0,1},{1,0},{2,3},{3,2},{4,5},{5,4},{6,7},{7,6},{8,9},{9,8},{10,11... | collective-permute-start | bytes 884744 | tf_op jit(solution)/shard_map/ppermute | solution.py:20
  15.0 4.0 %collective-permute-start.4 = (bf16[1,384,384]{2,1,0:T(8,128)(2,1)S(1)}, bf16[1,384,384]{2,1,0:T(8,128)(2,1)S(1)}, u32[]{:S(2)}, u32[]{:S(2)}) collective-permute-start(bf16[1,384,384]{2,1,0:T(8,128)(2,1)S(1)} %collective-permute-done.2.refs_1_), channel_id=1, source_target_pairs={{0,1},{1,0},{2,3},{3,2},{4,5},{5,4},{6,7},{7,6},{8,9},{9,8},{10,11... | collective-permute-start | bytes 884744 | tf_op jit(solution)/shard_map/ppermute | solution.py:20
  21.4 6.6 %collective-permute-start.9 = (bf16[2,48,384]{2,1,0:T(8,128)(2,1)S(1)}, bf16[2,48,384]{2,1,0:T(8,128)(2,1)S(1)}, u32[]{:S(2)}, u32[]{:S(2)}) collective-permute-start(bf16[2,48,384]{2,1,0:T(8,128)(2,1)S(1)} %get-tuple-element.42), channel_id=1, source_target_pairs={{0,12},{4,8},{8,4},{12,0},{16,28},{20,24},{24,20},{28,16},{1,13},{... | collective-permute-start | bytes 221192 | tf_op jit(solution)/shard_map/ppermute | solution.py:20
  24.4 5.5 %collective-permute-start.10 = (bf16[2,48,384]{2,1,0:T(8,128)(2,1)S(1)}, bf16[2,48,384]{2,1,0:T(8,128)(2,1)S(1)}, u32[]{:S(2)}, u32[]{:S(2)}) collective-permute-start(bf16[2,48,384]{2,1,0:T(8,128)(2,1)S(1)} %get-tuple-element.43), channel_id=1, source_target_pairs={{0,4},{4,0},{8,12},{12,8},{16,20},{20,16},{24,28},{28,24},{1,5},{5... | collective-permute-start | bytes 221192 | tf_op jit(solution)/shard_map/ppermute | solution.py:20
  24.5 5.5 %collective-permute-start.11 = (bf16[2,48,384]{2,1,0:T(8,128)(2,1)S(1)}, bf16[2,48,384]{2,1,0:T(8,128)(2,1)S(1)}, u32[]{:S(2)}, u32[]{:S(2)}) collective-permute-start(bf16[2,48,384]{2,1,0:T(8,128)(2,1)S(1)} %get-tuple-element.44), channel_id=1, source_target_pairs={{0,8},{4,12},{8,0},{12,4},{16,24},{20,28},{24,16},{28,20},{1,9},{5... | collective-permute-start | bytes 221192 | tf_op jit(solution)/shard_map/ppermute | solution.py:20
  25.1 7.5 %collective-permute-start.6 = (bf16[2,48,384]{2,1,0:T(8,128)(2,1)S(1)}, bf16[2,48,384]{2,1,0:T(8,128)(2,1)S(1)}, u32[]{:S(2)}, u32[]{:S(2)}) collective-permute-start(bf16[2,48,384]{2,1,0:T(8,128)(2,1)S(1)} %get-tuple-element.38), channel_id=1, source_target_pairs={{0,12},{4,8},{8,4},{12,0},{16,28},{20,24},{24,20},{28,16},{1,13},{... | collective-permute-start | bytes 221192 | tf_op jit(solution)/shard_map/ppermute | solution.py:20
  27.9 4.7 %collective-permute-start.7 = (bf16[2,48,384]{2,1,0:T(8,128)(2,1)S(1)}, bf16[2,48,384]{2,1,0:T(8,128)(2,1)S(1)}, u32[]{:S(2)}, u32[]{:S(2)}) collective-permute-start(bf16[2,48,384]{2,1,0:T(8,128)(2,1)S(1)} %get-tuple-element.39), channel_id=1, source_target_pairs={{0,4},{4,0},{8,12},{12,8},{16,20},{20,16},{24,28},{28,24},{1,5},{5... | collective-permute-start | bytes 221192 | tf_op jit(solution)/shard_map/ppermute | solution.py:20
  28.0 4.7 %collective-permute-start.8 = (bf16[2,48,384]{2,1,0:T(8,128)(2,1)S(1)}, bf16[2,48,384]{2,1,0:T(8,128)(2,1)S(1)}, u32[]{:S(2)}, u32[]{:S(2)}) collective-permute-start(bf16[2,48,384]{2,1,0:T(8,128)(2,1)S(1)} %get-tuple-element.40), channel_id=1, source_target_pairs={{0,8},{4,12},{8,0},{12,4},{16,24},{20,28},{24,16},{28,20},{1,9},{5... | collective-permute-start | bytes 221192 | tf_op jit(solution)/shard_map/ppermute | solution.py:20
  30.0 6.3 %collective-permute-start.12 = (bf16[2,48,384]{2,1,0:T(8,128)(2,1)S(1)}, bf16[2,48,384]{2,1,0:T(8,128)(2,1)S(1)}, u32[]{:S(2)}, u32[]{:S(2)}) collective-permute-start(bf16[2,48,384]{2,1,0:T(8,128)(2,1)S(1)} %add_convert_fusion.1), channel_id=1, source_target_pairs={{0,16},{4,20},{8,24},{12,28},{16,0},{20,4},{24,8},{28,12},{1,17},{... | collective-permute-start | bytes 221192 | tf_op jit(solution)/shard_map/ppermute | solution.py:20

commit v7 on v6

--- a/solution.py
+++ b/solution.py
@@ -13,7 +13,7 @@
 HALVES = 2
 NEAR = 2
 KERNEL_VMEM = 24_000_000
-PLAN_FLOPS = 20_000_000_000
+PLAN_FLOPS = 40_000_000_000
 
 
 def flip(x, axis, size, bit):

time: 36.8 us -> 37.3 us (1.014); the launches traced: 37 us -> 37 us
  waiting for transfers between devices: 7.25 us -> 8.42 us
  starting transfers between devices: 15.4 us -> 14.3 us
    ppermute x13, waiting for transfers between devices: 7.25 us -> 8.42 us  [flip(): return lax.ppermute(x, axis, [(i, i ^ bit) for i in range(size)])]
    ppermute x13, starting transfers between devices: 15.4 us -> 14.3 us  [flip(): return lax.ppermute(x, axis, [(i, i ^ bit) for i in range(size)])]
  transfers between devices with their start and end apart: 13 -> 13, of which waited for: 4 -> 7; matrix products, arithmetic and copies ran while one was open for 1% -> 1% of each run, Pallas kernels for 24% -> 16%
where the time goes in v7:
time: 37.3 us; the launch traced here: 37 us
  starting transfers between devices  14.3 us (38%)
  Pallas kernels  11.2 us (30%)
  waiting for transfers between devices  8.42 us (23%)
  local copies, waits for them, and re-layouts  2.58 us (7%)
    ppermute x13, starting transfers between devices, flip(): return lax.ppermute(x, axis, [(i, i ^ bit) for i in range(size)])  14.3 us
    pallas_call x3, Pallas kernels, products(): pl.pallas_call(functools.partial(products_kernel, kind, n_opg), out_shape...  9.63 us
    ppermute x13, waiting for transfers between devices, flip(): return lax.ppermute(x, axis, [(i, i ^ bit) for i in range(size)])  8.42 us
    pallas_call x1, Pallas kernels, on_device(): pl.pallas_call(functools.partial(plan_kernel, local), out_shape=jax.Shape...  1.6 us
    slice x1, local copies, waits for them, and re-layouts, on_device(): ours, rest, psi = lax.optimization_barrier((ours, psi[:local - 1], psi))  1.17 us
  transfers between devices with their start and end apart: 13, of which 7 were waited for; matrix products, arithmetic and copies ran while one was open for 1% of the time, Pallas kernels for 16%

profile of v7, /device:TPU:0, one launch (start us, length us, event | category | flops | bytes accessed | tf_op | source)
XLA Modules:
  0.0 37.0 jit_solution(8925209692061945443)
XLA Ops:
  0.0 1.2 %fusion.1 = (bf16[1,384,384]{2,1,0:T(8,128)(2,1)S(1)}, bf16[1,384,384]{2,1,0:T(8,128)(2,1)S(1)}) fusion(bf16[2,384,384]{2,1,0:T(8,128)(2,1)} %refs_0_), kind=kLoop, calls=%fused_computation.7 | loop fusion | bytes 1179648 | tf_op jit(solution)/shard_map/slice | solution.py:213
  1.2 3.0 %collective-permute-start = (bf16[192,384]{1,0:T(8,128)(2,1)S(1)}, bf16[192,384]{1,0:T(8,128)(2,1)S(1)}, u32[]{:S(2)}, u32[]{:S(2)}) collective-permute-start(bf16[192,384]{1,0:T(8,128)(2,1)S(1)} %dynamic-slice_bitcast_fusion), channel_id=1, source_target_pairs={{0,2},{1,3},{2,0},{3,1},{4,6},{5,7},{6,4},{7,5},{8,10},{9,11},{10,... | collective-permute-start | bytes 442376 | tf_op jit(solution)/shard_map/ppermute | solution.py:20
  4.2 0.1 collective-permute-start.2
  4.3 0.7 %copy-done.2 = s32[8,2]{0,1:T(2,128)S(1)} copy-done((s32[8,2]{0,1:T(2,128)S(1)}, s32[8,2]{0,1:T(2,128)}, u32[]{:S(2)}) %copy-start.2) | copy-done | bytes 88
  5.0 1.6 %shard_map.64.plan = s32[3,49]{1,0:T(4,128)S(1)} custom-call(s32[2,8]{1,0:T(2,128)S(1)} %bitcast.11), custom_call_target="tpu_custom_call" | custom-call | flops 40000000000 | tf_op jit(solution)/shard_map/pallas_call | solution.py:222
  6.7 0.2 select_reduce_fusion.coef
  6.8 2.1 %collective-permute-done = bf16[192,384]{1,0:T(8,128)(2,1)S(1)} collective-permute-done((bf16[192,384]{1,0:T(8,128)(2,1)S(1)}, bf16[192,384]{1,0:T(8,128)(2,1)S(1)}, u32[]{:S(2)}, u32[]{:S(2)}) %collective-permute-start) | collective-permute-done | bytes 147488 | tf_op jit(solution)/shard_map/ppermute | solution.py:20
  8.9 2.0 %collective-permute-start.1 = (bf16[192,384]{1,0:T(8,128)(2,1)S(1)}, bf16[192,384]{1,0:T(8,128)(2,1)S(1)}, u32[]{:S(2)}, u32[]{:S(2)}) collective-permute-start(bf16[192,384]{1,0:T(8,128)(2,1)S(1)} %collective-permute-done), channel_id=1, source_target_pairs={{0,4},{4,0},{8,12},{12,8},{16,20},{20,16},{24,28},{28,24},{1,5},{5... | collective-permute-start | bytes 442376 | tf_op jit(solution)/shard_map/ppermute | solution.py:20
  11.0 2.3 %shard_map.65.refs_0_ = f32[2,384,384]{2,1,0:T(8,128)S(1)} custom-call(s32[3,49]{1,0:T(4,128)S(1)} %shard_map.64.plan, f32[2,8]{1,0:T(2,128)S(1)} %select_reduce_fusion.coef, bf16[8,2,384,384]{3,2,1,0:T(8,128)(2,1)S(1)} %bitcast.10, bf16[8,2,384,384]{3,2,1,0:T(8,128)(2,1)S(1)} %copy-done, bf16[2,384,384]{2,1,0:T(8,128)(2,1)S(1)} %copy-done.1, ...), custom_call_target="tpu_custom_call" | custom-call | flops 384 | tf_op jit(solution)/shard_map/pallas_call | solution.py:177
  13.3 0.8 %collective-permute-done.1 = bf16[192,384]{1,0:T(8,128)(2,1)S(1)} collective-permute-done((bf16[192,384]{1,0:T(8,128)(2,1)S(1)}, bf16[192,384]{1,0:T(8,128)(2,1)S(1)}, u32[]{:S(2)}, u32[]{:S(2)}) %collective-permute-start.1) | collective-permute-done | bytes 147488 | tf_op jit(solution)/shard_map/ppermute | solution.py:20
  14.1 0.3 collective-permute-done.2.refs_1_
  14.4 0.1 collective-permute-start.5
  14.5 0.5 %collective-permute-start.4 = (bf16[1,384,384]{2,1,0:T(8,128)(2,1)S(1)}, bf16[1,384,384]{2,1,0:T(8,128)(2,1)S(1)}, u32[]{:S(2)}, u32[]{:S(2)}) collective-permute-start(bf16[1,384,384]{2,1,0:T(8,128)(2,1)S(1)} %collective-permute-done.2.refs_1_), channel_id=1, source_target_pairs={{0,1},{1,0},{2,3},{3,2},{4,5},{5,4},{6,7},{7,6},{8,9},{9,8},{10,11... | collective-permute-start | bytes 884744 | tf_op jit(solution)/shard_map/ppermute | solution.py:20
  15.0 2.2 %shard_map.66.refs_0_ = f32[2,384,384]{2,1,0:T(8,128)S(1)} custom-call(s32[3,49]{1,0:T(4,128)S(1)} %shard_map.64.plan, f32[2,8]{1,0:T(2,128)S(1)} %select_reduce_fusion.coef, bf16[8,2,384,384]{3,2,1,0:T(8,128)(2,1)S(1)} %bitcast.10, bf16[8,2,384,384]{3,2,1,0:T(8,128)(2,1)S(1)} %copy-done, f32[2,384,384]{2,1,0:T(8,128)S(1)} %shard_map.65.refs_0_, ...), custom_call_target="tpu_custom_call" | custom-call | flops 384 | tf_op jit(solution)/shard_map/pallas_call | solution.py:177
  17.3 0.0 collective-permute-done.5.refs_2_
  17.3 0.0 collective-permute-done.4.refs_1_
  17.3 5.1 %shard_map.67 = (f32[2,48,384]{2,1,0:T(8,128)S(1)}, bf16[2,48,384]{2,1,0:T(8,128)(2,1)S(1)}, bf16[2,48,384]{2,1,0:T(8,128)(2,1)S(1)}, bf16[2,48,384]{2,1,0:T(8,1...) custom-call(s32[3,49]{1,0:T(4,128)S(1)} %shard_map.64.plan, ...), custom_call_target="tpu_custom_call" | custom-call | flops 384 | tf_op jit(solution)/shard_map/pallas_call | solution.py:177
  22.4 0.5 %collective-permute-start.9 = (bf16[2,48,384]{2,1,0:T(8,128)(2,1)S(1)}, bf16[2,48,384]{2,1,0:T(8,128)(2,1)S(1)}, u32[]{:S(2)}, u32[]{:S(2)}) collective-permute-start(bf16[2,48,384]{2,1,0:T(8,128)(2,1)S(1)} %get-tuple-element.42), channel_id=1, source_target_pairs={{0,12},{4,8},{8,4},{12,0},{16,28},{20,24},{24,20},{28,16},{1,13},{... | collective-permute-start | bytes 221192 | tf_op jit(solution)/shard_map/ppermute | solution.py:20
  23.0 2.1 %collective-permute-start.10 = (bf16[2,48,384]{2,1,0:T(8,128)(2,1)S(1)}, bf16[2,48,384]{2,1,0:T(8,128)(2,1)S(1)}, u32[]{:S(2)}, u32[]{:S(2)}) collective-permute-start(bf16[2,48,384]{2,1,0:T(8,128)(2,1)S(1)} %get-tuple-element.43), channel_id=1, source_target_pairs={{0,4},{4,0},{8,12},{12,8},{16,20},{20,16},{24,28},{28,24},{1,5},{5... | collective-permute-start | bytes 221192 | tf_op jit(solution)/shard_map/ppermute | solution.py:20
  25.1 0.9 %collective-permute-start.11 = (bf16[2,48,384]{2,1,0:T(8,128)(2,1)S(1)}, bf16[2,48,384]{2,1,0:T(8,128)(2,1)S(1)}, u32[]{:S(2)}, u32[]{:S(2)}) collective-permute-start(bf16[2,48,384]{2,1,0:T(8,128)(2,1)S(1)} %get-tuple-element.44), channel_id=1, source_target_pairs={{0,8},{4,12},{8,0},{12,4},{16,24},{20,28},{24,16},{28,20},{1,9},{5... | collective-permute-start | bytes 221192 | tf_op jit(solution)/shard_map/ppermute | solution.py:20
  26.0 0.6 %collective-permute-start.6 = (bf16[2,48,384]{2,1,0:T(8,128)(2,1)S(1)}, bf16[2,48,384]{2,1,0:T(8,128)(2,1)S(1)}, u32[]{:S(2)}, u32[]{:S(2)}) collective-permute-start(bf16[2,48,384]{2,1,0:T(8,128)(2,1)S(1)} %get-tuple-element.38), channel_id=1, source_target_pairs={{0,12},{4,8},{8,4},{12,0},{16,28},{20,24},{24,20},{28,16},{1,13},{... | collective-permute-start | bytes 221192 | tf_op jit(solution)/shard_map/ppermute | solution.py:20
  26.6 2.0 %collective-permute-start.7 = (bf16[2,48,384]{2,1,0:T(8,128)(2,1)S(1)}, bf16[2,48,384]{2,1,0:T(8,128)(2,1)S(1)}, u32[]{:S(2)}, u32[]{:S(2)}) collective-permute-start(bf16[2,48,384]{2,1,0:T(8,128)(2,1)S(1)} %get-tuple-element.39), channel_id=1, source_target_pairs={{0,4},{4,0},{8,12},{12,8},{16,20},{20,16},{24,28},{28,24},{1,5},{5... | collective-permute-start | bytes 221192 | tf_op jit(solution)/shard_map/ppermute | solution.py:20
  28.6 0.0 collective-permute-done.9
  28.6 0.9 %collective-permute-start.8 = (bf16[2,48,384]{2,1,0:T(8,128)(2,1)S(1)}, bf16[2,48,384]{2,1,0:T(8,128)(2,1)S(1)}, u32[]{:S(2)}, u32[]{:S(2)}) collective-permute-start(bf16[2,48,384]{2,1,0:T(8,128)(2,1)S(1)} %get-tuple-element.40), channel_id=1, source_target_pairs={{0,8},{4,12},{8,0},{12,4},{16,24},{20,28},{24,16},{28,20},{1,9},{5... | collective-permute-start | bytes 221192 | tf_op jit(solution)/shard_map/ppermute | solution.py:20
  29.5 0.7 %collective-permute-done.11 = bf16[2,48,384]{2,1,0:T(8,128)(2,1)S(1)} collective-permute-done((bf16[2,48,384]{2,1,0:T(8,128)(2,1)S(1)}, bf16[2,48,384]{2,1,0:T(8,128)(2,1)S(1)}, u32[]{:S(2)}, u32[]{:S(2)}) %collective-permute-start.11) | collective-permute-done | bytes 73760 | tf_op jit(solution)/shard_map/ppermute | solution.py:20
  30.2 1.5 %collective-permute-start.12 = (bf16[2,48,384]{2,1,0:T(8,128)(2,1)S(1)}, bf16[2,48,384]{2,1,0:T(8,128)(2,1)S(1)}, u32[]{:S(2)}, u32[]{:S(2)}) collective-permute-start(bf16[2,48,384]{2,1,0:T(8,128)(2,1)S(1)} %add_convert_fusion.1), channel_id=1, source_target_pairs={{0,16},{4,20},{8,24},{12,28},{16,0},{20,4},{24,8},{28,12},{1,17},{... | collective-permute-start | bytes 221192 | tf_op jit(solution)/shard_map/ppermute | solution.py:20
  31.8 0.0 collective-permute-done.6
  31.8 1.1 %collective-permute-done.7 = bf16[2,48,384]{2,1,0:T(8,128)(2,1)S(1)} collective-permute-done((bf16[2,48,384]{2,1,0:T(8,128)(2,1)S(1)}, bf16[2,48,384]{2,1,0:T(8,128)(2,1)S(1)}, u32[]{:S(2)}, u32[]{:S(2)}) %collective-permute-start.7) | collective-permute-done | bytes 73760 | tf_op jit(solution)/shard_map/ppermute | solution.py:20
  32.8 0.1 collective-permute-done.8
  33.0 3.3 %collective-permute-done.12 = bf16[2,48,384]{2,1,0:T(8,128)(2,1)S(1)} collective-permute-done((bf16[2,48,384]{2,1,0:T(8,128)(2,1)S(1)}, bf16[2,48,384]{2,1,0:T(8,128)(2,1)S(1)}, u32[]{:S(2)}, u32[]{:S(2)}) %collective-permute-start.12) | collective-permute-done | bytes 73760 | tf_op jit(solution)/shard_map/ppermute | solution.py:20
  36.2 0.1 fusion
  36.3 0.7 %copy.8 = bf16[48,2,384]{2,1,0:T(2,128)(2,1)} copy(bf16[48,2,384]{2,0,1:T(8,128)(2,1)S(1)} %fusion) | data formatting | bytes 147456 | tf_op jit(solution)/shard_map/convert_element_type | solution.py:249
  (20 shorter events, 0.1 us)
Async XLA Ops:
  0.0 11.0 %slice-start = ((s8[4718592]{0:T(1024)(128)(4,1)}), s8[524288]{0:T(1024)(128)(4,1)S(1)}, s32[]{:S(2)}) async-start(s8[4718592]{0:T(1024)(128)(4,1)} %bitcast.9), calls=%async_computation | async-start | bytes 1048576
  1.2 7.7 %collective-permute-start = (bf16[192,384]{1,0:T(8,128)(2,1)S(1)}, bf16[192,384]{1,0:T(8,128)(2,1)S(1)}, u32[]{:S(2)}, u32[]{:S(2)}) collective-permute-start(bf16[192,384]{1,0:T(8,128)(2,1)S(1)} %dynamic-slice_bitcast_fusion), channel_id=1, source_target_pairs={{0,2},{1,3},{2,0},{3,1},{4,6},{5,7},{6,4},{7,5},{8,10},{9,11},{10,... | collective-permute-start | bytes 442376 | tf_op jit(solution)/shard_map/ppermute | solution.py:20
  4.2 10.2 %collective-permute-start.2 = (bf16[1,384,384]{2,1,0:T(8,128)(2,1)S(1)}, bf16[1,384,384]{2,1,0:T(8,128)(2,1)S(1)}, u32[]{:S(2)}, u32[]{:S(2)}) collective-permute-start(bf16[1,384,384]{2,1,0:T(8,128)(2,1)S(1)} %get-tuple-element.31), channel_id=1, source_target_pairs={{0,2},{1,3},{2,0},{3,1},{4,6},{5,7},{6,4},{7,5},{8,10},{9,11},{10,... | collective-permute-start | bytes 884744 | tf_op jit(solution)/shard_map/ppermute | solution.py:20
  4.3 6.6 %collective-permute-start.3 = (bf16[2,384,384]{2,1,0:T(8,128)(2,1)}, bf16[2,384,384]{2,1,0:T(8,128)(2,1)S(1)}, u32[]{:S(2)}, u32[]{:S(2)}) collective-permute-start(bf16[2,384,384]{2,1,0:T(8,128)(2,1)} %refs_0_), channel_id=1, source_target_pairs={{0,1},{1,0},{2,3},{3,2},{4,5},{5,4},{6,7},{7,6},{8,9},{9,8},{10,11... | collective-permute-start | bytes 1769480 | tf_op jit(solution)/shard_map/ppermute | solution.py:20
  4.3 0.7 %copy-start.2 = (s32[8,2]{0,1:T(2,128)S(1)}, s32[8,2]{0,1:T(2,128)}, u32[]{:S(2)}) copy-start(s32[8,2]{0,1:T(2,128)} %param.9) | copy-start | bytes 196
  5.0 1.6 %copy-start.3 = (s32[8,2]{0,1:T(2,128)S(1)}, s32[8,2]{0,1:T(2,128)}, u32[]{:S(2)}) copy-start(s32[8,2]{0,1:T(2,128)} %param.10) | copy-start | bytes 196
  5.0 1.6 %copy-start.4 = (f32[64]{0:T(128)S(1)}, f32[64]{0:T(128)}, u32[]{:S(2)}) copy-start(f32[64]{0:T(128)} %param.11) | copy-start | bytes 772
  5.0 5.9 %slice-start.1 = ((s8[4718592]{0:T(1024)(128)(4,1)}), s8[4194304]{0:T(1024)(128)(4,1)S(1)}, s32[]{:S(2)}) async-start(s8[4718592]{0:T(1024)(128)(4,1)} %bitcast.9), calls=%async_computation.1 | async-start | bytes 8388608
  5.0 6.0 %copy-start = (bf16[8,2,384,384]{3,2,1,0:T(8,128)(2,1)S(1)}, bf16[8,2,384,384]{3,2,1,0:T(8,128)(2,1)}, u32[]{:S(2)}) copy-start(bf16[8,2,384,384]{3,2,1,0:T(8,128)(2,1)} %right.5) | copy-start | bytes 14155780
  5.0 6.0 %copy-start.1 = (bf16[2,384,384]{2,1,0:T(8,128)(2,1)S(1)}, bf16[2,384,384]{2,1,0:T(8,128)(2,1)}, u32[]{:S(2)}) copy-start(bf16[2,384,384]{2,1,0:T(8,128)(2,1)} %refs_0_) | copy-start | bytes 1769476
  8.9 5.2 %collective-permute-start.1 = (bf16[192,384]{1,0:T(8,128)(2,1)S(1)}, bf16[192,384]{1,0:T(8,128)(2,1)S(1)}, u32[]{:S(2)}, u32[]{:S(2)}) collective-permute-start(bf16[192,384]{1,0:T(8,128)(2,1)S(1)} %collective-permute-done), channel_id=1, source_target_pairs={{0,4},{4,0},{8,12},{12,8},{16,20},{20,16},{24,28},{28,24},{1,5},{5... | collective-permute-start | bytes 442376 | tf_op jit(solution)/shard_map/ppermute | solution.py:20
  14.4 2.8 %collective-permute-start.5 = (bf16[2,192,384]{2,1,0:T(8,128)(2,1)S(1)}, bf16[2,192,384]{2,1,0:T(8,128)(2,1)S(1)}, u32[]{:S(2)}, u32[]{:S(2)}) collective-permute-start(bf16[2,192,384]{2,1,0:T(8,128)(2,1)S(1)} %pad_maximum_fusion.refs_2_), channel_id=1, source_target_pairs={{0,1},{1,0},{2,3},{3,2},{4,5},{5,4},{6,7},{7,6},{8,9},{9,8},{10,11... | collective-permute-start | bytes 884744 | tf_op jit(solution)/shard_map/ppermute | solution.py:20
  14.5 2.7 %collective-permute-start.4 = (bf16[1,384,384]{2,1,0:T(8,128)(2,1)S(1)}, bf16[1,384,384]{2,1,0:T(8,128)(2,1)S(1)}, u32[]{:S(2)}, u32[]{:S(2)}) collective-permute-start(bf16[1,384,384]{2,1,0:T(8,128)(2,1)S(1)} %collective-permute-done.2.refs_1_), channel_id=1, source_target_pairs={{0,1},{1,0},{2,3},{3,2},{4,5},{5,4},{6,7},{7,6},{8,9},{9,8},{10,11... | collective-permute-start | bytes 884744 | tf_op jit(solution)/shard_map/ppermute | solution.py:20
  22.4 6.2 %collective-permute-start.9 = (bf16[2,48,384]{2,1,0:T(8,128)(2,1)S(1)}, bf16[2,48,384]{2,1,0:T(8,128)(2,1)S(1)}, u32[]{:S(2)}, u32[]{:S(2)}) collective-permute-start(bf16[2,48,384]{2,1,0:T(8,128)(2,1)S(1)} %get-tuple-element.42), channel_id=1, source_target_pairs={{0,12},{4,8},{8,4},{12,0},{16,28},{20,24},{24,20},{28,16},{1,13},{... | collective-permute-start | bytes 221192 | tf_op jit(solution)/shard_map/ppermute | solution.py:20
  23.0 6.5 %collective-permute-start.10 = (bf16[2,48,384]{2,1,0:T(8,128)(2,1)S(1)}, bf16[2,48,384]{2,1,0:T(8,128)(2,1)S(1)}, u32[]{:S(2)}, u32[]{:S(2)}) collective-permute-start(bf16[2,48,384]{2,1,0:T(8,128)(2,1)S(1)} %get-tuple-element.43), channel_id=1, source_target_pairs={{0,4},{4,0},{8,12},{12,8},{16,20},{20,16},{24,28},{28,24},{1,5},{5... | collective-permute-start | bytes 221192 | tf_op jit(solution)/shard_map/ppermute | solution.py:20
  25.1 5.1 %collective-permute-start.11 = (bf16[2,48,384]{2,1,0:T(8,128)(2,1)S(1)}, bf16[2,48,384]{2,1,0:T(8,128)(2,1)S(1)}, u32[]{:S(2)}, u32[]{:S(2)}) collective-permute-start(bf16[2,48,384]{2,1,0:T(8,128)(2,1)S(1)} %get-tuple-element.44), channel_id=1, source_target_pairs={{0,8},{4,12},{8,0},{12,4},{16,24},{20,28},{24,16},{28,20},{1,9},{5... | collective-permute-start | bytes 221192 | tf_op jit(solution)/shard_map/ppermute | solution.py:20
  26.0 5.8 %collective-permute-start.6 = (bf16[2,48,384]{2,1,0:T(8,128)(2,1)S(1)}, bf16[2,48,384]{2,1,0:T(8,128)(2,1)S(1)}, u32[]{:S(2)}, u32[]{:S(2)}) collective-permute-start(bf16[2,48,384]{2,1,0:T(8,128)(2,1)S(1)} %get-tuple-element.38), channel_id=1, source_target_pairs={{0,12},{4,8},{8,4},{12,0},{16,28},{20,24},{24,20},{28,16},{1,13},{... | collective-permute-start | bytes 221192 | tf_op jit(solution)/shard_map/ppermute | solution.py:20
  26.6 6.3 %collective-permute-start.7 = (bf16[2,48,384]{2,1,0:T(8,128)(2,1)S(1)}, bf16[2,48,384]{2,1,0:T(8,128)(2,1)S(1)}, u32[]{:S(2)}, u32[]{:S(2)}) collective-permute-start(bf16[2,48,384]{2,1,0:T(8,128)(2,1)S(1)} %get-tuple-element.39), channel_id=1, source_target_pairs={{0,4},{4,0},{8,12},{12,8},{16,20},{20,16},{24,28},{28,24},{1,5},{5... | collective-permute-start | bytes 221192 | tf_op jit(solution)/shard_map/ppermute | solution.py:20
  28.6 4.4 %collective-permute-start.8 = (bf16[2,48,384]{2,1,0:T(8,128)(2,1)S(1)}, bf16[2,48,384]{2,1,0:T(8,128)(2,1)S(1)}, u32[]{:S(2)}, u32[]{:S(2)}) collective-permute-start(bf16[2,48,384]{2,1,0:T(8,128)(2,1)S(1)} %get-tuple-element.40), channel_id=1, source_target_pairs={{0,8},{4,12},{8,0},{12,4},{16,24},{20,28},{24,16},{28,20},{1,9},{5... | collective-permute-start | bytes 221192 | tf_op jit(solution)/shard_map/ppermute | solution.py:20
  30.2 6.0 %collective-permute-start.12 = (bf16[2,48,384]{2,1,0:T(8,128)(2,1)S(1)}, bf16[2,48,384]{2,1,0:T(8,128)(2,1)S(1)}, u32[]{:S(2)}, u32[]{:S(2)}) collective-permute-start(bf16[2,48,384]{2,1,0:T(8,128)(2,1)S(1)} %add_convert_fusion.1), channel_id=1, source_target_pairs={{0,16},{4,20},{8,24},{12,28},{16,0},{20,4},{24,8},{28,12},{1,17},{... | collective-permute-start | bytes 221192 | tf_op jit(solution)/shard_map/ppermute | solution.py:20

commit v8 on v6

--- a/solution.py
+++ b/solution.py
@@ -195,7 +195,7 @@
     for high in reversed(range(n_opg // PARTS)):
         at = high * PARTS
         total = sends[at]
-        for low in (3, 1, 2):
+        for low in (3, 1, 2) if high else (1, 3, 2):
             total = total + flip(sends[at + low], OPG, n_opg, low).astype(jnp.float32)
         if high:
             total = flip(total.astype(jnp.bfloat16), OPG, n_opg, at).astype(jnp.float32)

time: 36.8 us -> 36.4 us (0.989); the launches traced: 37 us -> 36.1 us
  waiting for transfers between devices: 7.25 us -> 4.95 us
  starting transfers between devices: 15.4 us -> 16.7 us
    ppermute x13, waiting for transfers between devices: 7.25 us -> 4.95 us  [flip(): return lax.ppermute(x, axis, [(i, i ^ bit) for i in range(size)])]
    ppermute x13, starting transfers between devices: 15.4 us -> 16.7 us  [flip(): return lax.ppermute(x, axis, [(i, i ^ bit) for i in range(size)])]
  transfers between devices with their start and end apart: 13 -> 13, of which waited for: 4 -> 3; matrix products, arithmetic and copies ran while one was open for 1% -> 1% of each run, Pallas kernels for 24% -> 26%
where the time goes in v8:
time: 36.4 us; the launch traced here: 36.1 us
  starting transfers between devices  16.7 us (46%)
  Pallas kernels  11.4 us (31%)
  waiting for transfers between devices  4.95 us (14%)
  local copies, waits for them, and re-layouts  2.58 us (7%)
    ppermute x13, starting transfers between devices, flip(): return lax.ppermute(x, axis, [(i, i ^ bit) for i in range(size)])  16.7 us
    pallas_call x3, Pallas kernels, products(): pl.pallas_call(functools.partial(products_kernel, kind, n_opg), out_shape...  9.79 us
    ppermute x13, waiting for transfers between devices, flip(): return lax.ppermute(x, axis, [(i, i ^ bit) for i in range(size)])  4.95 us
    pallas_call x1, Pallas kernels, on_device(): pl.pallas_call(functools.partial(plan_kernel, local), out_shape=jax.Shape...  1.6 us
    slice x1, local copies, waits for them, and re-layouts, on_device(): ours, rest, psi = lax.optimization_barrier((ours, psi[:local - 1], psi))  1.17 us
  transfers between devices with their start and end apart: 13, of which 3 were waited for; matrix products, arithmetic and copies ran while one was open for 1% of the time, Pallas kernels for 26%

profile of v8, /device:TPU:0, one launch (start us, length us, event | category | flops | bytes accessed | tf_op | source)
XLA Modules:
  0.0 36.1 jit_solution(5298435335350261609)
XLA Ops:
  0.0 1.2 %fusion.1 = (bf16[1,384,384]{2,1,0:T(8,128)(2,1)S(1)}, bf16[1,384,384]{2,1,0:T(8,128)(2,1)S(1)}) fusion(bf16[2,384,384]{2,1,0:T(8,128)(2,1)} %refs_0_), kind=kLoop, calls=%fused_computation.7 | loop fusion | bytes 1179648 | tf_op jit(solution)/shard_map/slice | solution.py:213
  1.2 3.0 %collective-permute-start = (bf16[192,384]{1,0:T(8,128)(2,1)S(1)}, bf16[192,384]{1,0:T(8,128)(2,1)S(1)}, u32[]{:S(2)}, u32[]{:S(2)}) collective-permute-start(bf16[192,384]{1,0:T(8,128)(2,1)S(1)} %dynamic-slice_bitcast_fusion), channel_id=1, source_target_pairs={{0,2},{1,3},{2,0},{3,1},{4,6},{5,7},{6,4},{7,5},{8,10},{9,11},{10,... | collective-permute-start | bytes 442376 | tf_op jit(solution)/shard_map/ppermute | solution.py:20
  4.2 0.1 collective-permute-start.2
  4.3 0.7 %copy-done.2 = s32[8,2]{0,1:T(2,128)S(1)} copy-done((s32[8,2]{0,1:T(2,128)S(1)}, s32[8,2]{0,1:T(2,128)}, u32[]{:S(2)}) %copy-start.2) | copy-done | bytes 88
  5.0 1.6 %shard_map.64.plan = s32[3,49]{1,0:T(4,128)S(1)} custom-call(s32[2,8]{1,0:T(2,128)S(1)} %bitcast.11), custom_call_target="tpu_custom_call" | custom-call | flops 20000000000 | tf_op jit(solution)/shard_map/pallas_call | solution.py:222
  6.7 0.2 select_reduce_fusion.coef
  6.8 2.1 %collective-permute-done = bf16[192,384]{1,0:T(8,128)(2,1)S(1)} collective-permute-done((bf16[192,384]{1,0:T(8,128)(2,1)S(1)}, bf16[192,384]{1,0:T(8,128)(2,1)S(1)}, u32[]{:S(2)}, u32[]{:S(2)}) %collective-permute-start) | collective-permute-done | bytes 147488 | tf_op jit(solution)/shard_map/ppermute | solution.py:20
  8.9 2.0 %collective-permute-start.1 = (bf16[192,384]{1,0:T(8,128)(2,1)S(1)}, bf16[192,384]{1,0:T(8,128)(2,1)S(1)}, u32[]{:S(2)}, u32[]{:S(2)}) collective-permute-start(bf16[192,384]{1,0:T(8,128)(2,1)S(1)} %collective-permute-done), channel_id=1, source_target_pairs={{0,4},{4,0},{8,12},{12,8},{16,20},{20,16},{24,28},{28,24},{1,5},{5... | collective-permute-start | bytes 442376 | tf_op jit(solution)/shard_map/ppermute | solution.py:20
  10.9 0.0 collective-permute-done.3.refs_1_
  11.0 5.2 %shard_map.65.refs_0_ = f32[2,384,384]{2,1,0:T(8,128)S(1)} custom-call(s32[3,49]{1,0:T(4,128)S(1)} %shard_map.64.plan, f32[2,8]{1,0:T(2,128)S(1)} %select_reduce_fusion.coef, bf16[8,2,384,384]{3,2,1,0:T(8,128)(2,1)S(1)} %bitcast.10, bf16[8,2,384,384]{3,2,1,0:T(8,128)(2,1)S(1)} %copy-done, bf16[2,384,384]{2,1,0:T(8,128)(2,1)S(1)} %copy-done.1, ...), custom_call_target="tpu_custom_call" | custom-call | flops 384 | tf_op jit(solution)/shard_map/pallas_call | solution.py:177
  16.2 0.0 collective-permute-done.1
  16.2 0.0 collective-permute-done.2.refs_1_
  16.2 0.1 collective-permute-start.5
  16.3 0.5 %collective-permute-start.4 = (bf16[1,384,384]{2,1,0:T(8,128)(2,1)S(1)}, bf16[1,384,384]{2,1,0:T(8,128)(2,1)S(1)}, u32[]{:S(2)}, u32[]{:S(2)}) collective-permute-start(bf16[1,384,384]{2,1,0:T(8,128)(2,1)S(1)} %collective-permute-done.2.refs_1_), channel_id=1, source_target_pairs={{0,1},{1,0},{2,3},{3,2},{4,5},{5,4},{6,7},{7,6},{8,9},{9,8},{10,11... | collective-permute-start | bytes 884744 | tf_op jit(solution)/shard_map/ppermute | solution.py:20
  16.8 2.7 %shard_map.66.refs_0_ = f32[2,384,384]{2,1,0:T(8,128)S(1)} custom-call(s32[3,49]{1,0:T(4,128)S(1)} %shard_map.64.plan, f32[2,8]{1,0:T(2,128)S(1)} %select_reduce_fusion.coef, bf16[8,2,384,384]{3,2,1,0:T(8,128)(2,1)S(1)} %bitcast.10, bf16[8,2,384,384]{3,2,1,0:T(8,128)(2,1)S(1)} %copy-done, f32[2,384,384]{2,1,0:T(8,128)S(1)} %shard_map.65.refs_0_, ...), custom_call_target="tpu_custom_call" | custom-call | flops 384 | tf_op jit(solution)/shard_map/pallas_call | solution.py:177
  19.5 0.0 collective-permute-done.4.refs_1_
  19.5 1.9 %shard_map.67 = (f32[2,48,384]{2,1,0:T(8,128)S(1)}, bf16[2,48,384]{2,1,0:T(8,128)(2,1)S(1)}, bf16[2,48,384]{2,1,0:T(8,128)(2,1)S(1)}, bf16[2,48,384]{2,1,0:T(8,1...) custom-call(s32[3,49]{1,0:T(4,128)S(1)} %shard_map.64.plan, ...), custom_call_target="tpu_custom_call" | custom-call | flops 384 | tf_op jit(solution)/shard_map/pallas_call | solution.py:177
  21.5 2.2 %collective-permute-start.9 = (bf16[2,48,384]{2,1,0:T(8,128)(2,1)S(1)}, bf16[2,48,384]{2,1,0:T(8,128)(2,1)S(1)}, u32[]{:S(2)}, u32[]{:S(2)}) collective-permute-start(bf16[2,48,384]{2,1,0:T(8,128)(2,1)S(1)} %get-tuple-element.42), channel_id=1, source_target_pairs={{0,12},{4,8},{8,4},{12,0},{16,28},{20,24},{24,20},{28,16},{1,13},{... | collective-permute-start | bytes 221192 | tf_op jit(solution)/shard_map/ppermute | solution.py:20
  23.6 1.0 %collective-permute-start.10 = (bf16[2,48,384]{2,1,0:T(8,128)(2,1)S(1)}, bf16[2,48,384]{2,1,0:T(8,128)(2,1)S(1)}, u32[]{:S(2)}, u32[]{:S(2)}) collective-permute-start(bf16[2,48,384]{2,1,0:T(8,128)(2,1)S(1)} %get-tuple-element.43), channel_id=1, source_target_pairs={{0,4},{4,0},{8,12},{12,8},{16,20},{20,16},{24,28},{28,24},{1,5},{5... | collective-permute-start | bytes 221192 | tf_op jit(solution)/shard_map/ppermute | solution.py:20
  24.6 0.4 %collective-permute-start.11 = (bf16[2,48,384]{2,1,0:T(8,128)(2,1)S(1)}, bf16[2,48,384]{2,1,0:T(8,128)(2,1)S(1)}, u32[]{:S(2)}, u32[]{:S(2)}) collective-permute-start(bf16[2,48,384]{2,1,0:T(8,128)(2,1)S(1)} %get-tuple-element.44), channel_id=1, source_target_pairs={{0,8},{4,12},{8,0},{12,4},{16,24},{20,28},{24,16},{28,20},{1,9},{5... | collective-permute-start | bytes 221192 | tf_op jit(solution)/shard_map/ppermute | solution.py:20
  25.0 1.1 %collective-permute-start.6 = (bf16[2,48,384]{2,1,0:T(8,128)(2,1)S(1)}, bf16[2,48,384]{2,1,0:T(8,128)(2,1)S(1)}, u32[]{:S(2)}, u32[]{:S(2)}) collective-permute-start(bf16[2,48,384]{2,1,0:T(8,128)(2,1)S(1)} %get-tuple-element.38), channel_id=1, source_target_pairs={{0,4},{4,0},{8,12},{12,8},{16,20},{20,16},{24,28},{28,24},{1,5},{5... | collective-permute-start | bytes 221192 | tf_op jit(solution)/shard_map/ppermute | solution.py:20
  26.1 2.0 %collective-permute-start.7 = (bf16[2,48,384]{2,1,0:T(8,128)(2,1)S(1)}, bf16[2,48,384]{2,1,0:T(8,128)(2,1)S(1)}, u32[]{:S(2)}, u32[]{:S(2)}) collective-permute-start(bf16[2,48,384]{2,1,0:T(8,128)(2,1)S(1)} %get-tuple-element.39), channel_id=1, source_target_pairs={{0,12},{4,8},{8,4},{12,0},{16,28},{20,24},{24,20},{28,16},{1,13},{... | collective-permute-start | bytes 221192 | tf_op jit(solution)/shard_map/ppermute | solution.py:20
  28.1 1.1 %collective-permute-start.8 = (bf16[2,48,384]{2,1,0:T(8,128)(2,1)S(1)}, bf16[2,48,384]{2,1,0:T(8,128)(2,1)S(1)}, u32[]{:S(2)}, u32[]{:S(2)}) collective-permute-start(bf16[2,48,384]{2,1,0:T(8,128)(2,1)S(1)} %get-tuple-element.40), channel_id=1, source_target_pairs={{0,8},{4,12},{8,0},{12,4},{16,24},{20,28},{24,16},{28,20},{1,9},{5... | collective-permute-start | bytes 221192 | tf_op jit(solution)/shard_map/ppermute | solution.py:20
  29.2 0.0 collective-permute-done.10
  29.2 0.5 %collective-permute-done.11 = bf16[2,48,384]{2,1,0:T(8,128)(2,1)S(1)} collective-permute-done((bf16[2,48,384]{2,1,0:T(8,128)(2,1)S(1)}, bf16[2,48,384]{2,1,0:T(8,128)(2,1)S(1)}, u32[]{:S(2)}, u32[]{:S(2)}) %collective-permute-start.11) | collective-permute-done | bytes 73760 | tf_op jit(solution)/shard_map/ppermute | solution.py:20
  29.7 3.3 %collective-permute-start.12 = (bf16[2,48,384]{2,1,0:T(8,128)(2,1)S(1)}, bf16[2,48,384]{2,1,0:T(8,128)(2,1)S(1)}, u32[]{:S(2)}, u32[]{:S(2)}) collective-permute-start(bf16[2,48,384]{2,1,0:T(8,128)(2,1)S(1)} %add_convert_fusion.1), channel_id=1, source_target_pairs={{0,16},{4,20},{8,24},{12,28},{16,0},{20,4},{24,8},{28,12},{1,17},{... | collective-permute-start | bytes 221192 | tf_op jit(solution)/shard_map/ppermute | solution.py:20
  33.0 0.0 collective-permute-done.6
  33.0 0.0 collective-permute-done.7
  33.0 0.0 collective-permute-done.8
  33.0 2.3 %collective-permute-done.12 = bf16[2,48,384]{2,1,0:T(8,128)(2,1)S(1)} collective-permute-done((bf16[2,48,384]{2,1,0:T(8,128)(2,1)S(1)}, bf16[2,48,384]{2,1,0:T(8,128)(2,1)S(1)}, u32[]{:S(2)}, u32[]{:S(2)}) %collective-permute-start.12) | collective-permute-done | bytes 73760 | tf_op jit(solution)/shard_map/ppermute | solution.py:20
  35.4 0.1 fusion
  35.4 0.7 %copy.8 = bf16[48,2,384]{2,1,0:T(2,128)(2,1)} copy(bf16[48,2,384]{2,0,1:T(8,128)(2,1)S(1)} %fusion) | data formatting | bytes 147456 | tf_op jit(solution)/shard_map/convert_element_type | solution.py:249
  (20 shorter events, 0.1 us)
Async XLA Ops:
  0.0 11.0 %slice-start = ((s8[4718592]{0:T(1024)(128)(4,1)}), s8[524288]{0:T(1024)(128)(4,1)S(1)}, s32[]{:S(2)}) async-start(s8[4718592]{0:T(1024)(128)(4,1)} %bitcast.9), calls=%async_computation | async-start | bytes 1048576
  1.2 7.7 %collective-permute-start = (bf16[192,384]{1,0:T(8,128)(2,1)S(1)}, bf16[192,384]{1,0:T(8,128)(2,1)S(1)}, u32[]{:S(2)}, u32[]{:S(2)}) collective-permute-start(bf16[192,384]{1,0:T(8,128)(2,1)S(1)} %dynamic-slice_bitcast_fusion), channel_id=1, source_target_pairs={{0,2},{1,3},{2,0},{3,1},{4,6},{5,7},{6,4},{7,5},{8,10},{9,11},{10,... | collective-permute-start | bytes 442376 | tf_op jit(solution)/shard_map/ppermute | solution.py:20
  4.2 11.9 %collective-permute-start.2 = (bf16[1,384,384]{2,1,0:T(8,128)(2,1)S(1)}, bf16[1,384,384]{2,1,0:T(8,128)(2,1)S(1)}, u32[]{:S(2)}, u32[]{:S(2)}) collective-permute-start(bf16[1,384,384]{2,1,0:T(8,128)(2,1)S(1)} %get-tuple-element.31), channel_id=1, source_target_pairs={{0,2},{1,3},{2,0},{3,1},{4,6},{5,7},{6,4},{7,5},{8,10},{9,11},{10,... | collective-permute-start | bytes 884744 | tf_op jit(solution)/shard_map/ppermute | solution.py:20
  4.3 6.6 %collective-permute-start.3 = (bf16[2,384,384]{2,1,0:T(8,128)(2,1)}, bf16[2,384,384]{2,1,0:T(8,128)(2,1)S(1)}, u32[]{:S(2)}, u32[]{:S(2)}) collective-permute-start(bf16[2,384,384]{2,1,0:T(8,128)(2,1)} %refs_0_), channel_id=1, source_target_pairs={{0,1},{1,0},{2,3},{3,2},{4,5},{5,4},{6,7},{7,6},{8,9},{9,8},{10,11... | collective-permute-start | bytes 1769480 | tf_op jit(solution)/shard_map/ppermute | solution.py:20
  4.3 0.7 %copy-start.2 = (s32[8,2]{0,1:T(2,128)S(1)}, s32[8,2]{0,1:T(2,128)}, u32[]{:S(2)}) copy-start(s32[8,2]{0,1:T(2,128)} %param.9) | copy-start | bytes 196
  5.0 1.6 %copy-start.3 = (s32[8,2]{0,1:T(2,128)S(1)}, s32[8,2]{0,1:T(2,128)}, u32[]{:S(2)}) copy-start(s32[8,2]{0,1:T(2,128)} %param.10) | copy-start | bytes 196
  5.0 1.6 %copy-start.4 = (f32[64]{0:T(128)S(1)}, f32[64]{0:T(128)}, u32[]{:S(2)}) copy-start(f32[64]{0:T(128)} %param.11) | copy-start | bytes 772
  5.0 5.9 %slice-start.1 = ((s8[4718592]{0:T(1024)(128)(4,1)}), s8[4194304]{0:T(1024)(128)(4,1)S(1)}, s32[]{:S(2)}) async-start(s8[4718592]{0:T(1024)(128)(4,1)} %bitcast.9), calls=%async_computation.1 | async-start | bytes 8388608
  5.0 6.0 %copy-start = (bf16[8,2,384,384]{3,2,1,0:T(8,128)(2,1)S(1)}, bf16[8,2,384,384]{3,2,1,0:T(8,128)(2,1)}, u32[]{:S(2)}) copy-start(bf16[8,2,384,384]{3,2,1,0:T(8,128)(2,1)} %right.5) | copy-start | bytes 14155780
  5.0 6.0 %copy-start.1 = (bf16[2,384,384]{2,1,0:T(8,128)(2,1)S(1)}, bf16[2,384,384]{2,1,0:T(8,128)(2,1)}, u32[]{:S(2)}) copy-start(bf16[2,384,384]{2,1,0:T(8,128)(2,1)} %refs_0_) | copy-start | bytes 1769476
  8.9 7.3 %collective-permute-start.1 = (bf16[192,384]{1,0:T(8,128)(2,1)S(1)}, bf16[192,384]{1,0:T(8,128)(2,1)S(1)}, u32[]{:S(2)}, u32[]{:S(2)}) collective-permute-start(bf16[192,384]{1,0:T(8,128)(2,1)S(1)} %collective-permute-done), channel_id=1, source_target_pairs={{0,4},{4,0},{8,12},{12,8},{16,20},{20,16},{24,28},{28,24},{1,5},{5... | collective-permute-start | bytes 442376 | tf_op jit(solution)/shard_map/ppermute | solution.py:20
  16.2 3.3 %collective-permute-start.5 = (bf16[2,192,384]{2,1,0:T(8,128)(2,1)S(1)}, bf16[2,192,384]{2,1,0:T(8,128)(2,1)S(1)}, u32[]{:S(2)}, u32[]{:S(2)}) collective-permute-start(bf16[2,192,384]{2,1,0:T(8,128)(2,1)S(1)} %pad_maximum_fusion.refs_2_), channel_id=1, source_target_pairs={{0,1},{1,0},{2,3},{3,2},{4,5},{5,4},{6,7},{7,6},{8,9},{9,8},{10,11... | collective-permute-start | bytes 884744 | tf_op jit(solution)/shard_map/ppermute | solution.py:20
  16.3 3.2 %collective-permute-start.4 = (bf16[1,384,384]{2,1,0:T(8,128)(2,1)S(1)}, bf16[1,384,384]{2,1,0:T(8,128)(2,1)S(1)}, u32[]{:S(2)}, u32[]{:S(2)}) collective-permute-start(bf16[1,384,384]{2,1,0:T(8,128)(2,1)S(1)} %collective-permute-done.2.refs_1_), channel_id=1, source_target_pairs={{0,1},{1,0},{2,3},{3,2},{4,5},{5,4},{6,7},{7,6},{8,9},{9,8},{10,11... | collective-permute-start | bytes 884744 | tf_op jit(solution)/shard_map/ppermute | solution.py:20
  21.5 6.6 %collective-permute-start.9 = (bf16[2,48,384]{2,1,0:T(8,128)(2,1)S(1)}, bf16[2,48,384]{2,1,0:T(8,128)(2,1)S(1)}, u32[]{:S(2)}, u32[]{:S(2)}) collective-permute-start(bf16[2,48,384]{2,1,0:T(8,128)(2,1)S(1)} %get-tuple-element.42), channel_id=1, source_target_pairs={{0,12},{4,8},{8,4},{12,0},{16,28},{20,24},{24,20},{28,16},{1,13},{... | collective-permute-start | bytes 221192 | tf_op jit(solution)/shard_map/ppermute | solution.py:20
  23.6 5.6 %collective-permute-start.10 = (bf16[2,48,384]{2,1,0:T(8,128)(2,1)S(1)}, bf16[2,48,384]{2,1,0:T(8,128)(2,1)S(1)}, u32[]{:S(2)}, u32[]{:S(2)}) collective-permute-start(bf16[2,48,384]{2,1,0:T(8,128)(2,1)S(1)} %get-tuple-element.43), channel_id=1, source_target_pairs={{0,4},{4,0},{8,12},{12,8},{16,20},{20,16},{24,28},{28,24},{1,5},{5... | collective-permute-start | bytes 221192 | tf_op jit(solution)/shard_map/ppermute | solution.py:20
  24.6 5.0 %collective-permute-start.11 = (bf16[2,48,384]{2,1,0:T(8,128)(2,1)S(1)}, bf16[2,48,384]{2,1,0:T(8,128)(2,1)S(1)}, u32[]{:S(2)}, u32[]{:S(2)}) collective-permute-start(bf16[2,48,384]{2,1,0:T(8,128)(2,1)S(1)} %get-tuple-element.44), channel_id=1, source_target_pairs={{0,8},{4,12},{8,0},{12,4},{16,24},{20,28},{24,16},{28,20},{1,9},{5... | collective-permute-start | bytes 221192 | tf_op jit(solution)/shard_map/ppermute | solution.py:20
  25.0 8.0 %collective-permute-start.6 = (bf16[2,48,384]{2,1,0:T(8,128)(2,1)S(1)}, bf16[2,48,384]{2,1,0:T(8,128)(2,1)S(1)}, u32[]{:S(2)}, u32[]{:S(2)}) collective-permute-start(bf16[2,48,384]{2,1,0:T(8,128)(2,1)S(1)} %get-tuple-element.38), channel_id=1, source_target_pairs={{0,4},{4,0},{8,12},{12,8},{16,20},{20,16},{24,28},{28,24},{1,5},{5... | collective-permute-start | bytes 221192 | tf_op jit(solution)/shard_map/ppermute | solution.py:20
  26.1 6.9 %collective-permute-start.7 = (bf16[2,48,384]{2,1,0:T(8,128)(2,1)S(1)}, bf16[2,48,384]{2,1,0:T(8,128)(2,1)S(1)}, u32[]{:S(2)}, u32[]{:S(2)}) collective-permute-start(bf16[2,48,384]{2,1,0:T(8,128)(2,1)S(1)} %get-tuple-element.39), channel_id=1, source_target_pairs={{0,12},{4,8},{8,4},{12,0},{16,28},{20,24},{24,20},{28,16},{1,13},{... | collective-permute-start | bytes 221192 | tf_op jit(solution)/shard_map/ppermute | solution.py:20
  28.1 4.9 %collective-permute-start.8 = (bf16[2,48,384]{2,1,0:T(8,128)(2,1)S(1)}, bf16[2,48,384]{2,1,0:T(8,128)(2,1)S(1)}, u32[]{:S(2)}, u32[]{:S(2)}) collective-permute-start(bf16[2,48,384]{2,1,0:T(8,128)(2,1)S(1)} %get-tuple-element.40), channel_id=1, source_target_pairs={{0,8},{4,12},{8,0},{12,4},{16,24},{20,28},{24,16},{28,20},{1,9},{5... | collective-permute-start | bytes 221192 | tf_op jit(solution)/shard_map/ppermute | solution.py:20
  29.7 5.6 %collective-permute-start.12 = (bf16[2,48,384]{2,1,0:T(8,128)(2,1)S(1)}, bf16[2,48,384]{2,1,0:T(8,128)(2,1)S(1)}, u32[]{:S(2)}, u32[]{:S(2)}) collective-permute-start(bf16[2,48,384]{2,1,0:T(8,128)(2,1)S(1)} %add_convert_fusion.1), channel_id=1, source_target_pairs={{0,16},{4,20},{8,24},{12,28},{16,0},{20,4},{24,8},{28,12},{1,17},{... | collective-permute-start | bytes 221192 | tf_op jit(solution)/shard_map/ppermute | solution.py:20

commit v9 on v8

--- a/solution.py
+++ b/solution.py
@@ -195,7 +195,7 @@
     for high in reversed(range(n_opg // PARTS)):
         at = high * PARTS
         total = sends[at]
-        for low in (3, 1, 2) if high else (1, 3, 2):
+        for low in (1, 3, 2) if high else (3, 1, 2):
             total = total + flip(sends[at + low], OPG, n_opg, low).astype(jnp.float32)
         if high:
             total = flip(total.astype(jnp.bfloat16), OPG, n_opg, at).astype(jnp.float32)

time: 36.4 us -> 36.9 us (1.014); the launches traced: 36.1 us -> 37.4 us
  waiting for transfers between devices: 4.95 us -> 7.63 us
  starting transfers between devices: 16.7 us -> 15.4 us
    ppermute x13, waiting for transfers between devices: 4.95 us -> 7.63 us  [flip(): return lax.ppermute(x, axis, [(i, i ^ bit) for i in range(size)])]
    ppermute x13, starting transfers between devices: 16.7 us -> 15.4 us  [flip(): return lax.ppermute(x, axis, [(i, i ^ bit) for i in range(size)])]
  transfers between devices with their start and end apart: 13 -> 13, of which waited for: 3 -> 7; matrix products, arithmetic and copies ran while one was open for 1% -> 1% of each run, Pallas kernels for 26% -> 21%
where the time goes in v9:
time: 36.9 us; the launch traced here: 37.4 us
  starting transfers between devices  15.4 us (42%)
  Pallas kernels  11.4 us (31%)
  waiting for transfers between devices  7.63 us (21%)
  local copies, waits for them, and re-layouts  2.58 us (7%)
    ppermute x13, starting transfers between devices, flip(): return lax.ppermute(x, axis, [(i, i ^ bit) for i in range(size)])  15.4 us
    pallas_call x3, Pallas kernels, products(): pl.pallas_call(functools.partial(products_kernel, kind, n_opg), out_shape...  9.77 us
    ppermute x13, waiting for transfers between devices, flip(): return lax.ppermute(x, axis, [(i, i ^ bit) for i in range(size)])  7.63 us
    pallas_call x1, Pallas kernels, on_device(): pl.pallas_call(functools.partial(plan_kernel, local), out_shape=jax.Shape...  1.6 us
    slice x1, local copies, waits for them, and re-layouts, on_device(): ours, rest, psi = lax.optimization_barrier((ours, psi[:local - 1], psi))  1.17 us
  transfers between devices with their start and end apart: 13, of which 7 were waited for; matrix products, arithmetic and copies ran while one was open for 1% of the time, Pallas kernels for 21%

profile of v9, /device:TPU:0, one launch (start us, length us, event | category | flops | bytes accessed | tf_op | source)
XLA Modules:
  0.0 37.4 jit_solution(16624888934346244163)
XLA Ops:
  0.0 1.2 %fusion.1 = (bf16[1,384,384]{2,1,0:T(8,128)(2,1)S(1)}, bf16[1,384,384]{2,1,0:T(8,128)(2,1)S(1)}) fusion(bf16[2,384,384]{2,1,0:T(8,128)(2,1)} %refs_0_), kind=kLoop, calls=%fused_computation.7 | loop fusion | bytes 1179648 | tf_op jit(solution)/shard_map/slice | solution.py:213
  1.2 3.0 %collective-permute-start = (bf16[192,384]{1,0:T(8,128)(2,1)S(1)}, bf16[192,384]{1,0:T(8,128)(2,1)S(1)}, u32[]{:S(2)}, u32[]{:S(2)}) collective-permute-start(bf16[192,384]{1,0:T(8,128)(2,1)S(1)} %dynamic-slice_bitcast_fusion), channel_id=1, source_target_pairs={{0,2},{1,3},{2,0},{3,1},{4,6},{5,7},{6,4},{7,5},{8,10},{9,11},{10,... | collective-permute-start | bytes 442376 | tf_op jit(solution)/shard_map/ppermute | solution.py:20
  4.2 0.1 collective-permute-start.2
  4.3 0.0 collective-permute-start.3
  4.3 0.7 %copy-done.2 = s32[8,2]{0,1:T(2,128)S(1)} copy-done((s32[8,2]{0,1:T(2,128)S(1)}, s32[8,2]{0,1:T(2,128)}, u32[]{:S(2)}) %copy-start.2) | copy-done | bytes 88
  5.0 1.6 %shard_map.64.plan = s32[3,49]{1,0:T(4,128)S(1)} custom-call(s32[2,8]{1,0:T(2,128)S(1)} %bitcast.11), custom_call_target="tpu_custom_call" | custom-call | flops 20000000000 | tf_op jit(solution)/shard_map/pallas_call | solution.py:222
  6.7 0.2 select_reduce_fusion.coef
  6.8 2.1 %collective-permute-done = bf16[192,384]{1,0:T(8,128)(2,1)S(1)} collective-permute-done((bf16[192,384]{1,0:T(8,128)(2,1)S(1)}, bf16[192,384]{1,0:T(8,128)(2,1)S(1)}, u32[]{:S(2)}, u32[]{:S(2)}) %collective-permute-start) | collective-permute-done | bytes 147488 | tf_op jit(solution)/shard_map/ppermute | solution.py:20
  8.9 2.0 %collective-permute-start.1 = (bf16[192,384]{1,0:T(8,128)(2,1)S(1)}, bf16[192,384]{1,0:T(8,128)(2,1)S(1)}, u32[]{:S(2)}, u32[]{:S(2)}) collective-permute-start(bf16[192,384]{1,0:T(8,128)(2,1)S(1)} %collective-permute-done), channel_id=1, source_target_pairs={{0,4},{4,0},{8,12},{12,8},{16,20},{20,16},{24,28},{28,24},{1,5},{5... | collective-permute-start | bytes 442376 | tf_op jit(solution)/shard_map/ppermute | solution.py:20
  10.9 0.0 collective-permute-done.3.refs_1_
  11.0 2.7 %shard_map.65.refs_0_ = f32[2,384,384]{2,1,0:T(8,128)S(1)} custom-call(s32[3,49]{1,0:T(4,128)S(1)} %shard_map.64.plan, f32[2,8]{1,0:T(2,128)S(1)} %select_reduce_fusion.coef, bf16[8,2,384,384]{3,2,1,0:T(8,128)(2,1)S(1)} %bitcast.10, bf16[8,2,384,384]{3,2,1,0:T(8,128)(2,1)S(1)} %copy-done, bf16[2,384,384]{2,1,0:T(8,128)(2,1)S(1)} %copy-done.1, ...), custom_call_target="tpu_custom_call" | custom-call | flops 384 | tf_op jit(solution)/shard_map/pallas_call | solution.py:177
  13.7 0.4 collective-permute-done.1
  14.1 0.3 collective-permute-done.2.refs_1_
  14.4 0.1 collective-permute-start.5
  14.5 0.5 %collective-permute-start.4 = (bf16[1,384,384]{2,1,0:T(8,128)(2,1)S(1)}, bf16[1,384,384]{2,1,0:T(8,128)(2,1)S(1)}, u32[]{:S(2)}, u32[]{:S(2)}) collective-permute-start(bf16[1,384,384]{2,1,0:T(8,128)(2,1)S(1)} %collective-permute-done.2.refs_1_), channel_id=1, source_target_pairs={{0,1},{1,0},{2,3},{3,2},{4,5},{5,4},{6,7},{7,6},{8,9},{9,8},{10,11... | collective-permute-start | bytes 884744 | tf_op jit(solution)/shard_map/ppermute | solution.py:20
  15.0 3.5 %shard_map.66.refs_0_ = f32[2,384,384]{2,1,0:T(8,128)S(1)} custom-call(s32[3,49]{1,0:T(4,128)S(1)} %shard_map.64.plan, f32[2,8]{1,0:T(2,128)S(1)} %select_reduce_fusion.coef, bf16[8,2,384,384]{3,2,1,0:T(8,128)(2,1)S(1)} %bitcast.10, bf16[8,2,384,384]{3,2,1,0:T(8,128)(2,1)S(1)} %copy-done, f32[2,384,384]{2,1,0:T(8,128)S(1)} %shard_map.65.refs_0_, ...), custom_call_target="tpu_custom_call" | custom-call | flops 384 | tf_op jit(solution)/shard_map/pallas_call | solution.py:177
  18.5 0.0 collective-permute-done.5.refs_2_
  18.6 3.5 %shard_map.67 = (f32[2,48,384]{2,1,0:T(8,128)S(1)}, bf16[2,48,384]{2,1,0:T(8,128)(2,1)S(1)}, bf16[2,48,384]{2,1,0:T(8,128)(2,1)S(1)}, bf16[2,48,384]{2,1,0:T(8,1...) custom-call(s32[3,49]{1,0:T(4,128)S(1)} %shard_map.64.plan, ...), custom_call_target="tpu_custom_call" | custom-call | flops 384 | tf_op jit(solution)/shard_map/pallas_call | solution.py:177
  22.1 1.3 %collective-permute-start.9 = (bf16[2,48,384]{2,1,0:T(8,128)(2,1)S(1)}, bf16[2,48,384]{2,1,0:T(8,128)(2,1)S(1)}, u32[]{:S(2)}, u32[]{:S(2)}) collective-permute-start(bf16[2,48,384]{2,1,0:T(8,128)(2,1)S(1)} %get-tuple-element.42), channel_id=1, source_target_pairs={{0,4},{4,0},{8,12},{12,8},{16,20},{20,16},{24,28},{28,24},{1,5},{5... | collective-permute-start | bytes 221192 | tf_op jit(solution)/shard_map/ppermute | solution.py:20
  23.4 1.0 %collective-permute-start.10 = (bf16[2,48,384]{2,1,0:T(8,128)(2,1)S(1)}, bf16[2,48,384]{2,1,0:T(8,128)(2,1)S(1)}, u32[]{:S(2)}, u32[]{:S(2)}) collective-permute-start(bf16[2,48,384]{2,1,0:T(8,128)(2,1)S(1)} %get-tuple-element.43), channel_id=1, source_target_pairs={{0,12},{4,8},{8,4},{12,0},{16,28},{20,24},{24,20},{28,16},{1,13},{... | collective-permute-start | bytes 221192 | tf_op jit(solution)/shard_map/ppermute | solution.py:20
  24.5 1.2 %collective-permute-start.11 = (bf16[2,48,384]{2,1,0:T(8,128)(2,1)S(1)}, bf16[2,48,384]{2,1,0:T(8,128)(2,1)S(1)}, u32[]{:S(2)}, u32[]{:S(2)}) collective-permute-start(bf16[2,48,384]{2,1,0:T(8,128)(2,1)S(1)} %get-tuple-element.44), channel_id=1, source_target_pairs={{0,8},{4,12},{8,0},{12,4},{16,24},{20,28},{24,16},{28,20},{1,9},{5... | collective-permute-start | bytes 221192 | tf_op jit(solution)/shard_map/ppermute | solution.py:20
  25.7 1.4 %collective-permute-start.6 = (bf16[2,48,384]{2,1,0:T(8,128)(2,1)S(1)}, bf16[2,48,384]{2,1,0:T(8,128)(2,1)S(1)}, u32[]{:S(2)}, u32[]{:S(2)}) collective-permute-start(bf16[2,48,384]{2,1,0:T(8,128)(2,1)S(1)} %get-tuple-element.38), channel_id=1, source_target_pairs={{0,12},{4,8},{8,4},{12,0},{16,28},{20,24},{24,20},{28,16},{1,13},{... | collective-permute-start | bytes 221192 | tf_op jit(solution)/shard_map/ppermute | solution.py:20
  27.1 0.9 %collective-permute-start.7 = (bf16[2,48,384]{2,1,0:T(8,128)(2,1)S(1)}, bf16[2,48,384]{2,1,0:T(8,128)(2,1)S(1)}, u32[]{:S(2)}, u32[]{:S(2)}) collective-permute-start(bf16[2,48,384]{2,1,0:T(8,128)(2,1)S(1)} %get-tuple-element.39), channel_id=1, source_target_pairs={{0,4},{4,0},{8,12},{12,8},{16,20},{20,16},{24,28},{28,24},{1,5},{5... | collective-permute-start | bytes 221192 | tf_op jit(solution)/shard_map/ppermute | solution.py:20
  28.0 0.0 collective-permute-done.9
  28.0 1.2 %collective-permute-start.8 = (bf16[2,48,384]{2,1,0:T(8,128)(2,1)S(1)}, bf16[2,48,384]{2,1,0:T(8,128)(2,1)S(1)}, u32[]{:S(2)}, u32[]{:S(2)}) collective-permute-start(bf16[2,48,384]{2,1,0:T(8,128)(2,1)S(1)} %get-tuple-element.40), channel_id=1, source_target_pairs={{0,8},{4,12},{8,0},{12,4},{16,24},{20,28},{24,16},{28,20},{1,9},{5... | collective-permute-start | bytes 221192 | tf_op jit(solution)/shard_map/ppermute | solution.py:20
  29.2 0.4 collective-permute-done.10
  29.5 0.2 collective-permute-done.11
  29.8 2.6 %collective-permute-start.12 = (bf16[2,48,384]{2,1,0:T(8,128)(2,1)S(1)}, bf16[2,48,384]{2,1,0:T(8,128)(2,1)S(1)}, u32[]{:S(2)}, u32[]{:S(2)}) collective-permute-start(bf16[2,48,384]{2,1,0:T(8,128)(2,1)S(1)} %add_convert_fusion.1), channel_id=1, source_target_pairs={{0,16},{4,20},{8,24},{12,28},{16,0},{20,4},{24,8},{28,12},{1,17},{... | collective-permute-start | bytes 221192 | tf_op jit(solution)/shard_map/ppermute | solution.py:20
  32.5 0.3 collective-permute-done.8
  32.8 3.9 %collective-permute-done.12 = bf16[2,48,384]{2,1,0:T(8,128)(2,1)S(1)} collective-permute-done((bf16[2,48,384]{2,1,0:T(8,128)(2,1)S(1)}, bf16[2,48,384]{2,1,0:T(8,128)(2,1)S(1)}, u32[]{:S(2)}, u32[]{:S(2)}) %collective-permute-start.12) | collective-permute-done | bytes 73760 | tf_op jit(solution)/shard_map/ppermute | solution.py:20
  36.7 0.1 fusion
  36.7 0.7 %copy.8 = bf16[48,2,384]{2,1,0:T(2,128)(2,1)} copy(bf16[48,2,384]{2,0,1:T(8,128)(2,1)S(1)} %fusion) | data formatting | bytes 147456 | tf_op jit(solution)/shard_map/convert_element_type | solution.py:249
  (20 shorter events, 0.1 us)
Async XLA Ops:
  0.0 11.0 %slice-start = ((s8[4718592]{0:T(1024)(128)(4,1)}), s8[524288]{0:T(1024)(128)(4,1)S(1)}, s32[]{:S(2)}) async-start(s8[4718592]{0:T(1024)(128)(4,1)} %bitcast.9), calls=%async_computation | async-start | bytes 1048576
  1.2 7.7 %collective-permute-start = (bf16[192,384]{1,0:T(8,128)(2,1)S(1)}, bf16[192,384]{1,0:T(8,128)(2,1)S(1)}, u32[]{:S(2)}, u32[]{:S(2)}) collective-permute-start(bf16[192,384]{1,0:T(8,128)(2,1)S(1)} %dynamic-slice_bitcast_fusion), channel_id=1, source_target_pairs={{0,2},{1,3},{2,0},{3,1},{4,6},{5,7},{6,4},{7,5},{8,10},{9,11},{10,... | collective-permute-start | bytes 442376 | tf_op jit(solution)/shard_map/ppermute | solution.py:20
  4.2 10.2 %collective-permute-start.2 = (bf16[1,384,384]{2,1,0:T(8,128)(2,1)S(1)}, bf16[1,384,384]{2,1,0:T(8,128)(2,1)S(1)}, u32[]{:S(2)}, u32[]{:S(2)}) collective-permute-start(bf16[1,384,384]{2,1,0:T(8,128)(2,1)S(1)} %get-tuple-element.31), channel_id=1, source_target_pairs={{0,2},{1,3},{2,0},{3,1},{4,6},{5,7},{6,4},{7,5},{8,10},{9,11},{10,... | collective-permute-start | bytes 884744 | tf_op jit(solution)/shard_map/ppermute | solution.py:20
  4.3 6.6 %collective-permute-start.3 = (bf16[2,384,384]{2,1,0:T(8,128)(2,1)}, bf16[2,384,384]{2,1,0:T(8,128)(2,1)S(1)}, u32[]{:S(2)}, u32[]{:S(2)}) collective-permute-start(bf16[2,384,384]{2,1,0:T(8,128)(2,1)} %refs_0_), channel_id=1, source_target_pairs={{0,1},{1,0},{2,3},{3,2},{4,5},{5,4},{6,7},{7,6},{8,9},{9,8},{10,11... | collective-permute-start | bytes 1769480 | tf_op jit(solution)/shard_map/ppermute | solution.py:20
  4.3 0.7 %copy-start.2 = (s32[8,2]{0,1:T(2,128)S(1)}, s32[8,2]{0,1:T(2,128)}, u32[]{:S(2)}) copy-start(s32[8,2]{0,1:T(2,128)} %param.9) | copy-start | bytes 196
  5.0 1.6 %copy-start.3 = (s32[8,2]{0,1:T(2,128)S(1)}, s32[8,2]{0,1:T(2,128)}, u32[]{:S(2)}) copy-start(s32[8,2]{0,1:T(2,128)} %param.10) | copy-start | bytes 196
  5.0 1.6 %copy-start.4 = (f32[64]{0:T(128)S(1)}, f32[64]{0:T(128)}, u32[]{:S(2)}) copy-start(f32[64]{0:T(128)} %param.11) | copy-start | bytes 772
  5.0 5.9 %slice-start.1 = ((s8[4718592]{0:T(1024)(128)(4,1)}), s8[4194304]{0:T(1024)(128)(4,1)S(1)}, s32[]{:S(2)}) async-start(s8[4718592]{0:T(1024)(128)(4,1)} %bitcast.9), calls=%async_computation.1 | async-start | bytes 8388608
  5.0 6.0 %copy-start = (bf16[8,2,384,384]{3,2,1,0:T(8,128)(2,1)S(1)}, bf16[8,2,384,384]{3,2,1,0:T(8,128)(2,1)}, u32[]{:S(2)}) copy-start(bf16[8,2,384,384]{3,2,1,0:T(8,128)(2,1)} %right.5) | copy-start | bytes 14155780
  5.0 6.0 %copy-start.1 = (bf16[2,384,384]{2,1,0:T(8,128)(2,1)S(1)}, bf16[2,384,384]{2,1,0:T(8,128)(2,1)}, u32[]{:S(2)}) copy-start(bf16[2,384,384]{2,1,0:T(8,128)(2,1)} %refs_0_) | copy-start | bytes 1769476
  8.9 5.2 %collective-permute-start.1 = (bf16[192,384]{1,0:T(8,128)(2,1)S(1)}, bf16[192,384]{1,0:T(8,128)(2,1)S(1)}, u32[]{:S(2)}, u32[]{:S(2)}) collective-permute-start(bf16[192,384]{1,0:T(8,128)(2,1)S(1)} %collective-permute-done), channel_id=1, source_target_pairs={{0,4},{4,0},{8,12},{12,8},{16,20},{20,16},{24,28},{28,24},{1,5},{5... | collective-permute-start | bytes 442376 | tf_op jit(solution)/shard_map/ppermute | solution.py:20
  14.4 4.1 %collective-permute-start.5 = (bf16[2,192,384]{2,1,0:T(8,128)(2,1)S(1)}, bf16[2,192,384]{2,1,0:T(8,128)(2,1)S(1)}, u32[]{:S(2)}, u32[]{:S(2)}) collective-permute-start(bf16[2,192,384]{2,1,0:T(8,128)(2,1)S(1)} %pad_maximum_fusion.refs_2_), channel_id=1, source_target_pairs={{0,1},{1,0},{2,3},{3,2},{4,5},{5,4},{6,7},{7,6},{8,9},{9,8},{10,11... | collective-permute-start | bytes 884744 | tf_op jit(solution)/shard_map/ppermute | solution.py:20
  14.5 4.0 %collective-permute-start.4 = (bf16[1,384,384]{2,1,0:T(8,128)(2,1)S(1)}, bf16[1,384,384]{2,1,0:T(8,128)(2,1)S(1)}, u32[]{:S(2)}, u32[]{:S(2)}) collective-permute-start(bf16[1,384,384]{2,1,0:T(8,128)(2,1)S(1)} %collective-permute-done.2.refs_1_), channel_id=1, source_target_pairs={{0,1},{1,0},{2,3},{3,2},{4,5},{5,4},{6,7},{7,6},{8,9},{9,8},{10,11... | collective-permute-start | bytes 884744 | tf_op jit(solution)/shard_map/ppermute | solution.py:20
  22.1 5.9 %collective-permute-start.9 = (bf16[2,48,384]{2,1,0:T(8,128)(2,1)S(1)}, bf16[2,48,384]{2,1,0:T(8,128)(2,1)S(1)}, u32[]{:S(2)}, u32[]{:S(2)}) collective-permute-start(bf16[2,48,384]{2,1,0:T(8,128)(2,1)S(1)} %get-tuple-element.42), channel_id=1, source_target_pairs={{0,4},{4,0},{8,12},{12,8},{16,20},{20,16},{24,28},{28,24},{1,5},{5... | collective-permute-start | bytes 221192 | tf_op jit(solution)/shard_map/ppermute | solution.py:20
  23.4 6.1 %collective-permute-start.10 = (bf16[2,48,384]{2,1,0:T(8,128)(2,1)S(1)}, bf16[2,48,384]{2,1,0:T(8,128)(2,1)S(1)}, u32[]{:S(2)}, u32[]{:S(2)}) collective-permute-start(bf16[2,48,384]{2,1,0:T(8,128)(2,1)S(1)} %get-tuple-element.43), channel_id=1, source_target_pairs={{0,12},{4,8},{8,4},{12,0},{16,28},{20,24},{24,20},{28,16},{1,13},{... | collective-permute-start | bytes 221192 | tf_op jit(solution)/shard_map/ppermute | solution.py:20
  24.5 5.3 %collective-permute-start.11 = (bf16[2,48,384]{2,1,0:T(8,128)(2,1)S(1)}, bf16[2,48,384]{2,1,0:T(8,128)(2,1)S(1)}, u32[]{:S(2)}, u32[]{:S(2)}) collective-permute-start(bf16[2,48,384]{2,1,0:T(8,128)(2,1)S(1)} %get-tuple-element.44), channel_id=1, source_target_pairs={{0,8},{4,12},{8,0},{12,4},{16,24},{20,28},{24,16},{28,20},{1,9},{5... | collective-permute-start | bytes 221192 | tf_op jit(solution)/shard_map/ppermute | solution.py:20
  25.7 6.8 %collective-permute-start.6 = (bf16[2,48,384]{2,1,0:T(8,128)(2,1)S(1)}, bf16[2,48,384]{2,1,0:T(8,128)(2,1)S(1)}, u32[]{:S(2)}, u32[]{:S(2)}) collective-permute-start(bf16[2,48,384]{2,1,0:T(8,128)(2,1)S(1)} %get-tuple-element.38), channel_id=1, source_target_pairs={{0,12},{4,8},{8,4},{12,0},{16,28},{20,24},{24,20},{28,16},{1,13},{... | collective-permute-start | bytes 221192 | tf_op jit(solution)/shard_map/ppermute | solution.py:20
  27.1 5.3 %collective-permute-start.7 = (bf16[2,48,384]{2,1,0:T(8,128)(2,1)S(1)}, bf16[2,48,384]{2,1,0:T(8,128)(2,1)S(1)}, u32[]{:S(2)}, u32[]{:S(2)}) collective-permute-start(bf16[2,48,384]{2,1,0:T(8,128)(2,1)S(1)} %get-tuple-element.39), channel_id=1, source_target_pairs={{0,4},{4,0},{8,12},{12,8},{16,20},{20,16},{24,28},{28,24},{1,5},{5... | collective-permute-start | bytes 221192 | tf_op jit(solution)/shard_map/ppermute | solution.py:20
  28.0 4.8 %collective-permute-start.8 = (bf16[2,48,384]{2,1,0:T(8,128)(2,1)S(1)}, bf16[2,48,384]{2,1,0:T(8,128)(2,1)S(1)}, u32[]{:S(2)}, u32[]{:S(2)}) collective-permute-start(bf16[2,48,384]{2,1,0:T(8,128)(2,1)S(1)} %get-tuple-element.40), channel_id=1, source_target_pairs={{0,8},{4,12},{8,0},{12,4},{16,24},{20,28},{24,16},{28,20},{1,9},{5... | collective-permute-start | bytes 221192 | tf_op jit(solution)/shard_map/ppermute | solution.py:20
  29.8 6.9 %collective-permute-start.12 = (bf16[2,48,384]{2,1,0:T(8,128)(2,1)S(1)}, bf16[2,48,384]{2,1,0:T(8,128)(2,1)S(1)}, u32[]{:S(2)}, u32[]{:S(2)}) collective-permute-start(bf16[2,48,384]{2,1,0:T(8,128)(2,1)S(1)} %add_convert_fusion.1), channel_id=1, source_target_pairs={{0,16},{4,20},{8,24},{12,28},{16,0},{20,4},{24,8},{28,12},{1,17},{... | collective-permute-start | bytes 221192 | tf_op jit(solution)/shard_map/ppermute | solution.py:20
